TPU v7x, 32 devices: a whole 2x2x4 slice. The times are simulated.
32 devices in a mesh: dp: 8 (over z, core), expert: 4 (over y, x).
Axes of the slice: x: 2, y: 2, z: 4, core: 2. Of those that a mesh axis runs over, the one named last changes fastest.
Arguments:
- normed: bfloat16 [1024, 6144], P(('dp', 'expert')), may hold values from -6 to 6
- upstream: bfloat16 [1024, 6144], P(('dp', 'expert')), may hold values from -6 to 6
- expert_ids: int32 [1024, 4], P(('dp', 'expert')), may hold values from 0 to 15, all different within a row; in each aligned block of 32 rows (0 to 31, 32 to 63, ...) at most 9 rows name the same one
- router_weight: bfloat16 [6144, 16], replicated, may hold values from -0.078125 to 0.078125
- gate_weight: bfloat16 [16, 20, 6144], P('expert'), may hold values from -0.078125 to 0.078125
- up_weight: bfloat16 [16, 20, 6144], P('expert'), may hold values from -0.078125 to 0.078125
- down_weight: bfloat16 [16, 20, 6144], P('expert'), may hold values from -1.25 to 1.25
- saved_inputs: bfloat16 [8, 16, 4, 9, 6144], P('dp', 'expert'), may hold values from -6 to 6
Outputs:
- grad_normed: bfloat16 [1024, 6144], P(('dp', 'expert'))
- router_grad: float32 [6144, 16], replicated
- grad_gate: float32 [16, 20, 6144], P('expert', None, 'dp')
- grad_up: float32 [16, 20, 6144], P('expert', None, 'dp')
- grad_down: float32 [16, 20, 6144], P('expert', None, 'dp')
Inputs may be any that keep to these rules, and one draw needn't show every extreme that they name: `expert_ids`: each token names 4 different experts. Among the tokens of one device no expert is named more than 9 times, a bound that some block reaches.
All inputs are finite; a program needn't handle non-finite values.
Results may differ from a plain program's by a relative error of at most 0.0064.
Values may be sent and summed in bfloat16 or wider, within the bound.
No kernel may reach another device: no remote copies, remote signals or barrier semaphores. Data moves between devices by JAX's collectives and lax.ppermute only.
A program may use at most 64 MiB of HBM per device.

v0:
```python
import jax
import jax.numpy as jnp
from jax import lax
from jax.sharding import PartitionSpec as P


def slot_index(ids, experts, exp_dev, n_expert, capacity):
    flat_ids = ids.reshape(-1)
    choose = (flat_ids[:, None] == jnp.arange(experts, dtype=jnp.int32)[None, :]).astype(jnp.int32)
    before = jnp.cumsum(choose, axis=0) - choose
    place = jnp.sum(before * choose, axis=1)
    local = flat_ids % exp_dev
    owner = flat_ids // exp_dev
    return (local * n_expert + owner) * capacity + place


def on_device(
    normed, upstream, expert_ids, router_weight, gate_weight, up_weight, down_weight, saved_inputs
):
    f32 = jnp.float32
    bf16 = jnp.bfloat16
    n_expert = lax.axis_size("expert")
    exp_dev, hidden_units, width = gate_weight.shape
    capacity = saved_inputs.shape[3]
    experts = exp_dev * n_expert
    tokens_here, top = expert_ids.shape
    total_slots = exp_dev * n_expert * capacity
    slot_count = n_expert * capacity
    target = slot_index(expert_ids, experts, exp_dev, n_expert, capacity)
    logits = jnp.dot(normed, router_weight, preferred_element_type=f32)
    expert_hot = (
        expert_ids[:, :, None] == jnp.arange(experts, dtype=jnp.int32)[None, None, :]
    ).astype(f32)
    chosen = jnp.sum(expert_hot * logits[:, None, :], axis=-1)
    top_weights = jax.nn.softmax(chosen, axis=-1)
    scaled = (
        (top_weights[:, :, None] * upstream[:, None, :].astype(f32))
        .astype(bf16)
        .reshape(tokens_here * top, width)
    )
    outgoing = jnp.zeros((total_slots, width), bf16).at[target].set(scaled)
    outgoing = outgoing.reshape(exp_dev, n_expert, capacity, width)
    incoming = lax.all_to_all(outgoing, "expert", split_axis=1, concat_axis=1, tiled=True)
    inputs = saved_inputs[0].reshape(exp_dev, slot_count, width)
    grads_in = incoming.reshape(exp_dev, slot_count, width)
    pre_gate = jnp.einsum("erd,efd->erf", inputs, gate_weight, preferred_element_type=f32)
    pre_up = jnp.einsum("erd,efd->erf", inputs, up_weight, preferred_element_type=f32)
    logistic = jax.nn.sigmoid(pre_gate)
    activated = pre_gate * logistic
    hidden = (activated * pre_up).astype(bf16)
    output = jnp.einsum("erf,efd->erd", hidden, down_weight, preferred_element_type=f32)
    score = jnp.sum(grads_in.astype(f32) * output, axis=-1).astype(bf16)
    grad_hidden = jnp.einsum("erd,efd->erf", grads_in, down_weight, preferred_element_type=f32)
    slope = logistic * (1.0 + pre_gate * (1.0 - logistic))
    grad_pre_gate = (grad_hidden * pre_up * slope).astype(bf16)
    grad_pre_up = (grad_hidden * activated).astype(bf16)
    row_grad = (
        jnp.einsum("erf,efd->erd", grad_pre_gate, gate_weight, preferred_element_type=f32)
        + jnp.einsum("erf,efd->erd", grad_pre_up, up_weight, preferred_element_type=f32)
    ).astype(bf16)
    back_rows, back_scores = (
        lax.all_to_all(
            row_grad.reshape(exp_dev, n_expert, capacity, width),
            "expert",
            split_axis=1,
            concat_axis=1,
            tiled=True,
        ),
        lax.all_to_all(
            score.reshape(exp_dev, n_expert, capacity),
            "expert",
            split_axis=1,
            concat_axis=1,
            tiled=True,
        ),
    )

    def column_terms(rows_left, source):
        return jnp.einsum("erf,erd->def", rows_left, source, preferred_element_type=f32)

    def to_output(summed_piece):
        return jnp.transpose(summed_piece, (1, 2, 0))

    summed = lax.psum_scatter(
        jnp.stack(
            [
                column_terms(grad_pre_gate, inputs),
                column_terms(grad_pre_up, inputs),
                column_terms(hidden, grads_in),
            ],
            axis=1,
        ),
        "dp",
        scatter_dimension=0,
        tiled=True,
    )
    grad_gate = to_output(summed[:, 0])
    grad_up = to_output(summed[:, 1])
    grad_down = to_output(summed[:, 2])
    returned_rows = back_rows.reshape(total_slots, width)
    gathered = returned_rows[target].astype(f32)
    expert_grad = jnp.sum(gathered.reshape(tokens_here, top, width), axis=1)
    picked = back_scores.reshape(total_slots)[target].astype(f32).reshape(tokens_here, top)
    grad_top = picked - top_weights * jnp.sum(picked, axis=1, keepdims=True)
    grad_logits = jnp.sum(expert_hot * grad_top[:, :, None], axis=1)
    router_term = jnp.dot(normed.astype(f32).T, grad_logits, precision=lax.Precision.HIGHEST)
    router_grad = lax.psum(router_term, ("dp", "expert"))
    through = jnp.dot(grad_logits, router_weight.astype(f32).T, precision=lax.Precision.HIGHEST)
    grad_normed = (expert_grad + through).astype(bf16)
    return (grad_normed, router_grad, grad_gate, grad_up, grad_down)


def solution(mesh):
    placed = (
        P(("dp", "expert"), None),
        P(("dp", "expert"), None),
        P(("dp", "expert"), None),
        P(),
        P("expert", None, None),
        P("expert", None, None),
        P("expert", None, None),
        P("dp", "expert", None, None, None),
    )
    return jax.shard_map(
        on_device,
        mesh=mesh,
        in_specs=placed,
        out_specs=(
            P(("dp", "expert"), None),
            P(),
            P("expert", None, "dp"),
            P("expert", None, "dp"),
            P("expert", None, "dp"),
        ),
        check_vma=False,
    )
```

profile of v0, /device:TPU:8, one launch (start us, length us, event | category | flops | bytes accessed | tf_op | source)
XLA Modules:
  0.0 266.2 jit_solution(6554427944809897375)
XLA Ops:
  9.1 1.3 fusion.29
  11.8 3.4 %mul.102 = f32[32,4,6144]{2,1,0:T(4,128)} broadcast(bf16[32,6144]{1,0:T(8,128)(2,1)} %param.9), dimensions={0,2} | broadcast | bytes 3538944 | tf_op jit(solution)/shard_map/mul | solution.py:37
  15.2 4.6 %mul.103 = f32[128,6144]{1,0:T(8,128)} reshape(f32[32,4,6144]{2,1,0:T(4,128)} %mul.102) | data formatting | bytes 6291456 | tf_op jit(solution)/shard_map/mul | solution.py:37
  19.8 4.6 %scatter_custom_fusion = bf16[144,6144]{1,0:T(8,128)(2,1)S(1)} fusion(s32[128]{0:T(128)S(1)} %fusion.28, f32[128,6144]{1,0:T(8,128)} %mul.103, f32[128]{0:T(128)S(1)} %div.39, bf16[]{:T(256)} %constant.38.clone.1), kind=kCustom, calls=%fused_computation.18 | custom fusion | flops 1572864 | bytes 4915714 | tf_op jit(solution)/shard_map/scatter | solution.py:41
  24.5 2.1 reshape.252
  26.6 4.6 %copy.103 = bf16[4,4,9,6144]{3,0,2,1:T(4,128)(2,1)} copy(bf16[4,4,9,6144]{3,2,1,0:T(8,128)(2,1)} %reshape.252) | data formatting | bytes 3538944 | tf_op jit(solution)/shard_map/reshape | solution.py:42
  31.1 4.4 %all-to-all-start = ((bf16[4,4,9,6144]{3,0,2,1:T(4,128)(2,1)}), bf16[4,4,9,6144]{3,0,2,1:T(4,128)(2,1)}, u32[]{:S(2)}, u32[]{:S(2)}) async-start(bf16[4,4,9,6144]{3,0,2,1:T(4,128)(2,1)} %copy.103), calls=%async_computation | async-start | bytes 3538944 | tf_op jit(solution)/shard_map/all_to_all | solution.py:43
  35.8 2.9 %copy.106 = bf16[1,4,4,9,6144]{4,1,3,2,0:T(4,128)(2,1)S(1)} copy(bf16[1,4,4,9,6144]{4,2,3,1,0:T(4,128)(2,1)} %param.15) | data formatting | bytes 3538944 | tf_op args[7]
  38.7 1.7 fusion.10
  40.4 16.8 %all-to-all-done = bf16[4,4,9,6144]{3,0,2,1:T(4,128)(2,1)} async-done(((bf16[4,4,9,6144]{3,0,2,1:T(4,128)(2,1)}), bf16[4,4,9,6144]{3,0,2,1:T(4,128)(2,1)}, u32[]{:S(2)}, u32[]{:S(2)}) %all-to-all-start) | async-done | bytes 1769504 | tf_op jit(solution)/shard_map/all_to_all | solution.py:43
  57.2 3.5 %fusion.3 = f32[4,36,20]{1,2,0:T(8,128)S(1)} fusion(bf16[4,36,6144]{2,0,1:T(4,128)(2,1)} %bitcast.2, bf16[4,20,6144]{2,0,1:T(4,128)(2,1)} %param.14), kind=kOutput, calls=%fused_computation.15 | convolution fusion | flops 35389440 | bytes 2764032 | tf_op jit(solution)/shard_map/erd,efd->erf/dot_general | solution.py:53
  60.7 1.7 multiply_convert_fusion.2
  62.4 3.5 %convolution_bitcast_fusion = f32[6144,1,4,20]{0,3,2,1:T(8,128)S(1)} fusion(bf16[4,36,20]{1,2,0:T(8,128)(2,1)S(1)} %get-tuple-element.33, bf16[4,36,6144]{2,0,1:T(4,128)(2,1)} %bitcast.2), kind=kOutput, calls=%fused_computation.6 | convolution fusion | flops 35389440 | bytes 3741312 | tf_op jit(solution)/shard_map/erf,erd->def/dot_general | solution.py:79
  65.9 2.2 convolution_bitcast_fusion.2
  68.1 2.4 convolution_bitcast_fusion.1
  70.5 3.5 %pad_maximum_fusion = f32[6144,3,4,20]{0,3,2,1:T(8,128)} fusion(f32[6144,1,4,20]{0,3,2,1:T(8,128)S(1)} %convolution_bitcast_fusion, f32[6144,1,4,20]{0,3,2,1:T(8,128)S(1)} %convolution_bitcast_fusion.1, f32[6144,1,4,20]{0,3,2,1:T(8,128)S(1)} %convolution_bitcast_fusion.2), kind=kLoop, calls=%fused_computation.9 | loop fusion | flops 2949120 | bytes 11796480 | tf_op jit(solution)/shard_map/stack | solution.py:85
  74.0 5.2 %fusion.5 = bf16[4,36]{1,0:T(4,128)(2,1)S(1)} fusion(bf16[4,36,20]{1,2,0:T(8,128)(2,1)S(1)} %get-tuple-element.33, bf16[4,36,6144]{2,0,1:T(4,128)(2,1)} %bitcast.2, bf16[4,20,6144]{2,0,1:T(4,128)(2,1)} %param.14), kind=kOutput, calls=%fused_computation.17 | convolution fusion | flops 38043504 | bytes 2758560 | tf_op jit(solution)/shard_map/erf,efd->erd/dot_general | solution.py:51
  79.9 3.2 %all-to-all-start.2 = ((bf16[4,4,9]{2,0,1:T(4,128)(2,1)}), bf16[4,4,9]{2,0,1:T(4,128)(2,1)S(1)}, u32[]{:S(2)}, u32[]{:S(2)}) async-start(bf16[4,4,9]{2,0,1:T(4,128)(2,1)} %copy.117), calls=%async_computation.2 | async-start | bytes 8192 | tf_op jit(solution)/shard_map/all_to_all | solution.py:69
  83.2 1.8 fusion.14
  85.0 2.0 fusion
  87.0 2.7 %copy.113 = bf16[4,36,6144]{2,0,1:T(4,128)(2,1)} copy(bf16[4,36,6144]{2,1,0:T(8,128)(2,1)S(1)} %fusion) | data formatting | bytes 3538944 | tf_op jit(solution)/shard_map/convert_element_type | solution.py:60
  89.6 4.3 %all-to-all-start.1 = ((bf16[4,4,9,6144]{3,0,2,1:T(4,128)(2,1)}), bf16[4,4,9,6144]{3,0,2,1:T(4,128)(2,1)S(1)}, u32[]{:S(2)}, u32[]{:S(2)}) async-start(bf16[4,4,9,6144]{3,0,2,1:T(4,128)(2,1)} %bitcast.4), calls=%async_computation.1 | async-start | bytes 3538944 | tf_op jit(solution)/shard_map/all_to_all | solution.py:62
  96.7 17.8 %all-to-all-done.1 = bf16[4,4,9,6144]{3,0,2,1:T(4,128)(2,1)S(1)} async-done(((bf16[4,4,9,6144]{3,0,2,1:T(4,128)(2,1)}), bf16[4,4,9,6144]{3,0,2,1:T(4,128)(2,1)S(1)}, u32[]{:S(2)}, u32[]{:S(2)}) %all-to-all-start.1) | async-done | bytes 1769504 | tf_op jit(solution)/shard_map/all_to_all | solution.py:62
  114.5 2.8 %copy.114 = bf16[4,4,9,6144]{3,2,1,0:T(8,128)(2,1)} copy(bf16[4,4,9,6144]{3,0,2,1:T(4,128)(2,1)S(1)} %all-to-all-done.1) | data formatting | bytes 3538944 | tf_op jit(solution)/shard_map/all_to_all | solution.py:62
  117.3 2.4 reshape.255
  119.7 2.6 gather_fusion
  122.3 4.0 %reshape.257 = f32[32,4,6144]{2,1,0:T(4,128)} reshape(bf16[128,6144]{1,0:T(8,128)(2,1)} %gather_fusion) | data formatting | bytes 4718592 | tf_op jit(solution)/shard_map/convert_element_type | solution.py:101
  126.3 3.9 %reduce_sum.69 = f32[32,6144]{1,0:T(8,128)S(1)} reduce(f32[32,4,6144]{2,1,0:T(4,128)} %reshape.257, f32[]{:T(128)} %constant.47.clone.1), dimensions={1}, to_apply=%region_6.7 | reduce | flops 589824 | bytes 3932164 | tf_op jit(solution)/shard_map/reduce_sum | solution.py:102
  130.2 1.3 fusion.1
  131.5 18.5 %reduce-scatter.2.cloned.1.call-done = f32[768,3,4,20]{0,3,2,1:T(8,128)} async-done(((f32[6144,3,4,20]{0,3,2,1:T(8,128)}), f32[768,3,4,20]{0,3,2,1:T(8,128)}) %reduce-scatter.2.cloned.1.call-update) | async-done | bytes 737296 | tf_op jit(solution)/shard_map/reduce_scatter | solution.py:84
  153.6 103.4 %all-reduce.2.cloned.1.call-done = f32[6144,16]{0,1:T(8,128)} async-done(((f32[6144,16]{0,1:T(8,128)}), f32[6144,16]{0,1:T(8,128)}) %all-reduce.2.cloned.1.call-update) | async-done | bytes 393232 | tf_op jit(solution)/shard_map/psum | solution.py:107
  257.0 1.8 copy.158
  (46 shorter events, 9.7 us)
Async XLA Ops:
  8.0 52.7 %copy-start = (bf16[4,20,6144]{2,0,1:T(4,128)(2,1)S(1)}, bf16[4,20,6144]{2,0,1:T(4,128)(2,1)}, u32[]{:S(2)}) copy-start(bf16[4,20,6144]{2,0,1:T(4,128)(2,1)} %param.13) | copy-start | bytes 2949124
  31.1 26.1 %all-to-all-start = ((bf16[4,4,9,6144]{3,0,2,1:T(4,128)(2,1)}), bf16[4,4,9,6144]{3,0,2,1:T(4,128)(2,1)}, u32[]{:S(2)}, u32[]{:S(2)}) async-start(bf16[4,4,9,6144]{3,0,2,1:T(4,128)(2,1)} %copy.103), calls=%async_computation | async-start | bytes 3538944 | tf_op jit(solution)/shard_map/all_to_all | solution.py:43
  35.5 114.5 %reduce-scatter.2.cloned.1.call-start = ((), (), s32[]{:S(2)}) async-start(), calls=%async_computation.5 | async-start | bytes 7962624 | tf_op jit(solution)/shard_map/reduce_scatter | solution.py:84
  35.8 2.9 %copy-start.2 = (bf16[4,20,6144]{2,0,1:T(4,128)(2,1)S(1)}, bf16[4,20,6144]{2,0,1:T(4,128)(2,1)}, u32[]{:S(2)}) copy-start(bf16[4,20,6144]{2,0,1:T(4,128)(2,1)} %param.12) | copy-start | bytes 2949124
  74.0 9.2 %copy-start.3 = (bf16[4,20,6144]{2,0,1:T(4,128)(2,1)S(1)}, bf16[4,20,6144]{2,0,1:T(4,128)(2,1)}, u32[]{:S(2)}) copy-start(bf16[4,20,6144]{2,0,1:T(4,128)(2,1)} %param.12) | copy-start | bytes 2949124
  79.9 9.7 %all-to-all-start.2 = ((bf16[4,4,9]{2,0,1:T(4,128)(2,1)}), bf16[4,4,9]{2,0,1:T(4,128)(2,1)S(1)}, u32[]{:S(2)}, u32[]{:S(2)}) async-start(bf16[4,4,9]{2,0,1:T(4,128)(2,1)} %copy.117), calls=%async_computation.2 | async-start | bytes 8192 | tf_op jit(solution)/shard_map/all_to_all | solution.py:69
  89.6 6.0 %copy-start.5 = (s32[32,4]{0,1:T(4,128)S(1)}, s32[32,4]{0,1:T(4,128)}, u32[]{:S(2)}) copy-start(s32[32,4]{0,1:T(4,128)} %param.10) | copy-start | bytes 1540
  89.6 6.0 %copy-start.1 = (bf16[32,6144]{1,0:T(8,128)(2,1)S(1)}, bf16[32,6144]{1,0:T(8,128)(2,1)}, u32[]{:S(2)}) copy-start(bf16[32,6144]{1,0:T(8,128)(2,1)} %param.8) | copy-start | bytes 1179652
  89.6 24.8 %all-to-all-start.1 = ((bf16[4,4,9,6144]{3,0,2,1:T(4,128)(2,1)}), bf16[4,4,9,6144]{3,0,2,1:T(4,128)(2,1)S(1)}, u32[]{:S(2)}, u32[]{:S(2)}) async-start(bf16[4,4,9,6144]{3,0,2,1:T(4,128)(2,1)} %bitcast.4), calls=%async_computation.1 | async-start | bytes 3538944 | tf_op jit(solution)/shard_map/all_to_all | solution.py:62
  93.9 163.1 %all-reduce.2.cloned.1.call-start = ((), (), s32[]{:S(2)}) async-start(), calls=%async_computation.4 | async-start | bytes 786432 | tf_op jit(solution)/shard_map/psum | solution.py:107
  126.3 3.9 %copy-start.4 = (bf16[6144,16]{0,1:T(8,128)(2,1)S(1)}, bf16[6144,16]{0,1:T(8,128)(2,1)}, u32[]{:S(2)}) copy-start(bf16[6144,16]{0,1:T(8,128)(2,1)} %param.11) | copy-start | bytes 589828
Sparse Core Ops, SparseCore 0:
  74.1 75.8 reduce-scatter.1
Sparse Core Ops, SparseCore 1:
  100.3 156.7 all-reduce.1
where the time goes:
time: 269 us; the launch traced here: 266 us
  waiting for transfers between devices  157 us (58%)
  local copies, waits for them, and re-layouts  41 us (15%)
  matrix products  27.5 us (10%)
  between operations  15.7 us (6%)
  other arithmetic  13.3 us (5%)
  starting transfers between devices  12.1 us (4%)
    psum x1, waiting for transfers between devices, on_device(): router_grad = lax.psum(router_term, ('dp', 'expert'))  103 us
    reduce_scatter x1, waiting for transfers between devices, on_device(): lax.psum_scatter(jnp.stack([column_terms(grad_pre_gate, inputs), column_t...  18.5 us
    all_to_all x1, waiting for transfers between devices, on_device(): lax.all_to_all(row_grad.reshape(exp_dev, n_expert, capacity, width), 'exp...  17.8 us
    all_to_all x1, waiting for transfers between devices, on_device(): lax.all_to_all(outgoing, 'expert', split_axis=1, concat_axis=1, tiled=True)  16.8 us
    dot_general x3, matrix products, column_terms(): jnp.einsum('erf,erd->def', rows_left, source, preferred_element_type=f32)  8.1 us
    mul x2, local copies, waits for them, and re-layouts, on_device(): top_weights[:, :, None] * upstream[:, None, :].astype(f32)  8.05 us
    unnamed x18, local copies, waits for them, and re-layouts  7.94 us
    reshape x2, local copies, waits for them, and re-layouts, on_device(): outgoing = outgoing.reshape(exp_dev, n_expert, capacity, width)  6.68 us
  transfers between devices with their start and end apart: 5, of which 4 were waited for; matrix products, arithmetic and copies ran while one was open for 15% of the time, Pallas kernels for 0%

commit v1 on v0

v1 whole, which is shorter than its diff:
```python
import functools

import jax
import jax.numpy as jnp
from jax import lax
from jax.experimental import pallas as pl
from jax.experimental.pallas import tpu as pltpu
from jax.sharding import PartitionSpec as P

F32 = jnp.float32
BF16 = jnp.bfloat16
LANES = 128
VMEM_BYTES = 48 * 2**20
HIGHEST = lax.Precision.HIGHEST


def dot(left, right, contract, precision=None):
    return lax.dot_general(
        left,
        right,
        ((contract[:1], contract[1:]), ((), ())),
        precision=precision,
        preferred_element_type=F32,
    )


def iota(shape, dim):
    return lax.broadcasted_iota(jnp.int32, shape, dim)


def whole(count):
    return [pl.BlockSpec(memory_space=pltpu.VMEM)] * count


def params(**more):
    return pltpu.CompilerParams(vmem_limit_bytes=VMEM_BYTES, **more)


def split_high_low(value):
    high = value.astype(BF16)
    return high, (value - high.astype(F32)).astype(BF16)


def route_kernel(experts, normed, router, ids, packed):
    tokens = normed.shape[0]
    logits = dot(normed[...], router[...], (1, 1))
    lane = iota((tokens, experts), 1)
    named = lane < 0
    for k in range(ids.shape[1]):
        named = named | (ids[:, k : k + 1] == lane)
    earlier = (iota((tokens, tokens), 1) < iota((tokens, tokens), 0)).astype(BF16)
    slot = dot(earlier, named.astype(F32).astype(BF16), (1, 0))
    largest = jnp.max(jnp.where(named, logits, -jnp.inf), axis=1, keepdims=True)
    weight = jnp.where(named, jnp.exp(jnp.where(named, logits - largest, 0.0)), 0.0)
    weight = weight / jnp.sum(weight, axis=1, keepdims=True)
    code = jnp.where(named, slot + 1.0, 0.0)
    packed[...] = jnp.concatenate(
        [weight, code, jnp.zeros((tokens, LANES - 2 * experts), F32)], axis=1
    )


def expert_kernel(sizes, me, *refs):
    n_expert, exp_dev, capacity, tokens_here = sizes
    rows_u, packs, rest = refs[:n_expert], refs[n_expert : 2 * n_expert], refs[2 * n_expert :]
    down, pre_gate, pre_up = rest[:3]
    scores = rest[3 : 3 + n_expert]
    tok_gate, tok_up, tok_hidden, slot_gate, slot_up = rest[3 + n_expert :]
    me = me[0]
    experts = exp_dev * n_expert
    tokens = tokens_here * n_expert
    hidden_all = down.shape[0]
    slots = exp_dev * capacity * n_expert
    packed = jnp.concatenate([p[...] for p in packs], axis=0)
    arrived = jnp.concatenate([u[...] for u in rows_u], axis=0)
    grad_hidden_raw = dot(arrived, down[...], (1, 1))

    lane_of_slot = me * exp_dev + iota((LANES, slots), 1) // (capacity * n_expert)
    pick_weight = (iota((LANES, slots), 0) == lane_of_slot).astype(F32)
    pick_code = (iota((LANES, slots), 0) == lane_of_slot + experts).astype(F32)
    weight_at = dot(packed, pick_weight, (1, 0), HIGHEST)
    code_at = dot(packed, pick_code, (1, 0))
    column = iota((tokens, slots), 1)
    source = me ^ (iota((tokens, slots), 0) // tokens_here)
    slot_code = ((column // n_expert) % capacity + 1).astype(F32)
    chosen = (source == column % n_expert) & (jnp.abs(code_at - slot_code) < 0.5)
    place = chosen.astype(F32).astype(BF16)
    place_weight = jnp.where(chosen, weight_at, 0.0)

    grad_hidden = dot(place_weight, grad_hidden_raw, (0, 0), HIGHEST)
    same = iota((slots, hidden_all), 1) % exp_dev == iota((slots, hidden_all), 0) // (capacity * n_expert)
    v = pre_gate[...]
    logistic = jax.nn.sigmoid(v)
    activated = v * logistic
    hidden = jnp.where(same, activated * pre_up[...], 0.0).astype(BF16)
    slope = logistic * (1.0 + v * (1.0 - logistic))
    grad_gate = jnp.where(same, grad_hidden * pre_up[...] * slope, 0.0).astype(BF16)
    grad_up = jnp.where(same, grad_hidden * activated, 0.0).astype(BF16)
    score = jnp.sum(hidden.astype(F32) * grad_hidden, axis=1, keepdims=True)
    lane_of_row = me * exp_dev + iota((slots, LANES), 0) // (capacity * n_expert)
    score = jnp.where(iota((slots, LANES), 1) == lane_of_row, score, 0.0).astype(BF16)
    picked = dot(place, score, (1, 0)).astype(BF16)
    for r in range(n_expert):
        scores[r][...] = picked[r * tokens_here : (r + 1) * tokens_here]
    slot_gate[...] = grad_gate
    slot_up[...] = grad_up
    tok_gate[...] = dot(place, grad_gate, (1, 0)).astype(BF16)
    tok_up[...] = dot(place, grad_up, (1, 0)).astype(BF16)
    lane_of_hidden = me * exp_dev + iota((LANES, hidden_all), 1) % exp_dev
    pick_hidden = (iota((LANES, hidden_all), 0) == lane_of_hidden).astype(F32)
    weight_hidden = dot(packed, pick_hidden, (1, 0), HIGHEST)
    tok_hidden[...] = (dot(place, hidden, (1, 0)) * weight_hidden).astype(BF16)


def weight_kernel(n_expert, at, slot_gate, slot_up, tok_hidden, inputs, *refs):
    del at
    rows_u, out = refs[:n_expert], refs[n_expert]
    n = slot_gate.shape[1]
    arrived = jnp.concatenate([u[...] for u in rows_u], axis=0)
    out[0, :n] = dot(slot_gate[...], inputs[...], (0, 0)).astype(out.dtype)
    out[0, n : 2 * n] = dot(slot_up[...], inputs[...], (0, 0)).astype(out.dtype)
    out[0, 2 * n :] = dot(tok_hidden[...], arrived, (0, 0)).astype(out.dtype)


def row_kernel(n_expert, tok_gate, tok_up, gate, up, *outs):
    total = dot(tok_gate[...], gate[...], (1, 0)) + dot(tok_up[...], up[...], (1, 0))
    size = total.shape[0] // n_expert
    for r in range(n_expert):
        outs[r][...] = total[r * size : (r + 1) * size].astype(outs[r].dtype)


def add_kernel(mine, theirs, *outs):
    for r in range(len(outs)):
        outs[r][...] = (mine[r].astype(F32) + theirs[r].astype(F32)).astype(outs[r].dtype)


def sum_kernel(*refs):
    pieces, outs = refs[:-3], refs[-3:]
    total = pieces[0][...].astype(F32)
    for piece in pieces[1:]:
        total = total + piece[...].astype(F32)
    n = total.shape[0] // 3
    for k in range(3):
        outs[k][...] = total[k * n : (k + 1) * n]


def router_kernel(experts, n_expert, at, *refs):
    del at
    scores, (packed, normed, router, term, through) = refs[:n_expert], refs[n_expert:]
    picked = scores[0][...].astype(F32)
    for s in scores[1:]:
        picked = picked + s[...].astype(F32)
    picked = picked[:, :experts]
    weight, code = packed[:, :experts], packed[:, experts : 2 * experts]
    grad = jnp.where(code > 0.5, picked - weight * jnp.sum(picked, axis=1, keepdims=True), 0.0)
    high, low = split_high_low(grad)
    term[...] = dot(high, normed[...], (0, 0)) + dot(low, normed[...], (0, 0))
    through[...] = dot(high, router[...], (1, 0)) + dot(low, router[...], (1, 0))


def final_kernel(*refs):
    pieces, out = refs[:-1], refs[-1]
    total = pieces[0][...].astype(F32)
    for piece in pieces[1:]:
        total = total + piece[...].astype(F32)
    out[...] = total.astype(out.dtype)


def on_device(normed, upstream, expert_ids, router_weight, gate_weight, up_weight, down_weight, saved_inputs):
    n_expert = lax.axis_size("expert")
    n_dp = lax.axis_size("dp")
    n_chip = n_dp // 2
    me = lax.axis_index("expert")
    dp = lax.axis_index("dp")
    core = dp & 1
    chip = dp >> 1
    exp_dev, hidden_units, width = gate_weight.shape
    capacity = saved_inputs.shape[3]
    experts = exp_dev * n_expert
    tokens_here = normed.shape[0]
    tokens = tokens_here * n_expert
    slots = exp_dev * capacity * n_expert
    hidden_all = exp_dev * hidden_units
    piece = width // n_dp
    shape = jax.ShapeDtypeStruct

    def over_expert(value, k):
        return lax.ppermute(value, "expert", [(i, i ^ k) for i in range(n_expert)])

    def over_core(value):
        return lax.ppermute(value, "dp", [(i, i ^ 1) for i in range(n_dp)])

    def over_chip(value, k):
        return lax.ppermute(value, "dp", [(i, i ^ (2 * k)) for i in range(n_dp)])

    def flat(weight):
        return jnp.transpose(weight, (1, 0, 2)).reshape(hidden_all, width)

    rows_u = [upstream] + [over_expert(upstream, k) for k in range(1, n_expert)]
    router = router_weight.T
    packed = pl.pallas_call(
        functools.partial(route_kernel, experts),
        out_shape=shape((tokens_here, LANES), F32),
        in_specs=whole(3),
        out_specs=pl.BlockSpec(memory_space=pltpu.VMEM),
        compiler_params=params(),
        name="route",
    )(normed, router, expert_ids)
    packs = [packed] + [over_expert(packed, k) for k in range(1, n_expert)]

    inputs = jnp.transpose(saved_inputs[0], (0, 2, 1, 3)).reshape(slots, width)
    gate, up, down = flat(gate_weight), flat(up_weight), flat(down_weight)
    pre_gate = dot(inputs, gate, (1, 1))
    pre_up = dot(inputs, up, (1, 1))

    here = jnp.stack([me]).astype(jnp.int32)
    outs = pl.pallas_call(
        functools.partial(expert_kernel, (n_expert, exp_dev, capacity, tokens_here)),
        out_shape=[shape((tokens_here, LANES), BF16)] * n_expert
        + [shape((tokens, hidden_all), BF16)] * 3
        + [shape((slots, hidden_all), BF16)] * 2,
        in_specs=[pl.BlockSpec(memory_space=pltpu.SMEM)] + whole(2 * n_expert + 3),
        out_specs=whole(n_expert + 5),
        compiler_params=params(),
        name="experts",
    )(here, *rows_u, *packs, down, pre_gate, pre_up)
    scores = outs[:n_expert]
    tok_gate, tok_up, tok_hidden, slot_gate, slot_up = outs[n_expert:]

    def weight_terms(owner_core, dtype):
        if piece % LANES:
            arrived = jnp.concatenate(rows_u, axis=0)
            terms = [dot(slot_gate, inputs, (0, 0)), dot(slot_up, inputs, (0, 0)), dot(tok_hidden, arrived, (0, 0))]
            terms = jnp.concatenate(terms, axis=0).reshape(3 * hidden_all, n_chip, 2, piece)
            terms = jnp.transpose(terms, (2, 1, 0, 3))[owner_core]
            return terms[chip ^ jnp.arange(n_chip)].astype(dtype)

        def block(r, at):
            return (0, 2 * (at[0] ^ r) + at[1])

        def same(r, at):
            return (0, 0)

        return pl.pallas_call(
            functools.partial(weight_kernel, n_expert),
            out_shape=shape((n_chip, 3 * hidden_all, piece), dtype),
            grid_spec=pltpu.PrefetchScalarGridSpec(
                num_scalar_prefetch=1,
                grid=(n_chip,),
                in_specs=[
                    pl.BlockSpec((slots, hidden_all), same),
                    pl.BlockSpec((slots, hidden_all), same),
                    pl.BlockSpec((tokens, hidden_all), same),
                    pl.BlockSpec((slots, piece), block),
                ]
                + [pl.BlockSpec((tokens_here, piece), block)] * n_expert,
                out_specs=pl.BlockSpec((1, 3 * hidden_all, piece), lambda r, at: (r, 0, 0)),
            ),
            compiler_params=params(),
            name="weight_terms",
        )(jnp.stack([chip, owner_core]).astype(jnp.int32), slot_gate, slot_up, tok_hidden, inputs, *rows_u)

    theirs = weight_terms(1 - core, BF16)
    from_core = over_core(theirs)
    mine = weight_terms(core, F32)

    row_pieces = pl.pallas_call(
        functools.partial(row_kernel, n_expert),
        out_shape=[shape((tokens_here, width), BF16)] * n_expert,
        grid=(8,),
        in_specs=[
            pl.BlockSpec((tokens, hidden_all), lambda j: (0, 0)),
            pl.BlockSpec((tokens, hidden_all), lambda j: (0, 0)),
            pl.BlockSpec((hidden_all, width // 8), lambda j: (0, j)),
            pl.BlockSpec((hidden_all, width // 8), lambda j: (0, j)),
        ],
        out_specs=[pl.BlockSpec((tokens_here, width // 8), lambda j: (0, j))] * n_expert,
        compiler_params=params(),
        name="row_terms",
    )(tok_gate, tok_up, gate, up)

    back_scores = [scores[0]] + [over_expert(scores[k], k) for k in range(1, n_expert)]
    back_rows = [row_pieces[0]] + [over_expert(row_pieces[k], k) for k in range(1, n_expert)]

    band = 3 * hidden_all if hidden_all % 16 else hidden_all
    chip_sums = pl.pallas_call(
        add_kernel,
        out_shape=[shape((3 * hidden_all, piece), F32)] + [shape((3 * hidden_all, piece), BF16)] * (n_chip - 1),
        grid=(3 * hidden_all // band,),
        in_specs=[pl.BlockSpec((n_chip, band, piece), lambda j: (0, j, 0))] * 2,
        out_specs=[pl.BlockSpec((band, piece), lambda j: (j, 0))] * n_chip,
        compiler_params=params(),
        name="core_sum",
    )(mine, from_core)
    chip_pieces = [chip_sums[0]] + [over_chip(chip_sums[k], k) for k in range(1, n_chip)]

    half = width // 2

    def parts(j, at):
        return (0, jnp.where(j == 0, 1 - at[0], at[0]))

    term, through = pl.pallas_call(
        functools.partial(router_kernel, experts, n_expert),
        out_shape=[shape((experts, width), F32), shape((tokens_here, width), F32)],
        grid_spec=pltpu.PrefetchScalarGridSpec(
            num_scalar_prefetch=1,
            grid=(2,),
            in_specs=[pl.BlockSpec((tokens_here, LANES), lambda j, at: (0, 0))] * (n_expert + 1)
            + [pl.BlockSpec((tokens_here, half), parts), pl.BlockSpec((experts, half), parts)],
            out_specs=[
                pl.BlockSpec((experts, half), lambda j, at: (0, j)),
                pl.BlockSpec((tokens_here, half), parts),
            ],
        ),
        compiler_params=params(),
        name="router_terms",
    )(jnp.stack([core]).astype(jnp.int32), *back_scores, packed, normed, router)
    total = term[:, half:] + over_core(term[:, :half])
    for k in range(n_expert.bit_length() - 1):
        low = total.astype(BF16)
        total = low.astype(F32) + over_expert(low, 1 << k).astype(F32)
    for k in range(n_chip.bit_length() - 1):
        low = total.astype(BF16)
        total = low.astype(F32) + over_chip(low, 1 << k).astype(F32)
    other = over_core(total)
    router_grad = jnp.where(
        core == 0, jnp.concatenate([total, other], axis=1), jnp.concatenate([other, total], axis=1)
    ).T

    grad_normed = pl.pallas_call(
        final_kernel,
        out_shape=shape((tokens_here, width), BF16),
        in_specs=whole(n_expert + 1),
        out_specs=pl.BlockSpec(memory_space=pltpu.VMEM),
        compiler_params=params(),
        name="grad_normed",
    )(through, *back_rows)
    grads = pl.pallas_call(
        sum_kernel,
        out_shape=[shape((hidden_all, piece), F32)] * 3,
        in_specs=whole(n_chip),
        out_specs=whole(3),
        compiler_params=params(),
        name="weight_sum",
    )(*chip_pieces)
    grads = [jnp.transpose(g.reshape(hidden_units, exp_dev, piece), (1, 0, 2)) for g in grads]
    return (grad_normed, router_grad, *grads)


def solution(mesh):
    placed = (
        P(("dp", "expert"), None),
        P(("dp", "expert"), None),
        P(("dp", "expert"), None),
        P(),
        P("expert", None, None),
        P("expert", None, None),
        P("expert", None, None),
        P("dp", "expert", None, None, None),
    )
    return jax.shard_map(
        on_device,
        mesh=mesh,
        in_specs=placed,
        out_specs=(
            P(("dp", "expert"), None),
            P(),
            P("expert", None, "dp"),
            P("expert", None, "dp"),
            P("expert", None, "dp"),
        ),
        check_vma=False,
    )
```

time: 269 us -> 142 us (0.53)
  waiting for transfers between devices: 157 us -> 53.7 us
  Pallas kernels: 0 us -> 23.9 us
  matrix products: 27.5 us -> 3.69 us
  between operations: 15.7 us -> 0.8 us
  starting transfers between devices: 12.1 us -> 22.8 us
  local copies, waits for them, and re-layouts: 41 us -> 31.2 us
  other arithmetic: 13.3 us -> 4.54 us
    psum x1 -> x0, waiting for transfers between devices: 103 us -> none  [on_device(): router_grad = lax.psum(router_term, ('dp', 'expert'))]
    ppermute x0 -> x22, waiting for transfers between devices: none -> 53.7 us  [the longest x5 29.1 us: over_chip(): return lax.ppermute(value, 'dp', [(i, i ^ 2 * k) for i in range(n_dp)])]
    all_to_all x3 -> x0, waiting for transfers between devices: 34.6 us -> none  [the longest x1 17.8 us: on_device(): lax.all_to_all(row_grad.reshape(exp_dev, n_expert, capacity, width), 'exp...]
    dot_general x12 -> x2, matrix products: 27.5 us -> 3.69 us  [dot(): lax.dot_general(left, right, ((contract[:1], contract[1:]), ((), ())), pr...]
    pallas_call x0 -> x9, Pallas kernels: none -> 23.9 us  [the longest x2 9.03 us: weight_terms(): pl.pallas_call(functools.partial(weight_kernel, n_expert), out_shape=shap...]
    ppermute x0 -> x22, starting transfers between devices: none -> 22.8 us  [the longest x14 16 us: over_expert(): return lax.ppermute(value, 'expert', [(i, i ^ k) for i in range(n_expert)])]
    reduce_scatter x1 -> x0, waiting for transfers between devices: 18.5 us -> none  [on_device(): lax.psum_scatter(jnp.stack([column_terms(grad_pre_gate, inputs), column_t...]
    unnamed x18 -> x61, local copies, waits for them, and re-layouts: 7.94 us -> 19.9 us
  transfers between devices with their start and end apart: 5 -> 22, of which waited for: 4 -> 12; matrix products, arithmetic and copies ran while one was open for 15% -> 11% of each run, Pallas kernels for 0% -> 13%
where the time goes in v1:
time: 142 us; the launch traced here: 141 us
  waiting for transfers between devices  53.7 us (38%)
  local copies, waits for them, and re-layouts  31.2 us (22%)
  Pallas kernels  23.9 us (17%)
  starting transfers between devices  22.8 us (16%)
  other arithmetic  4.54 us (3%)
  matrix products  3.69 us (3%)
    ppermute x5, waiting for transfers between devices, over_chip(): return lax.ppermute(value, 'dp', [(i, i ^ 2 * k) for i in range(n_dp)])  29.1 us
    ppermute x14, waiting for transfers between devices, over_expert(): return lax.ppermute(value, 'expert', [(i, i ^ k) for i in range(n_expert)])  23.2 us
    unnamed x61, local copies, waits for them, and re-layouts  19.9 us
    ppermute x14, starting transfers between devices, over_expert(): return lax.ppermute(value, 'expert', [(i, i ^ k) for i in range(n_expert)])  16 us
    pallas_call x2, Pallas kernels, weight_terms(): pl.pallas_call(functools.partial(weight_kernel, n_expert), out_shape=shap...  9.03 us
    ppermute x5, starting transfers between devices, over_chip(): return lax.ppermute(value, 'dp', [(i, i ^ 2 * k) for i in range(n_dp)])  6.72 us
    reshape x3, local copies, waits for them, and re-layouts, flat(): return jnp.transpose(weight, (1, 0, 2)).reshape(hidden_all, width)  6.57 us
    pallas_call x1, Pallas kernels, on_device(): pl.pallas_call(functools.partial(row_kernel, n_expert), out_shape=[shape(...  4.01 us
  transfers between devices with their start and end apart: 22, of which 12 were waited for; matrix products, arithmetic and copies ran while one was open for 11% of the time, Pallas kernels for 13%

profile of v1, /device:TPU:8, one launch (start us, length us, event | category | flops | bytes accessed | tf_op | source)
XLA Modules:
  0.0 140.6 jit_solution(14635151115471979704)
XLA Ops:
  3.7 2.5 %collective-permute-start.5 = (f32[32,128]{1,0:T(8,128)S(1)}, f32[32,128]{1,0:T(8,128)}, u32[]{:S(2)}, u32[]{:S(2)}) collective-permute-start(f32[32,128]{1,0:T(8,128)S(1)} %route.1.refs_4_), channel_id=1, source_target_pairs={{0,3},{1,2},{2,1},{3,0},{4,7},{5,6},{6,5},{7,4},{8,11},{9,10},{10,... | collective-permute-start | bytes 49160 | tf_op jit(solution)/shard_map/ppermute | solution.py:187
  6.8 1.5 %collective-permute-start.2 = (bf16[32,6144]{1,0:T(8,128)(2,1)}, bf16[32,6144]{1,0:T(8,128)(2,1)S(1)}, u32[]{:S(2)}, u32[]{:S(2)}) collective-permute-start(bf16[32,6144]{1,0:T(8,128)(2,1)} %refs_0_.5), channel_id=1, source_target_pairs={{0,3},{1,2},{2,1},{3,0},{4,7},{5,6},{6,5},{7,4},{8,11},{9,10},{10,... | collective-permute-start | bytes 1179656 | tf_op jit(solution)/shard_map/ppermute | solution.py:187
  8.7 1.5 %collective-permute-start = (bf16[32,6144]{1,0:T(8,128)(2,1)}, bf16[32,6144]{1,0:T(8,128)(2,1)}, u32[]{:S(2)}, u32[]{:S(2)}) collective-permute-start(bf16[32,6144]{1,0:T(8,128)(2,1)} %refs_0_.5), channel_id=1, source_target_pairs={{0,1},{1,0},{2,3},{3,2},{4,5},{5,4},{6,7},{7,6},{8,9},{9,8},{10,11... | collective-permute-start | bytes 1179656 | tf_op jit(solution)/shard_map/ppermute | solution.py:187
  10.2 1.7 %reshape.34.up = bf16[80,6144]{1,0:T(8,128)(2,1)S(1)} reshape(bf16[20,4,6144]{2,1,0:T(4,128)(2,1)} %bitcast.23) | data formatting | bytes 1966080 | tf_op jit(solution)/shard_map/reshape | solution.py:196
  11.9 2.4 %reshape.32.inputs = bf16[144,6144]{1,0:T(8,128)(2,1)S(1)} reshape(bf16[4,9,4,6144]{3,2,1,0:T(4,128)(2,1)} %bitcast.22) | data formatting | bytes 3538944 | tf_op jit(solution)/shard_map/reshape | solution.py:210
  14.4 1.2 fusion.2.refs_10_
  15.6 2.4 %reshape.33.gate = bf16[80,6144]{1,0:T(8,128)(2,1)} reshape(bf16[20,4,6144]{2,1,0:T(4,128)(2,1)} %bitcast.24) | data formatting | bytes 1966080 | tf_op jit(solution)/shard_map/reshape | solution.py:196
  18.6 2.4 %fusion.1.refs_9_ = f32[144,80]{1,0:T(8,128)} fusion(bf16[144,6144]{1,0:T(8,128)(2,1)S(1)} %reshape.32.inputs, bf16[80,6144]{1,0:T(8,128)(2,1)} %reshape.33.gate), kind=kOutput, calls=%fused_computation.9 | convolution fusion | flops 141557760 | bytes 2798592 | tf_op jit(solution)/shard_map/dot_general | solution.py:18
  21.0 2.4 %reshape.31.refs_8_ = bf16[80,6144]{1,0:T(8,128)(2,1)} reshape(bf16[20,4,6144]{2,1,0:T(4,128)(2,1)} %bitcast.25) | data formatting | bytes 1966080 | tf_op jit(solution)/shard_map/reshape | solution.py:196
  23.5 3.7 %collective-permute-done.3.refs_5_ = f32[32,128]{1,0:T(8,128)} collective-permute-done((f32[32,128]{1,0:T(8,128)S(1)}, f32[32,128]{1,0:T(8,128)}, u32[]{:S(2)}, u32[]{:S(2)}) %collective-permute-start.3) | collective-permute-done | bytes 16416 | tf_op jit(solution)/shard_map/ppermute | solution.py:187
  27.2 1.2 copy-done.1
  30.1 3.2 %experts.1 = (bf16[32,128]{1,0:T(8,128)(2,1)S(1)}, bf16[32,128]{1,0:T(8,128)(2,1)}, bf16[32,128]{1,0:T(8,128)(2,1)}, bf16[32,128]{1,0:T(8,128)(2,1)}, bf16[128,8...) custom-call(s32[1]{0:T(128)} %bitcast.1.me, ...), custom_call_target="tpu_custom_call" | custom-call | tf_op jit(solution)/shard_map/experts/pallas_call | solution.py:216
  38.6 1.9 %collective-permute-start.8 = (bf16[32,128]{1,0:T(8,128)(2,1)}, bf16[32,128]{1,0:T(8,128)(2,1)}, u32[]{:S(2)}, u32[]{:S(2)}) collective-permute-start(bf16[32,128]{1,0:T(8,128)(2,1)} %get-tuple-element.30), channel_id=1, source_target_pairs={{0,3},{1,2},{2,1},{3,0},{4,7},{5,6},{6,5},{7,4},{8,11},{9,10},{10,... | collective-permute-start | bytes 24584 | tf_op jit(solution)/shard_map/ppermute | solution.py:187
  41.5 1.9 %collective-permute-done.8.refs_3_ = bf16[32,128]{1,0:T(8,128)(2,1)} collective-permute-done((bf16[32,128]{1,0:T(8,128)(2,1)}, bf16[32,128]{1,0:T(8,128)(2,1)}, u32[]{:S(2)}, u32[]{:S(2)}) %collective-permute-start.8) | collective-permute-done | bytes 8224 | tf_op jit(solution)/shard_map/ppermute | solution.py:187
  46.1 2.0 %router_terms.1 = (f32[16,6144]{1,0:T(8,128)S(1)}, f32[32,6144]{1,0:T(8,128)S(1)}) custom-call(s32[1]{0:T(128)} %bitcast.at, bf16[32,128]{1,0:T(8,128)(2,1)S(1)} %copy-done.29, bf16[32,128]{1,0:T(8,128)(2,1)} %collective-permute-done.6.refs_1_, bf16[32,128]{1,0:T(8,128)(2,1)} %collective-permute-done.7.refs_2_, ...), custom_call_target="tpu_custom_call" | custom-call | tf_op jit(solution)/shard_map/router_terms/pallas_call | solution.py:301
  49.1 1.4 %collective-permute-done.12 = f32[16,3072]{1,0:T(8,128)S(1)} collective-permute-done((f32[16,3072]{1,0:T(8,128)S(1)}, f32[16,3072]{1,0:T(8,128)S(1)}, u32[]{:S(2)}, u32[]{:S(2)}) %collective-permute-start.12) | collective-permute-done | bytes 196640 | tf_op jit(solution)/shard_map/ppermute | solution.py:190
  51.6 3.9 %collective-permute-done.13 = bf16[16,3072]{1,0:T(8,128)(2,1)S(1)} collective-permute-done((bf16[16,3072]{1,0:T(8,128)(2,1)S(1)}, bf16[16,3072]{1,0:T(8,128)(2,1)S(1)}, u32[]{:S(2)}, u32[]{:S(2)}) %collective-permute-start.13) | collective-permute-done | bytes 98336 | tf_op jit(solution)/shard_map/ppermute | solution.py:187
  57.1 4.0 %collective-permute-done.14 = bf16[16,3072]{1,0:T(8,128)(2,1)} collective-permute-done((bf16[16,3072]{1,0:T(8,128)(2,1)}, bf16[16,3072]{1,0:T(8,128)(2,1)}, u32[]{:S(2)}, u32[]{:S(2)}) %collective-permute-start.14) | collective-permute-done | bytes 98336 | tf_op jit(solution)/shard_map/ppermute | solution.py:187
  64.9 4.4 %weight_terms.3 = bf16[4,240,768]{2,1,0:T(8,128)(2,1)} custom-call(s32[2]{0:T(128)S(1)} %pad_add_fusion.1.at, bf16[144,80]{1,0:T(8,128)(2,1)S(1)} %copy-done.16, bf16[144,80]{1,0:T(8,128)(2,1)S(1)} %copy-done.19, bf16[128,80]{1,0:T(8,128)(2,1)S(1)} %copy-done.22, bf16[144,6144]{1,0:T(8,128)(2,1)S(1)} %reshape.32.inputs, bf16[32,6144]{1,0:T(8,128)(2,1)S(1)} %copy-done.2, ...), custom_call_target="tpu_custom_call" | custom-call | tf_op jit(solution)/shard_map/weight_terms/pallas_call | solution.py:243
  69.4 2.7 %collective-permute-start.16 = (bf16[16,3072]{1,0:T(8,128)(2,1)S(1)}, bf16[16,3072]{1,0:T(8,128)(2,1)S(1)}, u32[]{:S(2)}, u32[]{:S(2)}) collective-permute-start(bf16[16,3072]{1,0:T(8,128)(2,1)S(1)} %add_convert_fusion), channel_id=1, source_target_pairs={{0,16},{4,20},{8,24},{12,28},{16,0},{20,4},{24,8},{28,12},{1,17},{... | collective-permute-start | bytes 294920 | tf_op jit(solution)/shard_map/ppermute | solution.py:193
  72.0 4.0 %row_terms.1 = (bf16[32,6144]{1,0:T(8,128)(2,1)S(1)}, bf16[32,6144]{1,0:T(8,128)(2,1)}, bf16[32,6144]{1,0:T(8,128)(2,1)}, bf16[32,6144]{1,0:T(8,128)(2,1)}) custom-call(bf16[128,80]{1,0:T(8,128)(2,1)S(1)} %copy-done.25, bf16[128,80]{1,0:T(8,128)(2,1)S(1)} %copy-done.27, bf16[80,6144]{1,0:T(8,128)(2,1)S(1)} %copy-done, bf16[80,6144]{1,0:T(8,128)(2,1)S(1)} %reshape.34.up), custom_call_target="tpu_custom_call" | custom-call | tf_op jit(solution)/shard_map/row_terms/pallas_call | solution.py:266
  77.8 1.5 %collective-permute-start.10 = (bf16[32,6144]{1,0:T(8,128)(2,1)}, bf16[32,6144]{1,0:T(8,128)(2,1)}, u32[]{:S(2)}, u32[]{:S(2)}) collective-permute-start(bf16[32,6144]{1,0:T(8,128)(2,1)} %get-tuple-element.36), channel_id=1, source_target_pairs={{0,2},{1,3},{2,0},{3,1},{4,6},{5,7},{6,4},{7,5},{8,10},{9,11},{10,... | collective-permute-start | bytes 1179656 | tf_op jit(solution)/shard_map/ppermute | solution.py:187
  83.4 4.6 %weight_terms.2.mine = f32[4,240,768]{2,1,0:T(8,128)} custom-call(s32[2]{0:T(128)S(1)} %pad_add_fusion.at, bf16[144,80]{1,0:T(8,128)(2,1)S(1)} %copy-done.17, bf16[144,80]{1,0:T(8,128)(2,1)S(1)} %copy-done.20, bf16[128,80]{1,0:T(8,128)(2,1)S(1)} %copy-done.23, bf16[144,6144]{1,0:T(8,128)(2,1)S(1)} %reshape.32.inputs, bf16[32,6144]{1,0:T(8,128)(2,1)S(1)} %copy-done.2, ...), custom_call_target="tpu_custom_call" | custom-call | tf_op jit(solution)/shard_map/weight_terms/pallas_call | solution.py:243
  89.7 7.7 %collective-permute-done.10.refs_3_ = bf16[32,6144]{1,0:T(8,128)(2,1)} collective-permute-done((bf16[32,6144]{1,0:T(8,128)(2,1)}, bf16[32,6144]{1,0:T(8,128)(2,1)}, u32[]{:S(2)}, u32[]{:S(2)}) %collective-permute-start.10) | collective-permute-done | bytes 393248 | tf_op jit(solution)/shard_map/ppermute | solution.py:187
  98.5 2.1 %grad_normed.1 = bf16[32,6144]{1,0:T(8,128)(2,1)} custom-call(f32[32,6144]{1,0:T(8,128)S(1)} %copy-done.8, bf16[32,6144]{1,0:T(8,128)(2,1)S(1)} %copy-done.10, bf16[32,6144]{1,0:T(8,128)(2,1)S(1)} %copy-done.12, bf16[32,6144]{1,0:T(8,128)(2,1)} %collective-permute-done.10.refs_3_, bf16[32,6144]{1,0:T(8,128)(2,1)} %collective-permute-done.11.refs_4_), custom_call_target="tpu_custom_call" | custom-call | tf_op jit(solution)/shard_map/grad_normed/pallas_call | solution.py:329
  100.6 2.9 %core_sum.1 = (f32[240,768]{1,0:T(8,128)S(1)}, bf16[240,768]{1,0:T(8,128)(2,1)S(1)}, bf16[240,768]{1,0:T(8,128)(2,1)S(1)}, bf16[240,768]{1,0:T(8,128)(2,1)S(1)}) custom-call(f32[4,240,768]{2,1,0:T(8,128)} %weight_terms.2.mine, bf16[4,240,768]{2,1,0:T(8,128)(2,1)} %collective-permute-done.18.theirs), custom_call_target="tpu_custom_call" | custom-call | tf_op jit(solution)/shard_map/core_sum/pallas_call | solution.py:285
  103.5 1.6 %collective-permute-start.19 = (bf16[240,768]{1,0:T(8,128)(2,1)S(1)}, bf16[240,768]{1,0:T(8,128)(2,1)S(1)}, u32[]{:S(2)}, u32[]{:S(2)}) collective-permute-start(bf16[240,768]{1,0:T(8,128)(2,1)S(1)} %get-tuple-element.43), channel_id=1, source_target_pairs={{0,8},{4,12},{8,0},{12,4},{16,24},{20,28},{24,16},{28,20},{1,9},{5... | collective-permute-start | bytes 1105928 | tf_op jit(solution)/shard_map/ppermute | solution.py:193
  105.5 1.6 %collective-permute-start.21 = (bf16[240,768]{1,0:T(8,128)(2,1)S(1)}, bf16[240,768]{1,0:T(8,128)(2,1)S(1)}, u32[]{:S(2)}, u32[]{:S(2)}) collective-permute-start(bf16[240,768]{1,0:T(8,128)(2,1)S(1)} %get-tuple-element.45), channel_id=1, source_target_pairs={{0,24},{4,28},{8,16},{12,20},{16,8},{20,12},{24,0},{28,4},{1,25},{... | collective-permute-start | bytes 1105928 | tf_op jit(solution)/shard_map/ppermute | solution.py:193
  107.1 2.0 %fusion = f32[6144,16]{0,1:T(8,128)} fusion(f32[16,3072]{1,0:T(8,128)} %collective-permute-done.17, f32[16,3072]{1,0:T(8,128)} %convert_add_fusion, pred[]{:T(512)S(6)} %eq.3), kind=kLoop, calls=%fused_computation.1 | loop fusion | flops 294912 | bytes 786433 | tf_op jit(solution)/shard_map/transpose | solution.py:327
  109.1 9.7 %collective-permute-done.19.refs_1_ = bf16[240,768]{1,0:T(8,128)(2,1)S(1)} collective-permute-done((bf16[240,768]{1,0:T(8,128)(2,1)S(1)}, bf16[240,768]{1,0:T(8,128)(2,1)S(1)}, u32[]{:S(2)}, u32[]{:S(2)}) %collective-permute-start.19) | collective-permute-done | bytes 368672 | tf_op jit(solution)/shard_map/ppermute | solution.py:193
  118.7 11.6 %collective-permute-done.20.refs_2_ = bf16[240,768]{1,0:T(8,128)(2,1)S(1)} collective-permute-done((bf16[240,768]{1,0:T(8,128)(2,1)S(1)}, bf16[240,768]{1,0:T(8,128)(2,1)S(1)}, u32[]{:S(2)}, u32[]{:S(2)}) %collective-permute-start.20) | collective-permute-done | bytes 368672 | tf_op jit(solution)/shard_map/ppermute | solution.py:193
  130.3 7.8 %collective-permute-done.21.refs_3_ = bf16[240,768]{1,0:T(8,128)(2,1)S(1)} collective-permute-done((bf16[240,768]{1,0:T(8,128)(2,1)S(1)}, bf16[240,768]{1,0:T(8,128)(2,1)S(1)}, u32[]{:S(2)}, u32[]{:S(2)}) %collective-permute-start.21) | collective-permute-done | bytes 368672 | tf_op jit(solution)/shard_map/ppermute | solution.py:193
  (100 shorter events, 34.1 us)
Async XLA Ops:
  1.4 1.0 copy-start.3
  3.7 14.3 %collective-permute-start.5 = (f32[32,128]{1,0:T(8,128)S(1)}, f32[32,128]{1,0:T(8,128)}, u32[]{:S(2)}, u32[]{:S(2)}) collective-permute-start(f32[32,128]{1,0:T(8,128)S(1)} %route.1.refs_4_), channel_id=1, source_target_pairs={{0,3},{1,2},{2,1},{3,0},{4,7},{5,6},{6,5},{7,4},{8,11},{9,10},{10,... | collective-permute-start | bytes 49160 | tf_op jit(solution)/shard_map/ppermute | solution.py:187
  6.2 17.2 %collective-permute-start.4 = (f32[32,128]{1,0:T(8,128)S(1)}, f32[32,128]{1,0:T(8,128)}, u32[]{:S(2)}, u32[]{:S(2)}) collective-permute-start(f32[32,128]{1,0:T(8,128)S(1)} %route.1.refs_4_), channel_id=1, source_target_pairs={{0,2},{1,3},{2,0},{3,1},{4,6},{5,7},{6,4},{7,5},{8,10},{9,11},{10,... | collective-permute-start | bytes 49160 | tf_op jit(solution)/shard_map/ppermute | solution.py:187
  6.8 20.4 %collective-permute-start.2 = (bf16[32,6144]{1,0:T(8,128)(2,1)}, bf16[32,6144]{1,0:T(8,128)(2,1)S(1)}, u32[]{:S(2)}, u32[]{:S(2)}) collective-permute-start(bf16[32,6144]{1,0:T(8,128)(2,1)} %refs_0_.5), channel_id=1, source_target_pairs={{0,3},{1,2},{2,1},{3,0},{4,7},{5,6},{6,5},{7,4},{8,11},{9,10},{10,... | collective-permute-start | bytes 1179656 | tf_op jit(solution)/shard_map/ppermute | solution.py:187
  8.2 18.9 %collective-permute-start.1 = (bf16[32,6144]{1,0:T(8,128)(2,1)}, bf16[32,6144]{1,0:T(8,128)(2,1)}, u32[]{:S(2)}, u32[]{:S(2)}) collective-permute-start(bf16[32,6144]{1,0:T(8,128)(2,1)} %refs_0_.5), channel_id=1, source_target_pairs={{0,2},{1,3},{2,0},{3,1},{4,6},{5,7},{6,4},{7,5},{8,10},{9,11},{10,... | collective-permute-start | bytes 1179656 | tf_op jit(solution)/shard_map/ppermute | solution.py:187
  8.7 18.4 %collective-permute-start = (bf16[32,6144]{1,0:T(8,128)(2,1)}, bf16[32,6144]{1,0:T(8,128)(2,1)}, u32[]{:S(2)}, u32[]{:S(2)}) collective-permute-start(bf16[32,6144]{1,0:T(8,128)(2,1)} %refs_0_.5), channel_id=1, source_target_pairs={{0,1},{1,0},{2,3},{3,2},{4,5},{5,4},{6,7},{7,6},{8,9},{9,8},{10,11... | collective-permute-start | bytes 1179656 | tf_op jit(solution)/shard_map/ppermute | solution.py:187
  18.1 9.1 %copy-start.2 = (bf16[32,6144]{1,0:T(8,128)(2,1)S(1)}, bf16[32,6144]{1,0:T(8,128)(2,1)}, u32[]{:S(2)}) copy-start(bf16[32,6144]{1,0:T(8,128)(2,1)} %refs_0_.5) | copy-start | bytes 1179652
  18.1 9.1 %collective-permute-start.3 = (f32[32,128]{1,0:T(8,128)S(1)}, f32[32,128]{1,0:T(8,128)}, u32[]{:S(2)}, u32[]{:S(2)}) collective-permute-start(f32[32,128]{1,0:T(8,128)S(1)} %route.1.refs_4_), channel_id=1, source_target_pairs={{0,1},{1,0},{2,3},{3,2},{4,5},{5,4},{6,7},{7,6},{8,9},{9,8},{10,11... | collective-permute-start | bytes 49160 | tf_op jit(solution)/shard_map/ppermute | solution.py:187
  27.2 1.2 copy-start.1
  37.0 4.0 %collective-permute-start.6 = (bf16[32,128]{1,0:T(8,128)(2,1)}, bf16[32,128]{1,0:T(8,128)(2,1)}, u32[]{:S(2)}, u32[]{:S(2)}) collective-permute-start(bf16[32,128]{1,0:T(8,128)(2,1)} %get-tuple-element.28), channel_id=1, source_target_pairs={{0,1},{1,0},{2,3},{3,2},{4,5},{5,4},{6,7},{7,6},{8,9},{9,8},{10,11... | collective-permute-start | bytes 24584 | tf_op jit(solution)/shard_map/ppermute | solution.py:187
  37.5 4.0 %collective-permute-start.7 = (bf16[32,128]{1,0:T(8,128)(2,1)}, bf16[32,128]{1,0:T(8,128)(2,1)}, u32[]{:S(2)}, u32[]{:S(2)}) collective-permute-start(bf16[32,128]{1,0:T(8,128)(2,1)} %get-tuple-element.29), channel_id=1, source_target_pairs={{0,2},{1,3},{2,0},{3,1},{4,6},{5,7},{6,4},{7,5},{8,10},{9,11},{10,... | collective-permute-start | bytes 24584 | tf_op jit(solution)/shard_map/ppermute | solution.py:187
  38.6 4.9 %collective-permute-start.8 = (bf16[32,128]{1,0:T(8,128)(2,1)}, bf16[32,128]{1,0:T(8,128)(2,1)}, u32[]{:S(2)}, u32[]{:S(2)}) collective-permute-start(bf16[32,128]{1,0:T(8,128)(2,1)} %get-tuple-element.30), channel_id=1, source_target_pairs={{0,3},{1,2},{2,1},{3,0},{4,7},{5,6},{6,5},{7,4},{8,11},{9,10},{10,... | collective-permute-start | bytes 24584 | tf_op jit(solution)/shard_map/ppermute | solution.py:187
  43.5 1.0 copy-start.4
  49.0 1.5 %collective-permute-start.12 = (f32[16,3072]{1,0:T(8,128)S(1)}, f32[16,3072]{1,0:T(8,128)S(1)}, u32[]{:S(2)}, u32[]{:S(2)}) collective-permute-start(f32[16,3072]{1,0:T(8,128)S(1)} %slice.7), channel_id=1, source_target_pairs={{0,4},{4,0},{8,12},{12,8},{16,20},{20,16},{24,28},{28,24},{1,5},{5... | collective-permute-start | bytes 589832 | tf_op jit(solution)/shard_map/ppermute | solution.py:190
  50.6 4.9 %collective-permute-start.13 = (bf16[16,3072]{1,0:T(8,128)(2,1)S(1)}, bf16[16,3072]{1,0:T(8,128)(2,1)S(1)}, u32[]{:S(2)}, u32[]{:S(2)}) collective-permute-start(bf16[16,3072]{1,0:T(8,128)(2,1)S(1)} %add_convert_fusion.3), channel_id=1, source_target_pairs={{0,1},{1,0},{2,3},{3,2},{4,5},{5,4},{6,7},{7,6},{8,9},{9,8},{10,11... | collective-permute-start | bytes 294920 | tf_op jit(solution)/shard_map/ppermute | solution.py:187
  56.1 4.9 %collective-permute-start.14 = (bf16[16,3072]{1,0:T(8,128)(2,1)}, bf16[16,3072]{1,0:T(8,128)(2,1)}, u32[]{:S(2)}, u32[]{:S(2)}) collective-permute-start(bf16[16,3072]{1,0:T(8,128)(2,1)} %add_convert_fusion.2), channel_id=1, source_target_pairs={{0,2},{1,3},{2,0},{3,1},{4,6},{5,7},{6,4},{7,5},{8,10},{9,11},{10,... | collective-permute-start | bytes 294920 | tf_op jit(solution)/shard_map/ppermute | solution.py:187
  62.0 7.3 %collective-permute-start.15 = (bf16[16,3072]{1,0:T(8,128)(2,1)S(1)}, bf16[16,3072]{1,0:T(8,128)(2,1)S(1)}, u32[]{:S(2)}, u32[]{:S(2)}) collective-permute-start(bf16[16,3072]{1,0:T(8,128)(2,1)S(1)} %add_convert_fusion.1), channel_id=1, source_target_pairs={{0,8},{4,12},{8,0},{12,4},{16,24},{20,28},{24,16},{28,20},{1,9},{5... | collective-permute-start | bytes 294920 | tf_op jit(solution)/shard_map/ppermute | solution.py:193
  64.9 7.1 %copy-start = (bf16[80,6144]{1,0:T(8,128)(2,1)S(1)}, bf16[80,6144]{1,0:T(8,128)(2,1)}, u32[]{:S(2)}) copy-start(bf16[80,6144]{1,0:T(8,128)(2,1)} %reshape.33.gate) | copy-start | bytes 2949124
  64.9 7.1 %copy-start.25 = (bf16[128,80]{1,0:T(8,128)(2,1)S(1)}, bf16[128,80]{1,0:T(8,128)(2,1)}, u32[]{:S(2)}) copy-start(bf16[128,80]{1,0:T(8,128)(2,1)} %copy-done.24) | copy-start | bytes 61444
  64.9 7.1 %copy-start.27 = (bf16[128,80]{1,0:T(8,128)(2,1)S(1)}, bf16[128,80]{1,0:T(8,128)(2,1)}, u32[]{:S(2)}) copy-start(bf16[128,80]{1,0:T(8,128)(2,1)} %copy-done.26) | copy-start | bytes 61444
  69.3 31.2 %collective-permute-start.18 = (bf16[4,240,768]{2,1,0:T(8,128)(2,1)}, bf16[4,240,768]{2,1,0:T(8,128)(2,1)}, u32[]{:S(2)}, u32[]{:S(2)}) collective-permute-start(bf16[4,240,768]{2,1,0:T(8,128)(2,1)} %weight_terms.3), channel_id=1, source_target_pairs={{0,4},{4,0},{8,12},{12,8},{16,20},{20,16},{24,28},{28,24},{1,5},{5... | collective-permute-start | bytes 4423688 | tf_op jit(solution)/shard_map/ppermute | solution.py:190
  69.4 11.0 %collective-permute-start.16 = (bf16[16,3072]{1,0:T(8,128)(2,1)S(1)}, bf16[16,3072]{1,0:T(8,128)(2,1)S(1)}, u32[]{:S(2)}, u32[]{:S(2)}) collective-permute-start(bf16[16,3072]{1,0:T(8,128)(2,1)S(1)} %add_convert_fusion), channel_id=1, source_target_pairs={{0,16},{4,20},{8,24},{12,28},{16,0},{20,4},{24,8},{28,12},{1,17},{... | collective-permute-start | bytes 294920 | tf_op jit(solution)/shard_map/ppermute | solution.py:193
  76.8 12.2 %collective-permute-start.9 = (bf16[32,6144]{1,0:T(8,128)(2,1)}, bf16[32,6144]{1,0:T(8,128)(2,1)S(1)}, u32[]{:S(2)}, u32[]{:S(2)}) collective-permute-start(bf16[32,6144]{1,0:T(8,128)(2,1)} %get-tuple-element.35), channel_id=1, source_target_pairs={{0,1},{1,0},{2,3},{3,2},{4,5},{5,4},{6,7},{7,6},{8,9},{9,8},{10,11... | collective-permute-start | bytes 1179656 | tf_op jit(solution)/shard_map/ppermute | solution.py:187
  77.8 19.7 %collective-permute-start.10 = (bf16[32,6144]{1,0:T(8,128)(2,1)}, bf16[32,6144]{1,0:T(8,128)(2,1)}, u32[]{:S(2)}, u32[]{:S(2)}) collective-permute-start(bf16[32,6144]{1,0:T(8,128)(2,1)} %get-tuple-element.36), channel_id=1, source_target_pairs={{0,2},{1,3},{2,0},{3,1},{4,6},{5,7},{6,4},{7,5},{8,10},{9,11},{10,... | collective-permute-start | bytes 1179656 | tf_op jit(solution)/shard_map/ppermute | solution.py:187
  79.3 18.2 %collective-permute-start.11 = (bf16[32,6144]{1,0:T(8,128)(2,1)}, bf16[32,6144]{1,0:T(8,128)(2,1)}, u32[]{:S(2)}, u32[]{:S(2)}) collective-permute-start(bf16[32,6144]{1,0:T(8,128)(2,1)} %get-tuple-element.37), channel_id=1, source_target_pairs={{0,3},{1,2},{2,1},{3,0},{4,7},{5,6},{6,5},{7,4},{8,11},{9,10},{10,... | collective-permute-start | bytes 1179656 | tf_op jit(solution)/shard_map/ppermute | solution.py:187
  81.0 26.1 %collective-permute-start.17 = (f32[16,3072]{1,0:T(8,128)}, f32[16,3072]{1,0:T(8,128)}, u32[]{:S(2)}, u32[]{:S(2)}) collective-permute-start(f32[16,3072]{1,0:T(8,128)} %convert_add_fusion), channel_id=1, source_target_pairs={{0,4},{4,0},{8,12},{12,8},{16,20},{20,16},{24,28},{28,24},{1,5},{5... | collective-permute-start | bytes 589832 | tf_op jit(solution)/shard_map/ppermute | solution.py:190
  83.4 14.1 %copy-start.8 = (f32[32,6144]{1,0:T(8,128)S(1)}, f32[32,6144]{1,0:T(8,128)}, u32[]{:S(2)}) copy-start(f32[32,6144]{1,0:T(8,128)} %copy-done.7) | copy-start | bytes 2359300
  83.4 14.1 %copy-start.10 = (bf16[32,6144]{1,0:T(8,128)(2,1)S(1)}, bf16[32,6144]{1,0:T(8,128)(2,1)}, u32[]{:S(2)}) copy-start(bf16[32,6144]{1,0:T(8,128)(2,1)} %copy-done.9) | copy-start | bytes 1179652
  97.5 1.0 copy-start.12
  103.5 15.2 %collective-permute-start.19 = (bf16[240,768]{1,0:T(8,128)(2,1)S(1)}, bf16[240,768]{1,0:T(8,128)(2,1)S(1)}, u32[]{:S(2)}, u32[]{:S(2)}) collective-permute-start(bf16[240,768]{1,0:T(8,128)(2,1)S(1)} %get-tuple-element.43), channel_id=1, source_target_pairs={{0,8},{4,12},{8,0},{12,4},{16,24},{20,28},{24,16},{28,20},{1,9},{5... | collective-permute-start | bytes 1105928 | tf_op jit(solution)/shard_map/ppermute | solution.py:193
  105.1 25.2 %collective-permute-start.20 = (bf16[240,768]{1,0:T(8,128)(2,1)S(1)}, bf16[240,768]{1,0:T(8,128)(2,1)S(1)}, u32[]{:S(2)}, u32[]{:S(2)}) collective-permute-start(bf16[240,768]{1,0:T(8,128)(2,1)S(1)} %get-tuple-element.44), channel_id=1, source_target_pairs={{0,16},{4,20},{8,24},{12,28},{16,0},{20,4},{24,8},{28,12},{1,17},{... | collective-permute-start | bytes 1105928 | tf_op jit(solution)/shard_map/ppermute | solution.py:193
  105.5 32.7 %collective-permute-start.21 = (bf16[240,768]{1,0:T(8,128)(2,1)S(1)}, bf16[240,768]{1,0:T(8,128)(2,1)S(1)}, u32[]{:S(2)}, u32[]{:S(2)}) collective-permute-start(bf16[240,768]{1,0:T(8,128)(2,1)S(1)} %get-tuple-element.45), channel_id=1, source_target_pairs={{0,24},{4,28},{8,16},{12,20},{16,8},{20,12},{24,0},{28,4},{1,25},{... | collective-permute-start | bytes 1105928 | tf_op jit(solution)/shard_map/ppermute | solution.py:193
  (20 other events, 15.0 us)

commit v2 on v0

v2 whole, which is shorter than its diff:
```python
import functools

import jax
import jax.numpy as jnp
from jax import lax
from jax.experimental import pallas as pl
from jax.experimental.pallas import tpu as pltpu
from jax.sharding import PartitionSpec as P

F32 = jnp.float32
BF16 = jnp.bfloat16
LANES = 128
TILE = 16
EARLY = 0
VMEM_BYTES = 16 * 2**20
HIGHEST = lax.Precision.HIGHEST


def dot(left, right, contract, precision=None):
    return lax.dot_general(
        left,
        right,
        ((contract[:1], contract[1:]), ((), ())),
        precision=precision,
        preferred_element_type=F32,
    )


def iota(shape, dim):
    return lax.broadcasted_iota(jnp.int32, shape, dim)


def split_high_low(value):
    high = value.astype(BF16)
    return high, (value - high.astype(F32)).astype(BF16)


def route_kernel(experts, ids, normed_hbm, router_hbm, upstream_hbm, packed, normed, router, upstream, sems):
    tokens, width = normed.shape
    copies = [
        pltpu.make_async_copy(source, target, sems.at[k])
        for k, (source, target) in enumerate(
            ((normed_hbm, normed), (router_hbm, router), (upstream_hbm, upstream))
        )
    ]
    for copy in copies:
        copy.start()
    expert = iota((experts, tokens), 0)
    named_t = expert < 0
    for k in range(ids.shape[0]):
        named_t = named_t | (ids[k : k + 1, :] == expert)
    unit = (iota((tokens, tokens), 0) == iota((tokens, tokens), 1)).astype(F32).astype(BF16)
    named_f = dot(unit, named_t.astype(F32).astype(BF16), (1, 1))
    named = named_f > 0.5
    earlier = (iota((tokens, tokens), 1) < iota((tokens, tokens), 0)).astype(F32).astype(BF16)
    slot = dot(earlier, named_f.astype(BF16), (1, 0))
    code = jnp.where(named, slot + 1.0, 0.0)
    copies[0].wait()
    copies[1].wait()
    logits = dot(normed[...], router[...], (1, 1))
    largest = jnp.max(jnp.where(named, logits, -jnp.inf), axis=1, keepdims=True)
    weight = jnp.where(named, jnp.exp(jnp.where(named, logits - largest, 0.0)), 0.0)
    weight = weight / jnp.sum(weight, axis=1, keepdims=True)
    high = weight.astype(BF16).astype(F32)
    middle = (weight - high).astype(BF16).astype(F32)
    low = weight - high - middle
    rest = jnp.zeros((tokens, LANES - 4 * experts), F32)
    packed[:, width:] = jnp.concatenate([high, middle, low, code, rest], axis=1).astype(BF16)
    copies[2].wait()
    packed[:, :width] = upstream[...]


def prepare_kernel(n_early, blocks, *refs):
    sources, refs = refs[:4], refs[4:]
    scratch, sems, refs = refs[-5:-1], refs[-1], refs[:-5]
    inputs, gate_rows, up_rows, down_rows, pre_gate, pre_up, *early = refs
    step = inputs.shape[1] // blocks
    copies = []
    for j in range(blocks):
        lanes = pl.ds(j * step, step)
        for k in range(4):
            copy = pltpu.make_async_copy(sources[k].at[:, :, lanes], scratch[k].at[:, :, lanes], sems.at[4 * j + k])
            copy.start()
            copies.append(copy)
    pre_gate[...] = jnp.zeros_like(pre_gate)
    pre_up[...] = jnp.zeros_like(pre_up)
    for j in range(blocks):
        lanes = slice(j * step, (j + 1) * step)
        for k, target in enumerate((inputs, gate_rows, up_rows, down_rows)):
            copies[4 * j + k].wait()
            target[:, lanes] = scratch[k][:, :, lanes].reshape(target.shape[0], step)
        pre_gate[...] += dot(inputs[:, lanes], gate_rows[:, lanes], (1, 1))
        pre_up[...] += dot(inputs[:, lanes], up_rows[:, lanes], (1, 1))
        if n_early:
            early[0][j] = inputs[: early[0].shape[1], lanes]


def pick(expert_of_column, experts, groups, columns):
    lane = iota((LANES, columns), 0)
    out = lane < 0
    for g in groups:
        out = out | (lane == expert_of_column + g * experts)
    return out.astype(F32).astype(BF16)


def unit_rows(rows, hidden_all, exp_dev, first, wanted):
    row, column = iota((rows, hidden_all), 0) - first, iota((rows, hidden_all), 1)
    return wanted(row, column // exp_dev, column % exp_dev).astype(F32).astype(BF16)


def block_terms(late, tok_hidden, inputs, rows_u, start, piece):
    at = pl.ds(pl.multiple_of(start, LANES), piece)
    arrived = jnp.concatenate([u[:, at] for u in rows_u], axis=0)
    return dot(late, inputs[:, at], (1, 0)), dot(tok_hidden, arrived, (1, 0))


def expert_kernel(sizes, at, *refs):
    n_expert, exp_dev, capacity, tokens_here, n_chip, piece, n_early = sizes
    rows_u, rest = refs[:n_expert], refs[n_expert:]
    down, pre_gate, pre_up, inputs = rest[:4]
    scores = rest[4 : 4 + n_expert]
    tok_gate, tok_up, tok_hidden, slot_late, slot_early = rest[4 + n_expert : 9 + n_expert]
    me, chip, core = at[0], at[1], at[2]
    experts = exp_dev * n_expert
    tokens = tokens_here * n_expert
    hidden_all, width = down.shape
    hidden_units = hidden_all // exp_dev
    slots = exp_dev * capacity * n_expert
    packed = jnp.concatenate([u[:, width:] for u in rows_u], axis=0)
    arrived = jnp.concatenate([u[:, :width] for u in rows_u], axis=0)
    grad_hidden_raw = dot(arrived, down[...], (1, 1))

    expert_of_slot = me * exp_dev + iota((LANES, slots), 1) // (capacity * n_expert)
    weight_at = dot(packed, pick(expert_of_slot, experts, (0, 1, 2), slots), (1, 0))
    code_at = dot(packed, pick(expert_of_slot, experts, (3,), slots), (1, 0))
    column = iota((tokens, slots), 1)
    source = me ^ (iota((tokens, slots), 0) // tokens_here)
    slot_code = ((column // n_expert) % capacity + 1).astype(F32)
    chosen = (source == column % n_expert) & (jnp.abs(code_at - slot_code) < 0.5)
    place = chosen.astype(F32).astype(BF16)
    place_weight = jnp.where(chosen, weight_at, 0.0)

    grad_hidden = dot(place_weight, grad_hidden_raw, (0, 0), HIGHEST)
    same = iota((slots, hidden_all), 1) % exp_dev == iota((slots, hidden_all), 0) // (capacity * n_expert)
    v = pre_gate[...]
    logistic = jax.nn.sigmoid(v)
    activated = v * logistic
    hidden = jnp.where(same, activated * pre_up[...], 0.0).astype(BF16)
    slope = logistic * (1.0 + v * (1.0 - logistic))
    grad_gate = jnp.where(same, grad_hidden * pre_up[...] * slope, 0.0).astype(BF16)
    grad_up = jnp.where(same, grad_hidden * activated, 0.0).astype(BF16)
    score = jnp.sum(hidden.astype(F32) * grad_hidden, axis=1, keepdims=True)
    expert_of_row = me * exp_dev + iota((slots, LANES), 0) // (capacity * n_expert)
    score = jnp.where(iota((slots, LANES), 1) == expert_of_row, score, 0.0)
    picked = dot(chosen.astype(F32), score, (1, 0), HIGHEST)
    for r in range(n_expert):
        scores[r][...] = picked[r * tokens_here : (r + 1) * tokens_here]
    tok_gate[...] = dot(place, grad_gate, (1, 0)).astype(BF16)
    tok_up[...] = dot(place, grad_up, (1, 0)).astype(BF16)
    expert_of_hidden = me * exp_dev + iota((LANES, hidden_all), 1) % exp_dev
    weight_hidden = dot(packed, pick(expert_of_hidden, experts, (0, 1, 2), hidden_all), (1, 0))
    scaled_hidden = (dot(place, hidden, (1, 0)) * weight_hidden).astype(BF16)
    n_late = exp_dev - n_early

    def pick_late(first):
        return unit_rows(
            slot_late.shape[0],
            hidden_all,
            exp_dev,
            first,
            lambda i, unit, e: (i >= 0) & (e >= n_early) & (i == (e - n_early) * hidden_units + unit),
        )

    late = dot(pick_late(0), grad_gate, (1, 1)) + dot(pick_late(n_late * hidden_units), grad_up, (1, 1))
    late = late.astype(BF16)
    order = unit_rows(hidden_all, hidden_all, exp_dev, 0, lambda i, unit, e: i == e * hidden_units + unit)
    turned = dot(order, scaled_hidden, (1, 1)).astype(BF16)
    slot_late[...], tok_hidden[...] = late, turned
    fold = [unit_rows(slot_early.shape[0], hidden_all, exp_dev, f, lambda i, unit, e: i == unit) for f in (0, hidden_units)]
    early = dot(fold[0], grad_gate, (1, 1)) + dot(fold[1], grad_up, (1, 1))
    slot_early[...] = early[:, :LANES].astype(BF16)
    if len(rest) > 9 + n_expert:
        theirs = rest[9 + n_expert]
        n = late.shape[0]
        for r in range(n_chip):
            start = (2 * (chip ^ r) + 1 - core) * piece
            first, second = block_terms(late, turned, inputs, rows_u, start, piece)
            theirs[r, :n] = first.astype(BF16)
            theirs[r, n:] = second.astype(BF16)


def weight_kernel(sizes, at, *refs):
    n_expert, n_chip, piece = sizes
    rows_u, (inputs, late, tok_hidden, mine) = refs[:n_expert], refs[n_expert:]
    chip, core = at[1], at[2]
    n = late.shape[0]
    for r in range(n_chip):
        start = (2 * (chip ^ r) + core) * piece
        first, second = block_terms(late[...], tok_hidden[...], inputs, rows_u, start, piece)
        mine[r, :n] = first
        mine[r, n:] = second


def add_kernel(n_early, mine, theirs, own, other, *refs):
    n_chip, m, _ = mine.shape
    outs = refs[-n_chip:]
    for r in range(n_chip):
        outs[r][:m] = (mine[r] + theirs[r].astype(F32)).astype(outs[r].dtype)
        if r and n_early:
            for k, lanes in enumerate(early_lanes(own.shape[0])):
                half = own if k < own.shape[0] // TILE else other
                block = k % (own.shape[0] // TILE)
                outs[r][m:, lanes] = half[block * TILE : (block + 1) * TILE]


def early_lanes(rows):
    return [slice(k * LANES, (k + 1) * LANES) for k in range(2 * rows // TILE)]


def row_kernel(n_expert, blocks, at, tok_gate, tok_up, gate, up, behind, out):
    del behind
    size = tok_gate.shape[0] // n_expert
    step = gate.shape[1] // blocks
    for j in range(blocks):
        lanes = slice(j * step, (j + 1) * step)
        total = dot(tok_gate[...], gate[:, lanes], (1, 0)) + dot(tok_up[...], up[:, lanes], (1, 0))
        for r in range(n_expert):
            out[at[0] ^ r, :, lanes] = total[r * size : (r + 1) * size].astype(out.dtype)


def sum_kernel(sizes, at, *refs):
    n_chip, exp_dev, hidden_units, slots_each, n_early = sizes
    pieces, own, other, rows = refs[:n_chip], refs[n_chip], refs[n_chip + 1], refs[n_chip + 2]
    outs = refs[-3:]
    chip, core = at[1], at[2]
    m = pieces[0].shape[0]
    n = m - exp_dev * hidden_units
    total = pieces[0][...]
    for piece in pieces[1:]:
        total = total + piece[:m].astype(F32)
    if n_early:
        count = n_early * hidden_units
        held, depth = own.shape[0], rows.shape[1]
        row, column = iota((2 * count, held), 0), iota((2 * count, held), 1)
        spread = (column == (row // count) * hidden_units + row % hidden_units).astype(F32).astype(BF16)
        same = (iota((2 * count, LANES), 0) % count) // hidden_units == iota((2 * count, LANES), 1) // slots_each
        early = jnp.zeros((2 * count, rows.shape[2]), F32)
        for r in range(n_chip):
            for c in range(2):
                if r:
                    half = early_lanes(held)[c * held // TILE : (c + 1) * held // TILE]
                    narrow = jnp.concatenate([pieces[r][m:, lanes] for lanes in half], axis=0)
                else:
                    narrow = (own, other)[c][...]
                wide = jnp.where(same, dot(spread, narrow, (1, 0)), 0.0).astype(BF16)
                early = early + dot(wide[:, :depth], rows[2 * (chip ^ r) + (core ^ c)], (1, 0))
    for k in range(2):
        for e in range(exp_dev):
            if e < n_early:
                first = (k * n_early + e) * hidden_units
                outs[k][:, e, :] = early[first : first + hidden_units]
            else:
                first = (k * (exp_dev - n_early) + e - n_early) * hidden_units
                outs[k][:, e, :] = total[first : first + hidden_units]
    for e in range(exp_dev):
        outs[2][:, e, :] = total[n + e * hidden_units : n + (e + 1) * hidden_units]


def router_kernel(experts, n_expert, at, *refs):
    scores, (packed, normed, router, other, own, through) = refs[:n_expert], refs[n_expert:]
    picked = scores[0][...]
    for s in scores[1:]:
        picked = picked + s[...]
    picked = picked[:, :experts]
    width = normed.shape[1]
    half = width // 2
    tail = packed[:, width:].astype(F32)
    weight = tail[:, :experts] + tail[:, experts : 2 * experts] + tail[:, 2 * experts : 3 * experts]
    code = tail[:, 3 * experts : 4 * experts]
    grad = jnp.where(code > 0.5, picked - weight * jnp.sum(picked, axis=1, keepdims=True), 0.0)
    high, low = split_high_low(grad)
    core = at[2]
    for out, part in ((other, 1 - core), (own, core)):
        values = normed[:, pl.ds(pl.multiple_of(part * half, LANES), half)]
        out[...] = dot(high, values, (0, 0)) + dot(low, values, (0, 0))
    through[...] = dot(high, router[...], (1, 0)) + dot(low, router[...], (1, 0))


def final_kernel(through, pieces, out):
    total = through[...]
    for r in range(pieces.shape[0]):
        total = total + pieces[r].astype(F32)
    out[...] = total.astype(out.dtype)


def on_device(normed, upstream, expert_ids, router_weight, gate_weight, up_weight, down_weight, saved_inputs):
    n_expert = lax.axis_size("expert")
    n_dp = lax.axis_size("dp")
    n_chip = n_dp // 2
    me = lax.axis_index("expert")
    dp = lax.axis_index("dp")
    core = dp & 1
    chip = dp >> 1
    exp_dev, hidden_units, width = gate_weight.shape
    capacity = saved_inputs.shape[3]
    experts = exp_dev * n_expert
    tokens_here = normed.shape[0]
    tokens = tokens_here * n_expert
    slots = exp_dev * capacity * n_expert
    hidden_all = exp_dev * hidden_units
    piece = width // n_dp
    half = width // 2
    even = piece % LANES == 0
    slots_each = capacity * n_expert
    narrow = -(-2 * hidden_units // TILE) * TILE
    n_early = EARLY * exp_dev // 4
    early_rows = -(-n_early * slots_each // TILE) * TILE
    if not even or early_rows > min(LANES, slots) or 2 * narrow // TILE * LANES > piece:
        n_early = 0
    late_rows = -(-2 * (exp_dev - n_early) * hidden_units // TILE) * TILE
    sent_rows = late_rows + hidden_all
    shape = jax.ShapeDtypeStruct

    def over_expert(value, k):
        return lax.ppermute(value, "expert", [(i, i ^ k) for i in range(n_expert)])

    def over_core(value):
        return lax.ppermute(value, "dp", [(i, i ^ 1) for i in range(n_dp)])

    def over_chip(value, k):
        return lax.ppermute(value, "dp", [(i, i ^ (2 * k)) for i in range(n_dp)])

    def call(kernel, name, outs, args, scalars=False, behind=0):
        specs = [pl.BlockSpec(memory_space=pltpu.VMEM)] * len(args)
        if scalars:
            specs[0] = pl.BlockSpec(memory_space=pltpu.SMEM)
        for k in range(behind):
            specs[-1 - k] = pl.BlockSpec(memory_space=pl.ANY)
        return pl.pallas_call(
            kernel,
            out_shape=outs,
            in_specs=specs,
            out_specs=[pl.BlockSpec(memory_space=pltpu.VMEM)] * len(outs),
            compiler_params=pltpu.CompilerParams(vmem_limit_bytes=VMEM_BYTES),
            cost_estimate=pl.CostEstimate(flops=0, bytes_accessed=0, transcendentals=0),
            name=name,
        )(*args)

    at = jnp.stack([me, chip, core]).astype(jnp.int32)
    router = router_weight.T
    packed = pl.pallas_call(
        functools.partial(route_kernel, experts),
        out_shape=shape((tokens_here, width + LANES), BF16),
        in_specs=[pl.BlockSpec(memory_space=pltpu.VMEM)] + [pl.BlockSpec(memory_space=pltpu.HBM)] * 3,
        out_specs=pl.BlockSpec(memory_space=pltpu.VMEM),
        scratch_shapes=[
            pltpu.VMEM((tokens_here, width), BF16),
            pltpu.VMEM((experts, width), BF16),
            pltpu.VMEM((tokens_here, width), BF16),
            pltpu.SemaphoreType.DMA((3,)),
        ],
        compiler_params=pltpu.CompilerParams(vmem_limit_bytes=VMEM_BYTES),
        cost_estimate=pl.CostEstimate(flops=0, bytes_accessed=0, transcendentals=0),
        name="route",
    )(expert_ids.T, normed, router, upstream)
    rows_u = [packed] + [over_expert(packed, k) for k in range(1, n_expert)]

    blocks = n_dp if even else 8
    sources = [jnp.transpose(saved_inputs[0], (0, 2, 1, 3)).reshape(exp_dev * capacity, n_expert, width)]
    sources += [jnp.transpose(w, (1, 0, 2)) for w in (gate_weight, up_weight, down_weight)]
    results = (
        [shape((slots, width), BF16)]
        + [shape((hidden_all, width), BF16)] * 3
        + [shape((slots, hidden_all), F32)] * 2
        + [shape((n_dp, early_rows, piece), BF16)] * bool(n_early)
    )
    inputs, gate, up, down, pre_gate, pre_up, *early_x = pl.pallas_call(
        functools.partial(prepare_kernel, n_early, blocks),
        out_shape=results,
        in_specs=[pl.BlockSpec(memory_space=pltpu.HBM)] * 4,
        out_specs=[pl.BlockSpec(memory_space=pltpu.VMEM)] * len(results),
        scratch_shapes=[pltpu.VMEM(source.shape, BF16) for source in sources]
        + [pltpu.SemaphoreType.DMA((4 * blocks,))],
        compiler_params=pltpu.CompilerParams(vmem_limit_bytes=VMEM_BYTES),
        cost_estimate=pl.CostEstimate(flops=0, bytes_accessed=0, transcendentals=0),
        name="prepare",
    )(*sources)
    if n_early:
        early_x = lax.all_to_all(early_x[0], "dp", 0, 0, tiled=True)

    outs = call(
        functools.partial(expert_kernel, (n_expert, exp_dev, capacity, tokens_here, n_chip, piece, n_early)),
        "experts",
        [shape((tokens_here, LANES), F32)] * n_expert
        + [shape((tokens, hidden_all), BF16)] * 2
        + [shape((hidden_all, tokens), BF16), shape((late_rows, slots), BF16), shape((narrow, LANES), BF16)]
        + [shape((n_chip, sent_rows, piece), BF16)] * even,
        (at, *rows_u, down, pre_gate, pre_up, inputs),
        scalars=True,
    )
    scores = outs[:n_expert]
    tok_gate, tok_up, tok_hidden, slot_late, own_narrow = outs[n_expert : n_expert + 5]
    back_scores = [scores[0]] + [over_expert(scores[k], k) for k in range(1, n_expert)]
    other_narrow = over_core(own_narrow) if n_early else own_narrow
    if even:
        from_core = over_core(outs[n_expert + 5])
        sent = shape((sent_rows + TILE * bool(n_early), piece), BF16)
        (mine,) = call(
            functools.partial(weight_kernel, (n_expert, n_chip, piece)),
            "weight_terms",
            [shape((n_chip, sent_rows, piece), F32)],
            (at, *rows_u, inputs, slot_late, tok_hidden),
            scalars=True,
        )
        chip_sums = call(
            functools.partial(add_kernel, n_early),
            "core_sum",
            [shape((sent_rows, piece), F32)] + [sent] * (n_chip - 1),
            (mine, from_core, own_narrow, other_narrow, *back_scores[1:]),
            behind=n_expert - 1,
        )
    else:
        arrived = jnp.concatenate([u[:, :width] for u in rows_u], axis=0)
        terms = [dot(slot_late, inputs, (1, 0)), dot(tok_hidden, arrived, (1, 0))]
        terms = jnp.concatenate(terms, axis=0).reshape(sent_rows, n_chip, 2, piece)
        terms = jnp.transpose(terms, (2, 1, 0, 3))
        from_core = over_core(terms[1 - core].astype(BF16))
        terms = terms[core] + from_core.astype(F32)
        chip_sums = [terms[chip ^ k].astype(BF16 if k else F32) for k in range(n_chip)]
    chip_pieces = [chip_sums[0]] + [over_chip(chip_sums[k], k) for k in range(1, n_chip)]

    always = expert_ids[0, 0] >= 0

    def sum_chips(total):
        for k in range(n_chip.bit_length() - 1):
            total = lax.reduce_precision(total, 8, 7)
            total = total + over_chip(total.astype(BF16), 1 << k).astype(F32)
        other = over_core(total)
        return jnp.where(
            core == 0, jnp.concatenate([total, other], axis=1), jnp.concatenate([other, total], axis=1)
        )

    def way_back(values):
        back_scores, packed, normed, router, tok_gate, tok_up, gate, up = values
        other, own, through = call(
            functools.partial(router_kernel, experts, n_expert),
            "router_terms",
            [shape((experts, half), F32)] * 2 + [shape((tokens_here, width), F32)],
            (at, *back_scores, packed, normed, router),
            scalars=True,
        )
        total = own + over_core(other)
        for k in range(n_expert.bit_length() - 1):
            total = lax.reduce_precision(total, 8, 7)
            total = total + over_expert(total.astype(BF16), 1 << k).astype(F32)
        (row_pieces,) = call(
            functools.partial(row_kernel, n_expert, 8),
            "row_terms",
            [shape((n_expert, tokens_here, width), BF16)],
            (at, tok_gate, tok_up, gate, up, total),
            scalars=True,
            behind=1,
        )
        back_rows = lax.all_to_all(row_pieces, "expert", 0, 0, tiled=True)
        total, _ = lax.optimization_barrier((total, row_pieces))
        router_grad = lax.cond(always, sum_chips, lambda total: jnp.concatenate([total, total], axis=1), total)
        (grad_normed,) = call(
            final_kernel, "grad_normed", [shape((tokens_here, width), BF16)], (through, back_rows)
        )
        return grad_normed, router_grad

    grad_normed, router_grad = lax.cond(
        always,
        way_back,
        lambda values: (jnp.zeros((tokens_here, width), BF16), jnp.zeros((experts, width), F32)),
        (back_scores, packed, normed, router, tok_gate, tok_up, gate, up),
    )
    if not n_early:
        early_x = jnp.zeros((TILE, LANES), BF16)
    grads = call(
        functools.partial(sum_kernel, (n_chip, exp_dev, hidden_units, slots_each, n_early)),
        "weight_sum",
        [shape((hidden_units, exp_dev, piece), F32)] * 3,
        (at, *chip_pieces, own_narrow, other_narrow, early_x, grad_normed, router_grad),
        scalars=True,
        behind=2,
    )
    grads = [jnp.transpose(g, (1, 0, 2)) for g in grads]
    return (grad_normed, router_grad.T, *grads)


def solution(mesh):
    placed = (
        P(("dp", "expert"), None),
        P(("dp", "expert"), None),
        P(("dp", "expert"), None),
        P(),
        P("expert", None, None),
        P("expert", None, None),
        P("expert", None, None),
        P("dp", "expert", None, None, None),
    )
    return jax.shard_map(
        on_device,
        mesh=mesh,
        in_specs=placed,
        out_specs=(
            P(("dp", "expert"), None),
            P(),
            P("expert", None, "dp"),
            P("expert", None, "dp"),
            P("expert", None, "dp"),
        ),
        check_vma=False,
    )
```

time: 269 us -> 85.7 us (0.32)
  the two profiles are of different devices: /device:TPU:8 before, /device:TPU:0 now
where the time goes in v2:
time: 85.7 us; the launch traced here: 85.2 us
  waiting for transfers between devices  30.9 us (36%)
  starting transfers between devices  20.9 us (24%)
  Pallas kernels  18.6 us (22%)
  local copies, waits for them, and re-layouts  7.52 us (9%)
  other arithmetic  5.74 us (7%)
  between operations  1.39 us (2%)
    ppermute x8, waiting for transfers between devices, over_expert(): return lax.ppermute(value, 'expert', [(i, i ^ k) for i in range(n_expert)])  18.7 us
    pallas_call x7, Pallas kernels, call(): pl.pallas_call(kernel, out_shape=outs, in_specs=specs, out_specs=[pl.Bloc...  12.1 us
    ppermute x8, starting transfers between devices, over_expert(): return lax.ppermute(value, 'expert', [(i, i ^ k) for i in range(n_expert)])  9.84 us
    ppermute x5, waiting for transfers between devices, over_chip(): return lax.ppermute(value, 'dp', [(i, i ^ 2 * k) for i in range(n_dp)])  9.02 us
    ppermute x5, starting transfers between devices, over_chip(): return lax.ppermute(value, 'dp', [(i, i ^ 2 * k) for i in range(n_dp)])  7.34 us
    unnamed x16, local copies, waits for them, and re-layouts  5.64 us
    pallas_call x1, Pallas kernels, on_device(): pl.pallas_call(functools.partial(prepare_kernel, n_early, blocks), out_sh...  4.86 us
    all_to_all x1, starting transfers between devices, way_back(): back_rows = lax.all_to_all(row_pieces, 'expert', 0, 0, tiled=True)  3.56 us
  transfers between devices with their start and end apart: 17, of which 9 were waited for; matrix products, arithmetic and copies ran while one was open for 8% of the time, Pallas kernels for 13%

profile of v2, /device:TPU:0, one launch (start us, length us, event | category | flops | bytes accessed | tf_op | source)
XLA Modules:
  0.0 85.2 jit_solution(13976853094534190321)
XLA Ops:
  2.4 1.6 %route.1.refs_0_ = bf16[32,6272]{1,0:T(8,128)(2,1)S(1)} custom-call(s32[4,32]{1,0:T(4,128)S(1)} %bitcast.22, bf16[32,6144]{1,0:T(8,128)(2,1)} %normed_hbm.1, bf16[16,6144]{1,0:T(8,128)(2,1)} %bitcast.23, bf16[32,6144]{1,0:T(8,128)(2,1)S(1)} %copy-done.4), custom_call_target="tpu_custom_call" | custom-call | tf_op jit(solution)/shard_map/route/pallas_call | solution.py:351
  4.0 3.0 %collective-permute-start.6 = (bf16[32,6272]{1,0:T(8,128)(2,1)S(1)}, bf16[32,6272]{1,0:T(8,128)(2,1)S(1)}, u32[]{:S(2)}, u32[]{:S(2)}) collective-permute-start(bf16[32,6272]{1,0:T(8,128)(2,1)S(1)} %route.1.refs_0_), channel_id=1, source_target_pairs={{0,1},{1,0},{2,3},{3,2},{4,5},{5,4},{6,7},{7,6},{8,9},{9,8},{10,11... | collective-permute-start | bytes 1204232 | tf_op jit(solution)/shard_map/ppermute | solution.py:325
  7.0 1.5 %collective-permute-start.7 = (bf16[32,6272]{1,0:T(8,128)(2,1)S(1)}, bf16[32,6272]{1,0:T(8,128)(2,1)S(1)}, u32[]{:S(2)}, u32[]{:S(2)}) collective-permute-start(bf16[32,6272]{1,0:T(8,128)(2,1)S(1)} %route.1.refs_0_), channel_id=1, source_target_pairs={{0,2},{1,3},{2,0},{3,1},{4,6},{5,7},{6,4},{7,5},{8,10},{9,11},{10,... | collective-permute-start | bytes 1204232 | tf_op jit(solution)/shard_map/ppermute | solution.py:325
  8.5 1.5 %copy-done = bf16[1,4,4,9,6144]{4,2,3,1,0:T(4,128)(2,1)S(1)} copy-done((bf16[1,4,4,9,6144]{4,2,3,1,0:T(4,128)(2,1)S(1)}, bf16[1,4,4,9,6144]{4,2,3,1,0:T(4,128)(2,1)}, u32[]{:S(2)}) %copy-start) | copy-done | bytes 1769496
  10.0 1.2 %copy-done.2 = bf16[4,20,6144]{2,0,1:T(4,128)(2,1)S(1)} copy-done((bf16[4,20,6144]{2,0,1:T(4,128)(2,1)S(1)}, bf16[4,20,6144]{2,0,1:T(4,128)(2,1)}, u32[]{:S(2)}) %copy-start.2) | copy-done | bytes 983064
  11.2 1.2 %copy-done.3 = bf16[4,20,6144]{2,0,1:T(4,128)(2,1)S(1)} copy-done((bf16[4,20,6144]{2,0,1:T(4,128)(2,1)S(1)}, bf16[4,20,6144]{2,0,1:T(4,128)(2,1)}, u32[]{:S(2)}) %copy-start.3) | copy-done | bytes 983064
  12.4 4.9 %prepare.1 = (bf16[144,6144]{1,0:T(8,128)(2,1)S(1)}, bf16[80,6144]{1,0:T(8,128)(2,1)}, bf16[80,6144]{1,0:T(8,128)(2,1)}, bf16[80,6144]{1,0:T(8,128)(2,1)S(1)}, f...) custom-call(bf16[36,4,6144]{2,1,0:T(4,128)(2,1)S(1)} %bitcast.18, bf16[20,4,6144]{2,1,0:T(4,128)(2,1)S(1)} %bitcast.19, ...), custom_call_target="tpu_custom_call" | custom-call | tf_op jit(solution)/shard_map/prepare/pallas_call | solution.py:377
  17.4 9.0 %collective-permute-done.7.refs_2_ = bf16[32,6272]{1,0:T(8,128)(2,1)S(1)} collective-permute-done((bf16[32,6272]{1,0:T(8,128)(2,1)S(1)}, bf16[32,6272]{1,0:T(8,128)(2,1)S(1)}, u32[]{:S(2)}, u32[]{:S(2)}) %collective-permute-start.7) | collective-permute-done | bytes 401440 | tf_op jit(solution)/shard_map/ppermute | solution.py:325
  26.4 2.9 %experts.1 = (f32[32,128]{1,0:T(8,128)S(1)}, f32[32,128]{1,0:T(8,128)S(1)}, f32[32,128]{1,0:T(8,128)S(1)}, f32[32,128]{1,0:T(8,128)S(1)}, bf16[128,80]{1,0:T(8,1...) custom-call(s32[3]{0:T(128)S(1)} %pad_add_fusion.at, ...), custom_call_target="tpu_custom_call" | custom-call | tf_op jit(solution)/shard_map/experts/pallas_call | solution.py:339
  29.4 1.6 %collective-permute-start.10 = (f32[32,128]{1,0:T(8,128)S(1)}, f32[32,128]{1,0:T(8,128)S(1)}, u32[]{:S(2)}, u32[]{:S(2)}) collective-permute-start(f32[32,128]{1,0:T(8,128)S(1)} %get-tuple-element.92), channel_id=1, source_target_pairs={{0,2},{1,3},{2,0},{3,1},{4,6},{5,7},{6,4},{7,5},{8,10},{9,11},{10,... | collective-permute-start | bytes 49160 | tf_op jit(solution)/shard_map/ppermute | solution.py:325
  30.9 1.2 %collective-permute-start.11 = (f32[32,128]{1,0:T(8,128)S(1)}, f32[32,128]{1,0:T(8,128)S(1)}, u32[]{:S(2)}, u32[]{:S(2)}) collective-permute-start(f32[32,128]{1,0:T(8,128)S(1)} %get-tuple-element.93), channel_id=1, source_target_pairs={{0,3},{1,2},{2,1},{3,0},{4,7},{5,6},{6,5},{7,4},{8,11},{9,10},{10,... | collective-permute-start | bytes 49160 | tf_op jit(solution)/shard_map/ppermute | solution.py:325
  32.9 1.1 %weight_terms.1.mine = f32[4,240,768]{2,1,0:T(8,128)S(1)} custom-call(s32[3]{0:T(128)S(1)} %pad_add_fusion.at, bf16[32,6272]{1,0:T(8,128)(2,1)S(1)} %route.1.refs_0_, bf16[32,6272]{1,0:T(8,128)(2,1)S(1)} %collective-permute-done.6.refs_1_, bf16[32,6272]{1,0:T(8,128)(2,1)S(1)} %collective-permute-done.7.refs_2_, ...), custom_call_target="tpu_custom_call" | custom-call | tf_op jit(solution)/shard_map/weight_terms/pallas_call | solution.py:339
  34.0 1.6 %collective-permute-done.11.refs_2_ = f32[32,128]{1,0:T(8,128)S(1)} collective-permute-done((f32[32,128]{1,0:T(8,128)S(1)}, f32[32,128]{1,0:T(8,128)S(1)}, u32[]{:S(2)}, u32[]{:S(2)}) %collective-permute-start.11) | collective-permute-done | bytes 16416 | tf_op jit(solution)/shard_map/ppermute | solution.py:325
  35.9 1.1 %core_sum.1 = (f32[240,768]{1,0:T(8,128)S(1)}, bf16[240,768]{1,0:T(8,128)(2,1)}, bf16[240,768]{1,0:T(8,128)(2,1)}, bf16[240,768]{1,0:T(8,128)(2,1)}) custom-call(f32[4,240,768]{2,1,0:T(8,128)S(1)} %weight_terms.1.mine, bf16[4,240,768]{2,1,0:T(8,128)(2,1)S(1)} %collective-permute-done.12.theirs, ...), custom_call_target="tpu_custom_call" | custom-call | tf_op jit(solution)/shard_map/core_sum/pallas_call | solution.py:339
  37.0 1.6 %collective-permute-start.13 = (bf16[240,768]{1,0:T(8,128)(2,1)}, bf16[240,768]{1,0:T(8,128)(2,1)S(1)}, u32[]{:S(2)}, u32[]{:S(2)}) collective-permute-start(bf16[240,768]{1,0:T(8,128)(2,1)} %get-tuple-element.105), channel_id=1, source_target_pairs={{0,8},{4,12},{8,0},{12,4},{16,24},{20,28},{24,16},{28,20},{1,9},{5... | collective-permute-start | bytes 1105928 | tf_op jit(solution)/shard_map/ppermute | solution.py:331
  38.6 2.6 %collective-permute-start.14 = (bf16[240,768]{1,0:T(8,128)(2,1)}, bf16[240,768]{1,0:T(8,128)(2,1)}, u32[]{:S(2)}, u32[]{:S(2)}) collective-permute-start(bf16[240,768]{1,0:T(8,128)(2,1)} %get-tuple-element.106), channel_id=1, source_target_pairs={{0,16},{4,20},{8,24},{12,28},{16,0},{20,4},{24,8},{28,12},{1,17},{... | collective-permute-start | bytes 1105928 | tf_op jit(solution)/shard_map/ppermute | solution.py:331
  41.4 1.2 %slice.3 = s32[1,1]{0,1:T(1,128)} slice(s32[32,4]{0,1:T(4,128)} %param.14), slice={[0:1], [0:1]} | slice | bytes 8 | tf_op jit(solution)/shard_map/slice | solution.py:432
  43.3 39.8 %conditional.2 = (bf16[32,6144]{1,0:T(8,128)(2,1)}, f32[16,6144]{1,0:T(8,128)}) conditional(s32[]{:T(128)} %convert_element_type.30, () %tuple.23, (s32[3]{0:T(128)S(1)}, f32[32,128]{1,0:T(8,128)S(1)}, f32[32,128]{1,0:T(8,128)S(1)}, f32[32,128]{1,0:T(8,128)S(1)}, f32[32,128]{1,0:T(8,128)S(1)}, /*index=5*/bf16[32,6272]{1,0:T(8,128)(2,1)S(1)}, ...), branch_computations={%region_0.0_spmd, %region_1.4_spmd} | conditional | flops 1720322 | bytes 20447642 | solution.py:472
  43.3 1.3 %router_terms.1 = (f32[16,3072]{1,0:T(8,128)S(1)}, f32[16,3072]{1,0:T(8,128)S(1)}, f32[32,6144]{1,0:T(8,128)S(1)}) custom-call(s32[3]{0:T(128)S(1)} %get-tuple-element.38.at, f32[32,128]{1,0:T(8,128)S(1)} %get-tuple-element.39.refs_0_, f32[32,128]{1,0:T(8,128)S(1)} %get-tuple-element.40.refs_1_, f32[32,128]{1,0:T(8,128)S(1)} %get-tuple-element.41.refs_2_, ...), custom_call_target="tpu_custom_call" | custom-call | tf_op jit(solution)/shard_map/cond/branch_1_fun/router_terms/pallas_call | solution.py:339
  44.6 1.4 %collective-permute-done.3 = f32[16,3072]{1,0:T(8,128)S(1)} collective-permute-done((f32[16,3072]{1,0:T(8,128)S(1)}, f32[16,3072]{1,0:T(8,128)S(1)}, u32[]{:S(2)}, u32[]{:S(2)}) %collective-permute-start.3) | collective-permute-done | bytes 196640 | tf_op jit(solution)/shard_map/cond/branch_1_fun/ppermute | solution.py:328
  47.0 4.0 %collective-permute-done.4 = bf16[16,3072]{1,0:T(8,128)(2,1)S(1)} collective-permute-done((bf16[16,3072]{1,0:T(8,128)(2,1)S(1)}, bf16[16,3072]{1,0:T(8,128)(2,1)S(1)}, u32[]{:S(2)}, u32[]{:S(2)}) %collective-permute-start.4) | collective-permute-done | bytes 98336 | tf_op jit(solution)/shard_map/cond/branch_1_fun/ppermute | solution.py:325
  51.9 3.8 %collective-permute-done.5 = bf16[16,3072]{1,0:T(8,128)(2,1)S(1)} collective-permute-done((bf16[16,3072]{1,0:T(8,128)(2,1)S(1)}, bf16[16,3072]{1,0:T(8,128)(2,1)S(1)}, u32[]{:S(2)}, u32[]{:S(2)}) %collective-permute-start.5) | collective-permute-done | bytes 98336 | tf_op jit(solution)/shard_map/cond/branch_1_fun/ppermute | solution.py:325
  56.5 2.7 %row_terms.1 = bf16[4,32,6144]{2,1,0:T(8,128)(2,1)} custom-call(s32[3]{0:T(128)S(1)} %get-tuple-element.38.at, bf16[128,80]{1,0:T(8,128)(2,1)S(1)} %get-tuple-element.47.tok_gate, bf16[128,80]{1,0:T(8,128)(2,1)S(1)} %get-tuple-element.48.tok_up, bf16[80,6144]{1,0:T(8,128)(2,1)S(1)} %copy-done.8, bf16[80,6144]{1,0:T(8,128)(2,1)S(1)} %copy-done.9, ...), custom_call_target="tpu_custom_call" | custom-call | tf_op jit(solution)/shard_map/cond/branch_1_fun/row_terms/pallas_call | solution.py:339
  59.2 3.6 %all-to-all-start = ((bf16[4,32,6144]{2,1,0:T(8,128)(2,1)}), bf16[4,32,6144]{2,1,0:T(8,128)(2,1)S(1)}, u32[]{:S(2)}, u32[]{:S(2)}) async-start(bf16[4,32,6144]{2,1,0:T(8,128)(2,1)} %row_terms.1), calls=%async_computation | async-start | bytes 3145728 | tf_op jit(solution)/shard_map/cond/branch_1_fun/all_to_all | solution.py:464
  62.7 19.3 %conditional = (f32[16,6144]{1,0:T(8,128)}) conditional(s32[]{:T(128)} %convert_element_type.28, f32[16,3072]{1,0:T(8,128)} %copy-done.6, (s32[]{:T(128)}, f32[16,3072]{1,0:T(8,128)}) %tuple.30), branch_computations={%region_2.0_spmd, %region_3.3_spmd} | conditional | flops 933889 | bytes 3637386 | solution.py:466
  64.4 3.9 %collective-permute-done = bf16[16,3072]{1,0:T(8,128)(2,1)S(1)} collective-permute-done((bf16[16,3072]{1,0:T(8,128)(2,1)S(1)}, bf16[16,3072]{1,0:T(8,128)(2,1)S(1)}, u32[]{:S(2)}, u32[]{:S(2)}) %collective-permute-start) | collective-permute-done | bytes 98336 | tf_op jit(solution)/shard_map/cond/branch_1_fun/cond/branch_1_fun/ppermute | solution.py:331
  69.3 2.2 %collective-permute-start.1 = (bf16[16,3072]{1,0:T(8,128)(2,1)S(1)}, bf16[16,3072]{1,0:T(8,128)(2,1)S(1)}, u32[]{:S(2)}, u32[]{:S(2)}) collective-permute-start(bf16[16,3072]{1,0:T(8,128)(2,1)S(1)} %fusion), channel_id=1, source_target_pairs={{0,16},{4,20},{8,24},{12,28},{16,0},{20,4},{24,8},{28,12},{1,17},{... | collective-permute-start | bytes 294920 | tf_op jit(solution)/shard_map/cond/branch_1_fun/cond/branch_1_fun/ppermute | solution.py:331
  71.5 5.1 %collective-permute-done.1 = bf16[16,3072]{1,0:T(8,128)(2,1)S(1)} collective-permute-done((bf16[16,3072]{1,0:T(8,128)(2,1)S(1)}, bf16[16,3072]{1,0:T(8,128)(2,1)S(1)}, u32[]{:S(2)}, u32[]{:S(2)}) %collective-permute-start.1) | collective-permute-done | bytes 98336 | tf_op jit(solution)/shard_map/cond/branch_1_fun/cond/branch_1_fun/ppermute | solution.py:331
  76.6 1.7 %convert_add_fusion = f32[16,3072]{1,0:T(8,128)} fusion(bf16[16,3072]{1,0:T(8,128)(2,1)S(1)} %collective-permute-done.1, bf16[16,3072]{1,0:T(8,128)(2,1)S(1)} %collective-permute-done, f32[16,3072]{1,0:T(8,128)} %get-tuple-element.37), kind=kLoop, calls=%fused_computation.2 | loop fusion | flops 294912 | bytes 589824 | tf_op jit(solution)/shard_map/cond/branch_1_fun/cond/branch_1_fun/add | solution.py:437
  78.3 1.8 %collective-permute-done.2 = f32[16,3072]{1,0:T(8,128)} collective-permute-done((f32[16,3072]{1,0:T(8,128)}, f32[16,3072]{1,0:T(8,128)}, u32[]{:S(2)}, u32[]{:S(2)}) %collective-permute-start.2) | collective-permute-done | bytes 196640 | tf_op jit(solution)/shard_map/cond/branch_1_fun/cond/branch_1_fun/ppermute | solution.py:328
  80.1 2.0 %maximum_select_fusion = f32[16,6144]{1,0:T(8,128)} fusion(f32[16,3072]{1,0:T(8,128)} %collective-permute-done.2, f32[16,3072]{1,0:T(8,128)} %convert_add_fusion, pred[]{:T(512)S(6)} %eq.2), kind=kLoop, calls=%fused_computation.1 | loop fusion | flops 294912 | bytes 786433 | tf_op jit(solution)/shard_map/cond/branch_1_fun/cond/branch_1_fun/jit(_where)/select_n | solution.py:439
  83.1 2.1 %weight_sum.1 = (f32[20,4,768]{2,1,0:T(4,128)}, f32[20,4,768]{2,1,0:T(4,128)}, f32[20,4,768]{2,1,0:T(4,128)}) custom-call(s32[3]{0:T(128)S(1)} %pad_add_fusion.at, f32[240,768]{1,0:T(8,128)S(1)} %get-tuple-element.104.refs_0_, bf16[240,768]{1,0:T(8,128)(2,1)S(1)} %collective-permute-done.13.refs_1_, bf16[240,768]{1,0:T(8,128)(2,1)} %collective-permute-done.14.refs_2_, ...), custom_call_target="tpu_custom_call" | custom-call | tf_op jit(solution)/shard_map/weight_sum/pallas_call | solution.py:339
  (45 shorter events, 9.5 us)
Async XLA Ops:
  0.6 7.9 %copy-start.1 = (bf16[4,20,6144]{2,0,1:T(4,128)(2,1)S(1)}, bf16[4,20,6144]{2,0,1:T(4,128)(2,1)}, u32[]{:S(2)}) copy-start(bf16[4,20,6144]{2,0,1:T(4,128)(2,1)} %param.16) | copy-start | bytes 2949124
  0.6 1.1 %copy-start.4 = (bf16[32,6144]{1,0:T(8,128)(2,1)S(1)}, bf16[32,6144]{1,0:T(8,128)(2,1)}, u32[]{:S(2)}) copy-start(bf16[32,6144]{1,0:T(8,128)(2,1)} %upstream_hbm.1) | copy-start | bytes 1179652
  1.7 0.7 copy-start.5
  4.0 13.4 %collective-permute-start.6 = (bf16[32,6272]{1,0:T(8,128)(2,1)S(1)}, bf16[32,6272]{1,0:T(8,128)(2,1)S(1)}, u32[]{:S(2)}, u32[]{:S(2)}) collective-permute-start(bf16[32,6272]{1,0:T(8,128)(2,1)S(1)} %route.1.refs_0_), channel_id=1, source_target_pairs={{0,1},{1,0},{2,3},{3,2},{4,5},{5,4},{6,7},{7,6},{8,9},{9,8},{10,11... | collective-permute-start | bytes 1204232 | tf_op jit(solution)/shard_map/ppermute | solution.py:325
  7.0 19.4 %collective-permute-start.7 = (bf16[32,6272]{1,0:T(8,128)(2,1)S(1)}, bf16[32,6272]{1,0:T(8,128)(2,1)S(1)}, u32[]{:S(2)}, u32[]{:S(2)}) collective-permute-start(bf16[32,6272]{1,0:T(8,128)(2,1)S(1)} %route.1.refs_0_), channel_id=1, source_target_pairs={{0,2},{1,3},{2,0},{3,1},{4,6},{5,7},{6,4},{7,5},{8,10},{9,11},{10,... | collective-permute-start | bytes 1204232 | tf_op jit(solution)/shard_map/ppermute | solution.py:325
  8.5 17.8 %collective-permute-start.8 = (bf16[32,6272]{1,0:T(8,128)(2,1)S(1)}, bf16[32,6272]{1,0:T(8,128)(2,1)S(1)}, u32[]{:S(2)}, u32[]{:S(2)}) collective-permute-start(bf16[32,6272]{1,0:T(8,128)(2,1)S(1)} %route.1.refs_0_), channel_id=1, source_target_pairs={{0,3},{1,2},{2,1},{3,0},{4,7},{5,6},{6,5},{7,4},{8,11},{9,10},{10,... | collective-permute-start | bytes 1204232 | tf_op jit(solution)/shard_map/ppermute | solution.py:325
  8.5 1.5 %copy-start = (bf16[1,4,4,9,6144]{4,2,3,1,0:T(4,128)(2,1)S(1)}, bf16[1,4,4,9,6144]{4,2,3,1,0:T(4,128)(2,1)}, u32[]{:S(2)}) copy-start(bf16[1,4,4,9,6144]{4,2,3,1,0:T(4,128)(2,1)} %param.19) | copy-start | bytes 5308420
  10.0 1.2 %copy-start.2 = (bf16[4,20,6144]{2,0,1:T(4,128)(2,1)S(1)}, bf16[4,20,6144]{2,0,1:T(4,128)(2,1)}, u32[]{:S(2)}) copy-start(bf16[4,20,6144]{2,0,1:T(4,128)(2,1)} %param.17) | copy-start | bytes 2949124
  11.2 1.2 %copy-start.3 = (bf16[4,20,6144]{2,0,1:T(4,128)(2,1)S(1)}, bf16[4,20,6144]{2,0,1:T(4,128)(2,1)}, u32[]{:S(2)}) copy-start(bf16[4,20,6144]{2,0,1:T(4,128)(2,1)} %param.18) | copy-start | bytes 2949124
  29.3 6.6 %collective-permute-start.12 = (bf16[4,240,768]{2,1,0:T(8,128)(2,1)S(1)}, bf16[4,240,768]{2,1,0:T(8,128)(2,1)S(1)}, u32[]{:S(2)}, u32[]{:S(2)}) collective-permute-start(bf16[4,240,768]{2,1,0:T(8,128)(2,1)S(1)} %get-tuple-element.102), channel_id=1, source_target_pairs={{0,4},{4,0},{8,12},{12,8},{16,20},{20,16},{24,28},{28,24},{1,5},{5... | collective-permute-start | bytes 4423688 | tf_op jit(solution)/shard_map/ppermute | solution.py:328
  29.4 4.6 %collective-permute-start.10 = (f32[32,128]{1,0:T(8,128)S(1)}, f32[32,128]{1,0:T(8,128)S(1)}, u32[]{:S(2)}, u32[]{:S(2)}) collective-permute-start(f32[32,128]{1,0:T(8,128)S(1)} %get-tuple-element.92), channel_id=1, source_target_pairs={{0,2},{1,3},{2,0},{3,1},{4,6},{5,7},{6,4},{7,5},{8,10},{9,11},{10,... | collective-permute-start | bytes 49160 | tf_op jit(solution)/shard_map/ppermute | solution.py:325
  30.9 4.6 %collective-permute-start.11 = (f32[32,128]{1,0:T(8,128)S(1)}, f32[32,128]{1,0:T(8,128)S(1)}, u32[]{:S(2)}, u32[]{:S(2)}) collective-permute-start(f32[32,128]{1,0:T(8,128)S(1)} %get-tuple-element.93), channel_id=1, source_target_pairs={{0,3},{1,2},{2,1},{3,0},{4,7},{5,6},{6,5},{7,4},{8,11},{9,10},{10,... | collective-permute-start | bytes 49160 | tf_op jit(solution)/shard_map/ppermute | solution.py:325
  32.1 3.7 %collective-permute-start.9 = (f32[32,128]{1,0:T(8,128)S(1)}, f32[32,128]{1,0:T(8,128)S(1)}, u32[]{:S(2)}, u32[]{:S(2)}) collective-permute-start(f32[32,128]{1,0:T(8,128)S(1)} %get-tuple-element.91), channel_id=1, source_target_pairs={{0,1},{1,0},{2,3},{3,2},{4,5},{5,4},{6,7},{7,6},{8,9},{9,8},{10,11... | collective-permute-start | bytes 49160 | tf_op jit(solution)/shard_map/ppermute | solution.py:325
  35.9 7.4 %copy-start.7 = (bf16[32,6144]{1,0:T(8,128)(2,1)S(1)}, bf16[32,6144]{1,0:T(8,128)(2,1)}, u32[]{:S(2)}) copy-start(bf16[32,6144]{1,0:T(8,128)(2,1)} %normed_hbm.1) | copy-start | bytes 1179652
  35.9 7.4 %copy-start.10 = (bf16[6144,16]{0,1:T(8,128)(2,1)S(1)}, bf16[6144,16]{0,1:T(8,128)(2,1)}, u32[]{:S(2)}) copy-start(bf16[6144,16]{0,1:T(8,128)(2,1)} %param.15) | copy-start | bytes 589828
  37.0 46.0 %collective-permute-start.13 = (bf16[240,768]{1,0:T(8,128)(2,1)}, bf16[240,768]{1,0:T(8,128)(2,1)S(1)}, u32[]{:S(2)}, u32[]{:S(2)}) collective-permute-start(bf16[240,768]{1,0:T(8,128)(2,1)} %get-tuple-element.105), channel_id=1, source_target_pairs={{0,8},{4,12},{8,0},{12,4},{16,24},{20,28},{24,16},{28,20},{1,9},{5... | collective-permute-start | bytes 1105928 | tf_op jit(solution)/shard_map/ppermute | solution.py:331
  38.6 44.5 %collective-permute-start.14 = (bf16[240,768]{1,0:T(8,128)(2,1)}, bf16[240,768]{1,0:T(8,128)(2,1)}, u32[]{:S(2)}, u32[]{:S(2)}) collective-permute-start(bf16[240,768]{1,0:T(8,128)(2,1)} %get-tuple-element.106), channel_id=1, source_target_pairs={{0,16},{4,20},{8,24},{12,28},{16,0},{20,4},{24,8},{28,12},{1,17},{... | collective-permute-start | bytes 1105928 | tf_op jit(solution)/shard_map/ppermute | solution.py:331
  41.2 41.9 %collective-permute-start.15 = (bf16[240,768]{1,0:T(8,128)(2,1)}, bf16[240,768]{1,0:T(8,128)(2,1)}, u32[]{:S(2)}, u32[]{:S(2)}) collective-permute-start(bf16[240,768]{1,0:T(8,128)(2,1)} %get-tuple-element.107), channel_id=1, source_target_pairs={{0,24},{4,28},{8,16},{12,20},{16,8},{20,12},{24,0},{28,4},{1,25},{... | collective-permute-start | bytes 1105928 | tf_op jit(solution)/shard_map/ppermute | solution.py:331
  43.3 13.2 %copy-start.8 = (bf16[80,6144]{1,0:T(8,128)(2,1)S(1)}, bf16[80,6144]{1,0:T(8,128)(2,1)}, u32[]{:S(2)}) copy-start(bf16[80,6144]{1,0:T(8,128)(2,1)} %get-tuple-element.49.gate) | copy-start | bytes 2949124 | tf_op jit(solution)/shard_map/cond
  43.3 13.2 %copy-start.9 = (bf16[80,6144]{1,0:T(8,128)(2,1)S(1)}, bf16[80,6144]{1,0:T(8,128)(2,1)}, u32[]{:S(2)}) copy-start(bf16[80,6144]{1,0:T(8,128)(2,1)} %get-tuple-element.50.up) | copy-start | bytes 2949124 | tf_op jit(solution)/shard_map/cond
  44.6 1.5 %collective-permute-start.3 = (f32[16,3072]{1,0:T(8,128)S(1)}, f32[16,3072]{1,0:T(8,128)S(1)}, u32[]{:S(2)}, u32[]{:S(2)}) collective-permute-start(f32[16,3072]{1,0:T(8,128)S(1)} %get-tuple-element.52), channel_id=1, source_target_pairs={{0,4},{4,0},{8,12},{12,8},{16,20},{20,16},{24,28},{28,24},{1,5},{5... | collective-permute-start | bytes 589832 | tf_op jit(solution)/shard_map/cond/branch_1_fun/ppermute | solution.py:328
  46.1 4.9 %collective-permute-start.4 = (bf16[16,3072]{1,0:T(8,128)(2,1)S(1)}, bf16[16,3072]{1,0:T(8,128)(2,1)S(1)}, u32[]{:S(2)}, u32[]{:S(2)}) collective-permute-start(bf16[16,3072]{1,0:T(8,128)(2,1)S(1)} %fusion.2), channel_id=1, source_target_pairs={{0,1},{1,0},{2,3},{3,2},{4,5},{5,4},{6,7},{7,6},{8,9},{9,8},{10,11... | collective-permute-start | bytes 294920 | tf_op jit(solution)/shard_map/cond/branch_1_fun/ppermute | solution.py:325
  51.0 4.7 %collective-permute-start.5 = (bf16[16,3072]{1,0:T(8,128)(2,1)S(1)}, bf16[16,3072]{1,0:T(8,128)(2,1)S(1)}, u32[]{:S(2)}, u32[]{:S(2)}) collective-permute-start(bf16[16,3072]{1,0:T(8,128)(2,1)S(1)} %fusion.1), channel_id=1, source_target_pairs={{0,2},{1,3},{2,0},{3,1},{4,6},{5,7},{6,4},{7,5},{8,10},{9,11},{10,... | collective-permute-start | bytes 294920 | tf_op jit(solution)/shard_map/cond/branch_1_fun/ppermute | solution.py:325
  55.8 0.7 copy-start.6
  59.2 22.9 %all-to-all-start = ((bf16[4,32,6144]{2,1,0:T(8,128)(2,1)}), bf16[4,32,6144]{2,1,0:T(8,128)(2,1)S(1)}, u32[]{:S(2)}, u32[]{:S(2)}) async-start(bf16[4,32,6144]{2,1,0:T(8,128)(2,1)} %row_terms.1), calls=%async_computation | async-start | bytes 3145728 | tf_op jit(solution)/shard_map/cond/branch_1_fun/all_to_all | solution.py:464
  63.7 4.7 %collective-permute-start = (bf16[16,3072]{1,0:T(8,128)(2,1)S(1)}, bf16[16,3072]{1,0:T(8,128)(2,1)S(1)}, u32[]{:S(2)}, u32[]{:S(2)}) collective-permute-start(bf16[16,3072]{1,0:T(8,128)(2,1)S(1)} %reduce-precision_convert_fusion), channel_id=1, source_target_pairs={{0,8},{4,12},{8,0},{12,4},{16,24},{20,28},{24,16},{28,20},{1,9},{5... | collective-permute-start | bytes 294920 | tf_op jit(solution)/shard_map/cond/branch_1_fun/cond/branch_1_fun/ppermute | solution.py:331
  69.3 7.3 %collective-permute-start.1 = (bf16[16,3072]{1,0:T(8,128)(2,1)S(1)}, bf16[16,3072]{1,0:T(8,128)(2,1)S(1)}, u32[]{:S(2)}, u32[]{:S(2)}) collective-permute-start(bf16[16,3072]{1,0:T(8,128)(2,1)S(1)} %fusion), channel_id=1, source_target_pairs={{0,16},{4,20},{8,24},{12,28},{16,0},{20,4},{24,8},{28,12},{1,17},{... | collective-permute-start | bytes 294920 | tf_op jit(solution)/shard_map/cond/branch_1_fun/cond/branch_1_fun/ppermute | solution.py:331
  78.3 1.8 %collective-permute-start.2 = (f32[16,3072]{1,0:T(8,128)}, f32[16,3072]{1,0:T(8,128)}, u32[]{:S(2)}, u32[]{:S(2)}) collective-permute-start(f32[16,3072]{1,0:T(8,128)} %convert_add_fusion), channel_id=1, source_target_pairs={{0,4},{4,0},{8,12},{12,8},{16,20},{20,16},{24,28},{28,24},{1,5},{5... | collective-permute-start | bytes 589832 | tf_op jit(solution)/shard_map/cond/branch_1_fun/cond/branch_1_fun/ppermute | solution.py:328

commit v3 on v2

--- a/solution.py
+++ b/solution.py
@@ -35,16 +35,17 @@
     return high, (value - high.astype(F32)).astype(BF16)
 
 
-def route_kernel(experts, ids, normed_hbm, router_hbm, upstream_hbm, packed, normed, router, upstream, sems):
+def route_kernel(experts, *refs):
+    sources, (first, packed, ids, normed, router, upstream, sems) = refs[:4], refs[4:]
     tokens, width = normed.shape
+    half = width // 2
     copies = [
         pltpu.make_async_copy(source, target, sems.at[k])
-        for k, (source, target) in enumerate(
-            ((normed_hbm, normed), (router_hbm, router), (upstream_hbm, upstream))
-        )
+        for k, (source, target) in enumerate(zip(sources, (ids, normed, router, upstream)))
     ]
     for copy in copies:
         copy.start()
+    copies[0].wait()
     expert = iota((experts, tokens), 0)
     named_t = expert < 0
     for k in range(ids.shape[0]):
@@ -55,8 +56,8 @@
     earlier = (iota((tokens, tokens), 1) < iota((tokens, tokens), 0)).astype(F32).astype(BF16)
     slot = dot(earlier, named_f.astype(BF16), (1, 0))
     code = jnp.where(named, slot + 1.0, 0.0)
-    copies[0].wait()
     copies[1].wait()
+    copies[2].wait()
     logits = dot(normed[...], router[...], (1, 1))
     largest = jnp.max(jnp.where(named, logits, -jnp.inf), axis=1, keepdims=True)
     weight = jnp.where(named, jnp.exp(jnp.where(named, logits - largest, 0.0)), 0.0)
@@ -65,9 +66,10 @@
     middle = (weight - high).astype(BF16).astype(F32)
     low = weight - high - middle
     rest = jnp.zeros((tokens, LANES - 4 * experts), F32)
-    packed[:, width:] = jnp.concatenate([high, middle, low, code, rest], axis=1).astype(BF16)
-    copies[2].wait()
-    packed[:, :width] = upstream[...]
+    packed[:, half:] = jnp.concatenate([high, middle, low, code, rest], axis=1).astype(BF16)
+    copies[3].wait()
+    first[...] = upstream[:, :half]
+    packed[:, :half] = upstream[:, half:]
 
 
 def prepare_kernel(n_early, blocks, *refs):
@@ -108,27 +110,30 @@
     return wanted(row, column // exp_dev, column % exp_dev).astype(F32).astype(BF16)
 
 
-def block_terms(late, tok_hidden, inputs, rows_u, start, piece):
+def block_terms(late, tok_hidden, inputs, arrived, start, piece):
     at = pl.ds(pl.multiple_of(start, LANES), piece)
-    arrived = jnp.concatenate([u[:, at] for u in rows_u], axis=0)
-    return dot(late, inputs[:, at], (1, 0)), dot(tok_hidden, arrived, (1, 0))
+    return dot(late, inputs[:, at], (1, 0)), dot(tok_hidden, arrived[:, at], (1, 0))
 
 
 def expert_kernel(sizes, at, *refs):
-    n_expert, exp_dev, capacity, tokens_here, n_chip, piece, n_early = sizes
-    rows_u, rest = refs[:n_expert], refs[n_expert:]
+    n_expert, exp_dev, capacity, tokens_here, n_chip, piece, n_early, even = sizes
+    firsts, seconds, rest = refs[:n_expert], refs[n_expert : 2 * n_expert], refs[2 * n_expert :]
     down, pre_gate, pre_up, inputs = rest[:4]
     scores = rest[4 : 4 + n_expert]
-    tok_gate, tok_up, tok_hidden, slot_late, slot_early = rest[4 + n_expert : 9 + n_expert]
+    tok_gate, tok_up, tok_hidden, slot_late, slot_early, arrived = rest[4 + n_expert : 10 + n_expert]
     me, chip, core = at[0], at[1], at[2]
     experts = exp_dev * n_expert
     tokens = tokens_here * n_expert
     hidden_all, width = down.shape
+    half = width // 2
     hidden_units = hidden_all // exp_dev
     slots = exp_dev * capacity * n_expert
-    packed = jnp.concatenate([u[:, width:] for u in rows_u], axis=0)
-    arrived = jnp.concatenate([u[:, :width] for u in rows_u], axis=0)
-    grad_hidden_raw = dot(arrived, down[...], (1, 1))
+    packed = jnp.concatenate([u[:, half:] for u in seconds], axis=0)
+    for r in range(n_expert):
+        rows = slice(r * tokens_here, (r + 1) * tokens_here)
+        arrived[rows, :half] = firsts[r][...]
+        arrived[rows, half:] = seconds[r][:, :half]
+    grad_hidden_raw = dot(arrived[...], down[...], (1, 1))
 
     expert_of_slot = me * exp_dev + iota((LANES, slots), 1) // (capacity * n_expert)
     weight_at = dot(packed, pick(expert_of_slot, experts, (0, 1, 2), slots), (1, 0))
@@ -179,24 +184,23 @@
     fold = [unit_rows(slot_early.shape[0], hidden_all, exp_dev, f, lambda i, unit, e: i == unit) for f in (0, hidden_units)]
     early = dot(fold[0], grad_gate, (1, 1)) + dot(fold[1], grad_up, (1, 1))
     slot_early[...] = early[:, :LANES].astype(BF16)
-    if len(rest) > 9 + n_expert:
-        theirs = rest[9 + n_expert]
+    if even:
+        theirs = rest[10 + n_expert]
         n = late.shape[0]
         for r in range(n_chip):
             start = (2 * (chip ^ r) + 1 - core) * piece
-            first, second = block_terms(late, turned, inputs, rows_u, start, piece)
+            first, second = block_terms(late, turned, inputs, arrived, start, piece)
             theirs[r, :n] = first.astype(BF16)
             theirs[r, n:] = second.astype(BF16)
 
 
-def weight_kernel(sizes, at, *refs):
-    n_expert, n_chip, piece = sizes
-    rows_u, (inputs, late, tok_hidden, mine) = refs[:n_expert], refs[n_expert:]
+def weight_kernel(sizes, at, arrived, inputs, late, tok_hidden, mine):
+    n_chip, piece = sizes
     chip, core = at[1], at[2]
     n = late.shape[0]
     for r in range(n_chip):
         start = (2 * (chip ^ r) + core) * piece
-        first, second = block_terms(late[...], tok_hidden[...], inputs, rows_u, start, piece)
+        first, second = block_terms(late[...], tok_hidden[...], inputs, arrived, start, piece)
         mine[r, :n] = first
         mine[r, n:] = second
 
@@ -228,11 +232,45 @@
             out[at[0] ^ r, :, lanes] = total[r * size : (r + 1) * size].astype(out.dtype)
 
 
-def sum_kernel(sizes, at, *refs):
+def router_kernel(experts, n_expert, at, *refs):
+    scores, (packed, normed, router, other, own, through) = refs[:n_expert], refs[n_expert:]
+    picked = scores[0][...]
+    for s in scores[1:]:
+        picked = picked + s[...]
+    picked = picked[:, :experts]
+    half = normed.shape[1] // 2
+    tail = packed[:, half:].astype(F32)
+    weight = tail[:, :experts] + tail[:, experts : 2 * experts] + tail[:, 2 * experts : 3 * experts]
+    code = tail[:, 3 * experts : 4 * experts]
+    grad = jnp.where(code > 0.5, picked - weight * jnp.sum(picked, axis=1, keepdims=True), 0.0)
+    high, low = split_high_low(grad)
+    core = at[2]
+    for out, part in ((other, 1 - core), (own, core)):
+        values = normed[:, pl.ds(pl.multiple_of(part * half, LANES), half)]
+        out[...] = dot(high, values, (0, 0)) + dot(low, values, (0, 0))
+    through[...] = dot(high, router[...], (1, 0)) + dot(low, router[...], (1, 0))
+
+
+def terms_kernel(count, *refs):
+    terms, out = refs[:count], refs[-1]
+    while len(terms) > 1:
+        terms = [terms[k][...].astype(F32) + terms[k + 1][...].astype(F32) for k in range(0, len(terms), 2)]
+    out[...] = terms[0].astype(out.dtype)
+
+
+def finish_kernel(sizes, at, *refs):
     n_chip, exp_dev, hidden_units, slots_each, n_early = sizes
     pieces, own, other, rows = refs[:n_chip], refs[n_chip], refs[n_chip + 1], refs[n_chip + 2]
-    outs = refs[-3:]
+    mine, theirs, through, back = refs[n_chip + 3 : n_chip + 7]
+    grad_normed, router_grad, *outs = refs[-5:]
     chip, core = at[1], at[2]
+    half = mine.shape[1]
+    router_grad[:, pl.ds(pl.multiple_of(core * half, LANES), half)] = mine[...]
+    router_grad[:, pl.ds(pl.multiple_of((1 - core) * half, LANES), half)] = theirs[...]
+    rows_total = through[...]
+    for r in range(back.shape[0]):
+        rows_total = rows_total + back[r].astype(F32)
+    grad_normed[...] = rows_total.astype(grad_normed.dtype)
     m = pieces[0].shape[0]
     n = m - exp_dev * hidden_units
     total = pieces[0][...]
@@ -266,33 +304,6 @@
         outs[2][:, e, :] = total[n + e * hidden_units : n + (e + 1) * hidden_units]
 
 
-def router_kernel(experts, n_expert, at, *refs):
-    scores, (packed, normed, router, other, own, through) = refs[:n_expert], refs[n_expert:]
-    picked = scores[0][...]
-    for s in scores[1:]:
-        picked = picked + s[...]
-    picked = picked[:, :experts]
-    width = normed.shape[1]
-    half = width // 2
-    tail = packed[:, width:].astype(F32)
-    weight = tail[:, :experts] + tail[:, experts : 2 * experts] + tail[:, 2 * experts : 3 * experts]
-    code = tail[:, 3 * experts : 4 * experts]
-    grad = jnp.where(code > 0.5, picked - weight * jnp.sum(picked, axis=1, keepdims=True), 0.0)
-    high, low = split_high_low(grad)
-    core = at[2]
-    for out, part in ((other, 1 - core), (own, core)):
-        values = normed[:, pl.ds(pl.multiple_of(part * half, LANES), half)]
-        out[...] = dot(high, values, (0, 0)) + dot(low, values, (0, 0))
-    through[...] = dot(high, router[...], (1, 0)) + dot(low, router[...], (1, 0))
-
-
-def final_kernel(through, pieces, out):
-    total = through[...]
-    for r in range(pieces.shape[0]):
-        total = total + pieces[r].astype(F32)
-    out[...] = total.astype(out.dtype)
-
-
 def on_device(normed, upstream, expert_ids, router_weight, gate_weight, up_weight, down_weight, saved_inputs):
     n_expert = lax.axis_size("expert")
     n_dp = lax.axis_size("dp")
@@ -330,6 +341,9 @@
     def over_chip(value, k):
         return lax.ppermute(value, "dp", [(i, i ^ (2 * k)) for i in range(n_dp)])
 
+    def in_hbm(*values):
+        return [pltpu.with_memory_space_constraint(value, pltpu.HBM) for value in values]
+
     def call(kernel, name, outs, args, scalars=False, behind=0):
         specs = [pl.BlockSpec(memory_space=pltpu.VMEM)] * len(args)
         if scalars:
@@ -348,22 +362,30 @@
 
     at = jnp.stack([me, chip, core]).astype(jnp.int32)
     router = router_weight.T
-    packed = pl.pallas_call(
+    first, packed = pl.pallas_call(
         functools.partial(route_kernel, experts),
-        out_shape=shape((tokens_here, width + LANES), BF16),
-        in_specs=[pl.BlockSpec(memory_space=pltpu.VMEM)] + [pl.BlockSpec(memory_space=pltpu.HBM)] * 3,
-        out_specs=pl.BlockSpec(memory_space=pltpu.VMEM),
+        out_shape=[shape((tokens_here, half), BF16), shape((tokens_here, half + LANES), BF16)],
+        in_specs=[pl.BlockSpec(memory_space=pltpu.HBM)] * 4,
+        out_specs=[pl.BlockSpec(memory_space=pltpu.VMEM)] * 2,
         scratch_shapes=[
+            pltpu.VMEM(expert_ids.shape[::-1], jnp.int32),
             pltpu.VMEM((tokens_here, width), BF16),
             pltpu.VMEM((experts, width), BF16),
             pltpu.VMEM((tokens_here, width), BF16),
-            pltpu.SemaphoreType.DMA((3,)),
+            pltpu.SemaphoreType.DMA((4,)),
         ],
         compiler_params=pltpu.CompilerParams(vmem_limit_bytes=VMEM_BYTES),
         cost_estimate=pl.CostEstimate(flops=0, bytes_accessed=0, transcendentals=0),
         name="route",
-    )(expert_ids.T, normed, router, upstream)
-    rows_u = [packed] + [over_expert(packed, k) for k in range(1, n_expert)]
+    )(*in_hbm(expert_ids.T, normed, router, upstream))
+    if n_expert == 4:
+        first_1, second_2 = over_expert(first, 1), over_expert(packed, 2)
+        second_1, first_2 = over_expert(packed, 1), over_expert(first, 2)
+        firsts = [first, first_1, first_2, over_expert(first_1, 2)]
+        seconds = [packed, second_1, second_2, over_expert(second_2, 1)]
+    else:
+        firsts = [first] + [over_expert(first, k) for k in range(1, n_expert)]
+        seconds = [packed] + [over_expert(packed, k) for k in range(1, n_expert)]
 
     blocks = n_dp if even else 8
     sources = [jnp.transpose(saved_inputs[0], (0, 2, 1, 3)).reshape(exp_dev * capacity, n_expert, width)]
@@ -384,32 +406,33 @@
         compiler_params=pltpu.CompilerParams(vmem_limit_bytes=VMEM_BYTES),
         cost_estimate=pl.CostEstimate(flops=0, bytes_accessed=0, transcendentals=0),
         name="prepare",
-    )(*sources)
+    )(*in_hbm(*sources))
     if n_early:
         early_x = lax.all_to_all(early_x[0], "dp", 0, 0, tiled=True)
 
     outs = call(
-        functools.partial(expert_kernel, (n_expert, exp_dev, capacity, tokens_here, n_chip, piece, n_early)),
+        functools.partial(expert_kernel, (n_expert, exp_dev, capacity, tokens_here, n_chip, piece, n_early, even)),
         "experts",
         [shape((tokens_here, LANES), F32)] * n_expert
         + [shape((tokens, hidden_all), BF16)] * 2
         + [shape((hidden_all, tokens), BF16), shape((late_rows, slots), BF16), shape((narrow, LANES), BF16)]
+        + [shape((tokens, width), BF16)]
         + [shape((n_chip, sent_rows, piece), BF16)] * even,
-        (at, *rows_u, down, pre_gate, pre_up, inputs),
+        (at, *firsts, *seconds, down, pre_gate, pre_up, inputs),
         scalars=True,
     )
     scores = outs[:n_expert]
-    tok_gate, tok_up, tok_hidden, slot_late, own_narrow = outs[n_expert : n_expert + 5]
+    tok_gate, tok_up, tok_hidden, slot_late, own_narrow, arrived = outs[n_expert : n_expert + 6]
     back_scores = [scores[0]] + [over_expert(scores[k], k) for k in range(1, n_expert)]
     other_narrow = over_core(own_narrow) if n_early else own_narrow
     if even:
-        from_core = over_core(outs[n_expert + 5])
+        from_core = over_core(outs[n_expert + 6])
         sent = shape((sent_rows + TILE * bool(n_early), piece), BF16)
         (mine,) = call(
-            functools.partial(weight_kernel, (n_expert, n_chip, piece)),
+            functools.partial(weight_kernel, (n_chip, piece)),
             "weight_terms",
             [shape((n_chip, sent_rows, piece), F32)],
-            (at, *rows_u, inputs, slot_late, tok_hidden),
+            (at, arrived, inputs, slot_late, tok_hidden),
             scalars=True,
         )
         chip_sums = call(
@@ -420,25 +443,33 @@
             behind=n_expert - 1,
         )
     else:
-        arrived = jnp.concatenate([u[:, :width] for u in rows_u], axis=0)
         terms = [dot(slot_late, inputs, (1, 0)), dot(tok_hidden, arrived, (1, 0))]
         terms = jnp.concatenate(terms, axis=0).reshape(sent_rows, n_chip, 2, piece)
         terms = jnp.transpose(terms, (2, 1, 0, 3))
         from_core = over_core(terms[1 - core].astype(BF16))
         terms = terms[core] + from_core.astype(F32)
         chip_sums = [terms[chip ^ k].astype(BF16 if k else F32) for k in range(n_chip)]
-    chip_pieces = [chip_sums[0]] + [over_chip(chip_sums[k], k) for k in range(1, n_chip)]
-
-    always = expert_ids[0, 0] >= 0
+    moved = {k: over_chip(chip_sums[k], k) for k in range(n_chip - 1, 0, -1)}
+    chip_pieces = [chip_sums[0]] + [moved[k] for k in range(1, n_chip)]
+
+    always = dp < n_dp
+
+    def add_terms(terms, dtype, *behind):
+        kernel = functools.partial(terms_kernel, len(terms))
+        return call(kernel, "add_terms", [shape(terms[0].shape, dtype)], (*terms, *behind), behind=len(behind))[0]
+
+    def sum_over(total, move, count, dtype, at_once, *behind):
+        if at_once:
+            return add_terms([total] + [move(total, k) for k in range(1, count)], dtype, *behind)
+        rounds = count.bit_length() - 1
+        for k in range(rounds):
+            last = k == rounds - 1
+            total = add_terms([total, move(total, 1 << k)], dtype if last else BF16, *behind * last)
+        return total
 
     def sum_chips(total):
-        for k in range(n_chip.bit_length() - 1):
-            total = lax.reduce_precision(total, 8, 7)
-            total = total + over_chip(total.astype(BF16), 1 << k).astype(F32)
-        other = over_core(total)
-        return jnp.where(
-            core == 0, jnp.concatenate([total, other], axis=1), jnp.concatenate([other, total], axis=1)
-        )
+        total = sum_over(total, over_chip, n_chip, F32, False)
+        return total, over_core(total)
 
     def way_back(values):
         back_scores, packed, normed, router, tok_gate, tok_up, gate, up = values
@@ -449,41 +480,40 @@
             (at, *back_scores, packed, normed, router),
             scalars=True,
         )
-        total = own + over_core(other)
-        for k in range(n_expert.bit_length() - 1):
-            total = lax.reduce_precision(total, 8, 7)
-            total = total + over_expert(total.astype(BF16), 1 << k).astype(F32)
         (row_pieces,) = call(
             functools.partial(row_kernel, n_expert, 8),
             "row_terms",
             [shape((n_expert, tokens_here, width), BF16)],
-            (at, tok_gate, tok_up, gate, up, total),
+            (at, tok_gate, tok_up, gate, up, other),
             scalars=True,
             behind=1,
         )
+        total = add_terms([own, over_core(other)], BF16)
+        total = sum_over(total, over_expert, n_expert, BF16, False, row_pieces)
+        row_pieces, total = lax.optimization_barrier((row_pieces, total))
         back_rows = lax.all_to_all(row_pieces, "expert", 0, 0, tiled=True)
-        total, _ = lax.optimization_barrier((total, row_pieces))
-        router_grad = lax.cond(always, sum_chips, lambda total: jnp.concatenate([total, total], axis=1), total)
-        (grad_normed,) = call(
-            final_kernel, "grad_normed", [shape((tokens_here, width), BF16)], (through, back_rows)
-        )
-        return grad_normed, router_grad
-
-    grad_normed, router_grad = lax.cond(
+        mine, theirs = lax.cond(always, sum_chips, lambda total: (jnp.zeros((experts, half), F32),) * 2, total)
+        return mine, theirs, through, back_rows
+
+    first_score, _ = lax.optimization_barrier((back_scores[0], chip_sums[0]))
+    back_scores = [first_score] + back_scores[1:]
+    outs = [shape((experts, half), F32)] * 2 + [shape((tokens_here, width), F32)]
+    outs += [shape((n_expert, tokens_here, width), BF16)]
+    back = lax.cond(
         always,
         way_back,
-        lambda values: (jnp.zeros((tokens_here, width), BF16), jnp.zeros((experts, width), F32)),
+        lambda values: tuple(jnp.zeros(o.shape, o.dtype) for o in outs),
         (back_scores, packed, normed, router, tok_gate, tok_up, gate, up),
     )
     if not n_early:
         early_x = jnp.zeros((TILE, LANES), BF16)
-    grads = call(
-        functools.partial(sum_kernel, (n_chip, exp_dev, hidden_units, slots_each, n_early)),
-        "weight_sum",
-        [shape((hidden_units, exp_dev, piece), F32)] * 3,
-        (at, *chip_pieces, own_narrow, other_narrow, early_x, grad_normed, router_grad),
+    grad_normed, router_grad, *grads = call(
+        functools.partial(finish_kernel, (n_chip, exp_dev, hidden_units, slots_each, n_early)),
+        "finish",
+        [shape((tokens_here, width), BF16), shape((experts, width), F32)]
+        + [shape((hidden_units, exp_dev, piece), F32)] * 3,
+        (at, *chip_pieces, own_narrow, other_narrow, early_x, *back),
         scalars=True,
-        behind=2,
     )
     grads = [jnp.transpose(g, (1, 0, 2)) for g in grads]
     return (grad_normed, router_grad.T, *grads)

time: 85.7 us -> 79.2 us (0.924)
  local copies, waits for them, and re-layouts: 7.52 us -> 0.35 us
  other arithmetic: 5.74 us -> 0.08 us
  Pallas kernels: 18.6 us -> 22.5 us
  starting transfers between devices: 20.9 us -> 24.3 us
    ppermute x8 -> x11, waiting for transfers between devices: 18.7 us -> 11.8 us  [over_expert(): return lax.ppermute(value, 'expert', [(i, i ^ k) for i in range(n_expert)])]
    ppermute x5, waiting for transfers between devices: 9.02 us -> 15.8 us  [over_chip(): return lax.ppermute(value, 'dp', [(i, i ^ 2 * k) for i in range(n_dp)])]
    unnamed x16 -> x10, local copies, waits for them, and re-layouts: 5.64 us -> 0.33 us
    ppermute x8 -> x11, starting transfers between devices: 9.84 us -> 14.5 us  [over_expert(): return lax.ppermute(value, 'expert', [(i, i ^ k) for i in range(n_expert)])]
    pallas_call x7 -> x11, Pallas kernels: 12.1 us -> 15.1 us  [call(): pl.pallas_call(kernel, out_shape=outs, in_specs=specs, out_specs=[pl.Bloc...]
    select_n x1 -> x0, other arithmetic: 2.01 us -> none  [sum_chips(): jnp.where(core == 0, jnp.concatenate([total, other], axis=1), jnp.concate...]
    convert_element_type x4 -> x0, other arithmetic: 1.95 us -> none  [the longest x2 1.9 us: sum_chips(): total = total + over_chip(total.astype(BF16), 1 << k).astype(F32)]
    ppermute x5, starting transfers between devices: 7.34 us -> 5.45 us  [over_chip(): return lax.ppermute(value, 'dp', [(i, i ^ 2 * k) for i in range(n_dp)])]
  transfers between devices with their start and end apart: 17 -> 20, of which waited for: 9 -> 10; matrix products, arithmetic and copies ran while one was open for 8% -> 0% of each run, Pallas kernels for 13% -> 17%
where the time goes in v3:
time: 79.2 us; the launch traced here: 78.9 us
  waiting for transfers between devices  30.8 us (39%)
  starting transfers between devices  24.3 us (31%)
  Pallas kernels  22.5 us (28%)
    ppermute x5, waiting for transfers between devices, over_chip(): return lax.ppermute(value, 'dp', [(i, i ^ 2 * k) for i in range(n_dp)])  15.8 us
    pallas_call x11, Pallas kernels, call(): pl.pallas_call(kernel, out_shape=outs, in_specs=specs, out_specs=[pl.Bloc...  15.1 us
    ppermute x11, starting transfers between devices, over_expert(): return lax.ppermute(value, 'expert', [(i, i ^ k) for i in range(n_expert)])  14.5 us
    ppermute x11, waiting for transfers between devices, over_expert(): return lax.ppermute(value, 'expert', [(i, i ^ k) for i in range(n_expert)])  11.8 us
    ppermute x5, starting transfers between devices, over_chip(): return lax.ppermute(value, 'dp', [(i, i ^ 2 * k) for i in range(n_dp)])  5.45 us
    pallas_call x1, Pallas kernels, on_device(): pl.pallas_call(functools.partial(prepare_kernel, n_early, blocks), out_sh...  5.16 us
    all_to_all x1, starting transfers between devices, way_back(): back_rows = lax.all_to_all(row_pieces, 'expert', 0, 0, tiled=True)  4.34 us
    ppermute x3, waiting for transfers between devices, over_core(): return lax.ppermute(value, 'dp', [(i, i ^ 1) for i in range(n_dp)])  3.22 us
  transfers between devices with their start and end apart: 20, of which 10 were waited for; matrix products, arithmetic and copies ran while one was open for 0% of the time, Pallas kernels for 17%

profile of v3, /device:TPU:0, one launch (start us, length us, event | category | flops | bytes accessed | tf_op | source)
XLA Modules:
  0.0 78.9 jit_solution(15495275560509228768)
XLA Ops:
  0.6 2.3 %route.1 = (bf16[32,3072]{1,0:T(8,128)(2,1)S(1)}, bf16[32,3200]{1,0:T(8,128)(2,1)}) custom-call(s32[4,32]{1,0:T(4,128)} %bitcast.23, bf16[32,6144]{1,0:T(8,128)(2,1)} %refs_1_.1, bf16[16,6144]{1,0:T(8,128)(2,1)} %bitcast.21, bf16[32,6144]{1,0:T(8,128)(2,1)} %refs_3_.1), custom_call_target="tpu_custom_call" | custom-call | tf_op jit(solution)/shard_map/route/pallas_call | solution.py:365
  2.9 3.0 %collective-permute-start.10 = (bf16[32,3200]{1,0:T(8,128)(2,1)}, bf16[32,3200]{1,0:T(8,128)(2,1)S(1)}, u32[]{:S(2)}, u32[]{:S(2)}) collective-permute-start(bf16[32,3200]{1,0:T(8,128)(2,1)} %get-tuple-element.86.refs_4_), channel_id=1, source_target_pairs={{0,2},{1,3},{2,0},{3,1},{4,6},{5,7},{6,4},{7,5},{8,10},{9,11},{10,... | collective-permute-start | bytes 614408 | tf_op jit(solution)/shard_map/ppermute | solution.py:336
  6.0 1.5 %collective-permute-start.6 = (bf16[32,3072]{1,0:T(8,128)(2,1)S(1)}, bf16[32,3072]{1,0:T(8,128)(2,1)S(1)}, u32[]{:S(2)}, u32[]{:S(2)}) collective-permute-start(bf16[32,3072]{1,0:T(8,128)(2,1)S(1)} %get-tuple-element.85.refs_0_), channel_id=1, source_target_pairs={{0,1},{1,0},{2,3},{3,2},{4,5},{5,4},{6,7},{7,6},{8,9},{9,8},{10,11... | collective-permute-start | bytes 589832 | tf_op jit(solution)/shard_map/ppermute | solution.py:336
  8.0 3.3 %collective-permute-done.10.refs_6_ = bf16[32,3200]{1,0:T(8,128)(2,1)S(1)} collective-permute-done((bf16[32,3200]{1,0:T(8,128)(2,1)}, bf16[32,3200]{1,0:T(8,128)(2,1)S(1)}, u32[]{:S(2)}, u32[]{:S(2)}) %collective-permute-start.10) | collective-permute-done | bytes 204832 | tf_op jit(solution)/shard_map/ppermute | solution.py:336
  11.2 1.7 %collective-permute-start.11 = (bf16[32,3200]{1,0:T(8,128)(2,1)S(1)}, bf16[32,3200]{1,0:T(8,128)(2,1)S(1)}, u32[]{:S(2)}, u32[]{:S(2)}) collective-permute-start(bf16[32,3200]{1,0:T(8,128)(2,1)S(1)} %collective-permute-done.10.refs_6_), channel_id=1, source_target_pairs={{0,1},{1,0},{2,3},{3,2},{4,5},{5,4},{6,7},{7,6},{8,9},{9,8},{10,11... | collective-permute-start | bytes 614408 | tf_op jit(solution)/shard_map/ppermute | solution.py:336
  12.9 1.5 %collective-permute-start.7 = (bf16[32,3072]{1,0:T(8,128)(2,1)S(1)}, bf16[32,3072]{1,0:T(8,128)(2,1)S(1)}, u32[]{:S(2)}, u32[]{:S(2)}) collective-permute-start(bf16[32,3072]{1,0:T(8,128)(2,1)S(1)} %get-tuple-element.85.refs_0_), channel_id=1, source_target_pairs={{0,2},{1,3},{2,0},{3,1},{4,6},{5,7},{6,4},{7,5},{8,10},{9,11},{10,... | collective-permute-start | bytes 589832 | tf_op jit(solution)/shard_map/ppermute | solution.py:336
  15.0 5.2 %prepare.1 = (bf16[144,6144]{1,0:T(8,128)(2,1)S(1)}, bf16[80,6144]{1,0:T(8,128)(2,1)}, bf16[80,6144]{1,0:T(8,128)(2,1)}, bf16[80,6144]{1,0:T(8,128)(2,1)S(1)}, f...) custom-call(bf16[36,4,6144]{2,1,0:T(4,128)(2,1)} %bitcast.17, bf16[20,4,6144]{2,1,0:T(4,128)(2,1)} %bitcast.18, ...), custom_call_target="tpu_custom_call" | custom-call | tf_op jit(solution)/shard_map/prepare/pallas_call | solution.py:399
  20.6 2.1 %collective-permute-done.8.refs_3_ = bf16[32,3072]{1,0:T(8,128)(2,1)S(1)} collective-permute-done((bf16[32,3072]{1,0:T(8,128)(2,1)S(1)}, bf16[32,3072]{1,0:T(8,128)(2,1)S(1)}, u32[]{:S(2)}, u32[]{:S(2)}) %collective-permute-start.8) | collective-permute-done | bytes 196640 | tf_op jit(solution)/shard_map/ppermute | solution.py:336
  22.7 3.8 %experts.1 = (f32[32,128]{1,0:T(8,128)}, f32[32,128]{1,0:T(8,128)S(1)}, f32[32,128]{1,0:T(8,128)S(1)}, f32[32,128]{1,0:T(8,128)S(1)}, bf16[128,80]{1,0:T(8,128)(...) custom-call(s32[3]{0:T(128)S(1)} %pad_add_fusion.at, ...), custom_call_target="tpu_custom_call" | custom-call | tf_op jit(solution)/shard_map/experts/pallas_call | solution.py:353
  26.4 0.6 collective-permute-start.13
  27.1 1.4 %collective-permute-start.14 = (f32[32,128]{1,0:T(8,128)S(1)}, f32[32,128]{1,0:T(8,128)S(1)}, u32[]{:S(2)}, u32[]{:S(2)}) collective-permute-start(f32[32,128]{1,0:T(8,128)S(1)} %get-tuple-element.97), channel_id=1, source_target_pairs={{0,2},{1,3},{2,0},{3,1},{4,6},{5,7},{6,4},{7,5},{8,10},{9,11},{10,... | collective-permute-start | bytes 49160 | tf_op jit(solution)/shard_map/ppermute | solution.py:336
  28.5 1.4 %collective-permute-start.15 = (f32[32,128]{1,0:T(8,128)S(1)}, f32[32,128]{1,0:T(8,128)S(1)}, u32[]{:S(2)}, u32[]{:S(2)}) collective-permute-start(f32[32,128]{1,0:T(8,128)S(1)} %get-tuple-element.98), channel_id=1, source_target_pairs={{0,3},{1,2},{2,1},{3,0},{4,7},{5,6},{6,5},{7,4},{8,11},{9,10},{10,... | collective-permute-start | bytes 49160 | tf_op jit(solution)/shard_map/ppermute | solution.py:336
  29.9 1.1 %weight_terms.1.mine = f32[4,240,768]{2,1,0:T(8,128)S(1)} custom-call(s32[3]{0:T(128)S(1)} %pad_add_fusion.at, bf16[128,6144]{1,0:T(8,128)(2,1)S(1)} %get-tuple-element.91.arrived, bf16[144,6144]{1,0:T(8,128)(2,1)S(1)} %get-tuple-element.90.refs_11_.inputs, bf16[160,144]{1,0:T(8,128)(2,1)S(1)} %get-tuple-element.92.late, ...), custom_call_target="tpu_custom_call" | custom-call | tf_op jit(solution)/shard_map/weight_terms/pallas_call | solution.py:353
  31.1 2.1 %collective-permute-done.15.refs_2_ = f32[32,128]{1,0:T(8,128)S(1)} collective-permute-done((f32[32,128]{1,0:T(8,128)S(1)}, f32[32,128]{1,0:T(8,128)S(1)}, u32[]{:S(2)}, u32[]{:S(2)}) %collective-permute-start.15) | collective-permute-done | bytes 16416 | tf_op jit(solution)/shard_map/ppermute | solution.py:336
  33.7 1.6 %collective-permute-start.16 = (bf16[240,768]{1,0:T(8,128)(2,1)S(1)}, bf16[240,768]{1,0:T(8,128)(2,1)S(1)}, u32[]{:S(2)}, u32[]{:S(2)}) collective-permute-start(bf16[240,768]{1,0:T(8,128)(2,1)S(1)} %get-tuple-element.100), channel_id=1, source_target_pairs={{0,8},{4,12},{8,0},{12,4},{16,24},{20,28},{24,16},{28,20},{1,9},{5... | collective-permute-start | bytes 1105928 | tf_op jit(solution)/shard_map/ppermute | solution.py:342
  35.3 2.6 %collective-permute-start.17 = (bf16[240,768]{1,0:T(8,128)(2,1)S(1)}, bf16[240,768]{1,0:T(8,128)(2,1)S(1)}, u32[]{:S(2)}, u32[]{:S(2)}) collective-permute-start(bf16[240,768]{1,0:T(8,128)(2,1)S(1)} %get-tuple-element.101), channel_id=1, source_target_pairs={{0,16},{4,20},{8,24},{12,28},{16,0},{20,4},{24,8},{28,12},{1,17},{... | collective-permute-start | bytes 1105928 | tf_op jit(solution)/shard_map/ppermute | solution.py:342
  38.1 37.6 %conditional.2 = (f32[16,3072]{1,0:T(8,128)}, f32[16,3072]{1,0:T(8,128)}, f32[32,6144]{1,0:T(8,128)}, bf16[4,32,6144]{2,1,0:T(8,128)(2,1)}) conditional(s32[]{:T(128)} %convert_element_type.6, () %tuple.26, (pred[]{:T(512)}, s32[3]{0:T(128)S(1)}, f32[32,128]{1,0:T(8,128)}, f32[32,128]{1,0:T(8,128)}, f32[32,128]{1,0:T(8,128)}, ...), branch_computations={%region_0.0_spmd, %region_1.0_spmd} | conditional | flops 1 | bytes 11960729 | solution.py:502
  38.1 2.7 %router_terms.1 = (f32[16,3072]{1,0:T(8,128)S(1)}, f32[16,3072]{1,0:T(8,128)S(1)}, f32[32,6144]{1,0:T(8,128)}) custom-call(s32[3]{0:T(128)S(1)} %get-tuple-element.28.at, f32[32,128]{1,0:T(8,128)} %get-tuple-element.33.refs_0_, f32[32,128]{1,0:T(8,128)} %get-tuple-element.34.refs_1_, f32[32,128]{1,0:T(8,128)} %get-tuple-element.35.refs_2_, ...), custom_call_target="tpu_custom_call" | custom-call | tf_op jit(solution)/shard_map/cond/branch_1_fun/router_terms/pallas_call | solution.py:353
  40.9 1.4 %collective-permute-done.3.refs_1_ = f32[16,3072]{1,0:T(8,128)S(1)} collective-permute-done((f32[16,3072]{1,0:T(8,128)S(1)}, f32[16,3072]{1,0:T(8,128)S(1)}, u32[]{:S(2)}, u32[]{:S(2)}) %collective-permute-start.3) | collective-permute-done | bytes 196640 | tf_op jit(solution)/shard_map/cond/branch_1_fun/ppermute | solution.py:339
  42.3 1.6 %collective-permute-start.4 = (bf16[16,3072]{1,0:T(8,128)(2,1)S(1)}, bf16[16,3072]{1,0:T(8,128)(2,1)S(1)}, u32[]{:S(2)}, u32[]{:S(2)}) collective-permute-start(bf16[16,3072]{1,0:T(8,128)(2,1)S(1)} %add_terms.7.refs_0_), channel_id=1, source_target_pairs={{0,1},{1,0},{2,3},{3,2},{4,5},{5,4},{6,7},{7,6},{8,9},{9,8},{10,11... | collective-permute-start | bytes 294920 | tf_op jit(solution)/shard_map/cond/branch_1_fun/ppermute | solution.py:336
  43.9 3.4 %collective-permute-done.4.refs_1_ = bf16[16,3072]{1,0:T(8,128)(2,1)S(1)} collective-permute-done((bf16[16,3072]{1,0:T(8,128)(2,1)S(1)}, bf16[16,3072]{1,0:T(8,128)(2,1)S(1)}, u32[]{:S(2)}, u32[]{:S(2)}) %collective-permute-start.4) | collective-permute-done | bytes 98336 | tf_op jit(solution)/shard_map/cond/branch_1_fun/ppermute | solution.py:336
  47.2 0.7 collective-permute-start.5
  47.9 3.4 %row_terms.1.refs_2_ = bf16[4,32,6144]{2,1,0:T(8,128)(2,1)} custom-call(s32[3]{0:T(128)S(1)} %get-tuple-element.28.at, bf16[128,80]{1,0:T(8,128)(2,1)S(1)} %copy-done.6, bf16[128,80]{1,0:T(8,128)(2,1)S(1)} %copy-done.7, bf16[80,6144]{1,0:T(8,128)(2,1)S(1)} %copy-done.1, bf16[80,6144]{1,0:T(8,128)(2,1)} %get-tuple-element.32.up, ...), custom_call_target="tpu_custom_call" | custom-call | tf_op jit(solution)/shard_map/cond/branch_1_fun/row_terms/pallas_call | solution.py:353
  51.3 0.6 collective-permute-done.5.refs_1_
  52.0 4.3 %all-to-all-start = ((bf16[4,32,6144]{2,1,0:T(8,128)(2,1)}), bf16[4,32,6144]{2,1,0:T(8,128)(2,1)}, u32[]{:S(2)}, u32[]{:S(2)}) async-start(bf16[4,32,6144]{2,1,0:T(8,128)(2,1)} %row_terms.1.refs_2_), calls=%async_computation | async-start | bytes 3145728 | tf_op jit(solution)/shard_map/cond/branch_1_fun/all_to_all | solution.py:494
  56.3 19.4 %conditional = (f32[16,3072]{1,0:T(8,128)}, f32[16,3072]{1,0:T(8,128)}) conditional(s32[]{:T(128)} %convert_element_type.4, () %tuple.18, bf16[16,3072]{1,0:T(8,128)(2,1)S(1)} %add_terms.9), branch_computations={%region_2.0_spmd, %region_3.0_spmd} | conditional | bytes 1573000 | solution.py:495
  56.3 0.7 collective-permute-start
  57.1 7.3 %collective-permute-done.refs_1_ = bf16[16,3072]{1,0:T(8,128)(2,1)S(1)} collective-permute-done((bf16[16,3072]{1,0:T(8,128)(2,1)S(1)}, bf16[16,3072]{1,0:T(8,128)(2,1)S(1)}, u32[]{:S(2)}, u32[]{:S(2)}) %collective-permute-start) | collective-permute-done | bytes 98336 | tf_op jit(solution)/shard_map/cond/branch_1_fun/cond/branch_1_fun/ppermute | solution.py:342
  64.7 8.5 %collective-permute-done.1.refs_1_ = bf16[16,3072]{1,0:T(8,128)(2,1)S(1)} collective-permute-done((bf16[16,3072]{1,0:T(8,128)(2,1)S(1)}, bf16[16,3072]{1,0:T(8,128)(2,1)S(1)}, u32[]{:S(2)}, u32[]{:S(2)}) %collective-permute-start.1) | collective-permute-done | bytes 98336 | tf_op jit(solution)/shard_map/cond/branch_1_fun/cond/branch_1_fun/ppermute | solution.py:342
  73.2 0.7 add_terms.6
  73.9 1.8 %collective-permute-done.2 = f32[16,3072]{1,0:T(8,128)} collective-permute-done((f32[16,3072]{1,0:T(8,128)}, f32[16,3072]{1,0:T(8,128)}, u32[]{:S(2)}, u32[]{:S(2)}) %collective-permute-start.2) | collective-permute-done | bytes 196640 | tf_op jit(solution)/shard_map/cond/branch_1_fun/cond/branch_1_fun/ppermute | solution.py:339
  75.7 3.1 %finish.1 = (bf16[32,6144]{1,0:T(8,128)(2,1)}, f32[16,6144]{1,0:T(8,128)}, f32[20,4,768]{2,1,0:T(4,128)}, f32[20,4,768]{2,1,0:T(4,128)}, f32[20,4,768]{2,1,0:T(4,128)}) custom-call(s32[3]{0:T(128)S(1)} %pad_add_fusion.at, f32[240,768]{1,0:T(8,128)S(1)} %get-tuple-element.99.refs_0_, bf16[240,768]{1,0:T(8,128)(2,1)S(1)} %collective-permute-done.16.refs_1_, ...), custom_call_target="tpu_custom_call" | custom-call | tf_op jit(solution)/shard_map/finish/pallas_call | solution.py:353
  (41 shorter events, 2.7 us)
Async XLA Ops:
  2.9 8.3 %collective-permute-start.10 = (bf16[32,3200]{1,0:T(8,128)(2,1)}, bf16[32,3200]{1,0:T(8,128)(2,1)S(1)}, u32[]{:S(2)}, u32[]{:S(2)}) collective-permute-start(bf16[32,3200]{1,0:T(8,128)(2,1)} %get-tuple-element.86.refs_4_), channel_id=1, source_target_pairs={{0,2},{1,3},{2,0},{3,1},{4,6},{5,7},{6,4},{7,5},{8,10},{9,11},{10,... | collective-permute-start | bytes 614408 | tf_op jit(solution)/shard_map/ppermute | solution.py:336
  6.0 8.5 %collective-permute-start.6 = (bf16[32,3072]{1,0:T(8,128)(2,1)S(1)}, bf16[32,3072]{1,0:T(8,128)(2,1)S(1)}, u32[]{:S(2)}, u32[]{:S(2)}) collective-permute-start(bf16[32,3072]{1,0:T(8,128)(2,1)S(1)} %get-tuple-element.85.refs_0_), channel_id=1, source_target_pairs={{0,1},{1,0},{2,3},{3,2},{4,5},{5,4},{6,7},{7,6},{8,9},{9,8},{10,11... | collective-permute-start | bytes 589832 | tf_op jit(solution)/shard_map/ppermute | solution.py:336
  7.4 13.1 %collective-permute-start.9 = (bf16[32,3200]{1,0:T(8,128)(2,1)}, bf16[32,3200]{1,0:T(8,128)(2,1)S(1)}, u32[]{:S(2)}, u32[]{:S(2)}) collective-permute-start(bf16[32,3200]{1,0:T(8,128)(2,1)} %get-tuple-element.86.refs_4_), channel_id=1, source_target_pairs={{0,1},{1,0},{2,3},{3,2},{4,5},{5,4},{6,7},{7,6},{8,9},{9,8},{10,11... | collective-permute-start | bytes 614408 | tf_op jit(solution)/shard_map/ppermute | solution.py:336
  11.2 11.4 %collective-permute-start.11 = (bf16[32,3200]{1,0:T(8,128)(2,1)S(1)}, bf16[32,3200]{1,0:T(8,128)(2,1)S(1)}, u32[]{:S(2)}, u32[]{:S(2)}) collective-permute-start(bf16[32,3200]{1,0:T(8,128)(2,1)S(1)} %collective-permute-done.10.refs_6_), channel_id=1, source_target_pairs={{0,1},{1,0},{2,3},{3,2},{4,5},{5,4},{6,7},{7,6},{8,9},{9,8},{10,11... | collective-permute-start | bytes 614408 | tf_op jit(solution)/shard_map/ppermute | solution.py:336
  12.9 7.6 %collective-permute-start.7 = (bf16[32,3072]{1,0:T(8,128)(2,1)S(1)}, bf16[32,3072]{1,0:T(8,128)(2,1)S(1)}, u32[]{:S(2)}, u32[]{:S(2)}) collective-permute-start(bf16[32,3072]{1,0:T(8,128)(2,1)S(1)} %get-tuple-element.85.refs_0_), channel_id=1, source_target_pairs={{0,2},{1,3},{2,0},{3,1},{4,6},{5,7},{6,4},{7,5},{8,10},{9,11},{10,... | collective-permute-start | bytes 589832 | tf_op jit(solution)/shard_map/ppermute | solution.py:336
  14.5 8.2 %collective-permute-start.8 = (bf16[32,3072]{1,0:T(8,128)(2,1)S(1)}, bf16[32,3072]{1,0:T(8,128)(2,1)S(1)}, u32[]{:S(2)}, u32[]{:S(2)}) collective-permute-start(bf16[32,3072]{1,0:T(8,128)(2,1)S(1)} %collective-permute-done.6.refs_1_), channel_id=1, source_target_pairs={{0,2},{1,3},{2,0},{3,1},{4,6},{5,7},{6,4},{7,5},{8,10},{9,11},{10,... | collective-permute-start | bytes 589832 | tf_op jit(solution)/shard_map/ppermute | solution.py:336
  26.4 6.7 %collective-permute-start.12 = (bf16[4,240,768]{2,1,0:T(8,128)(2,1)S(1)}, bf16[4,240,768]{2,1,0:T(8,128)(2,1)S(1)}, u32[]{:S(2)}, u32[]{:S(2)}) collective-permute-start(bf16[4,240,768]{2,1,0:T(8,128)(2,1)S(1)} %get-tuple-element.94), channel_id=1, source_target_pairs={{0,4},{4,0},{8,12},{12,8},{16,20},{20,16},{24,28},{28,24},{1,5},{5... | collective-permute-start | bytes 4423688 | tf_op jit(solution)/shard_map/ppermute | solution.py:339
  26.4 4.6 %collective-permute-start.13 = (f32[32,128]{1,0:T(8,128)S(1)}, f32[32,128]{1,0:T(8,128)S(1)}, u32[]{:S(2)}, u32[]{:S(2)}) collective-permute-start(f32[32,128]{1,0:T(8,128)S(1)} %get-tuple-element.96), channel_id=1, source_target_pairs={{0,1},{1,0},{2,3},{3,2},{4,5},{5,4},{6,7},{7,6},{8,9},{9,8},{10,11... | collective-permute-start | bytes 49160 | tf_op jit(solution)/shard_map/ppermute | solution.py:336
  27.1 4.0 %collective-permute-start.14 = (f32[32,128]{1,0:T(8,128)S(1)}, f32[32,128]{1,0:T(8,128)S(1)}, u32[]{:S(2)}, u32[]{:S(2)}) collective-permute-start(f32[32,128]{1,0:T(8,128)S(1)} %get-tuple-element.97), channel_id=1, source_target_pairs={{0,2},{1,3},{2,0},{3,1},{4,6},{5,7},{6,4},{7,5},{8,10},{9,11},{10,... | collective-permute-start | bytes 49160 | tf_op jit(solution)/shard_map/ppermute | solution.py:336
  28.5 4.6 %collective-permute-start.15 = (f32[32,128]{1,0:T(8,128)S(1)}, f32[32,128]{1,0:T(8,128)S(1)}, u32[]{:S(2)}, u32[]{:S(2)}) collective-permute-start(f32[32,128]{1,0:T(8,128)S(1)} %get-tuple-element.98), channel_id=1, source_target_pairs={{0,3},{1,2},{2,1},{3,0},{4,7},{5,6},{6,5},{7,4},{8,11},{9,10},{10,... | collective-permute-start | bytes 49160 | tf_op jit(solution)/shard_map/ppermute | solution.py:336
  31.0 2.4 %copy-start.3 = (f32[32,128]{1,0:T(8,128)}, f32[32,128]{1,0:T(8,128)S(1)}, u32[]{:S(2)}) copy-start(f32[32,128]{1,0:T(8,128)S(1)} %collective-permute-done.13.refs_0_) | copy-start | bytes 49156
  31.1 2.4 %copy-start.4 = (f32[32,128]{1,0:T(8,128)}, f32[32,128]{1,0:T(8,128)S(1)}, u32[]{:S(2)}) copy-start(f32[32,128]{1,0:T(8,128)S(1)} %collective-permute-done.14.refs_1_) | copy-start | bytes 49156
  33.1 0.6 copy-start.5
  33.1 5.0 %copy-start = (bf16[32,6144]{1,0:T(8,128)(2,1)S(1)}, bf16[32,6144]{1,0:T(8,128)(2,1)}, u32[]{:S(2)}) copy-start(bf16[32,6144]{1,0:T(8,128)(2,1)} %refs_1_.1) | copy-start | bytes 1179652
  33.1 5.0 %copy-start.2 = (bf16[6144,16]{0,1:T(8,128)(2,1)S(1)}, bf16[6144,16]{0,1:T(8,128)(2,1)}, u32[]{:S(2)}) copy-start(bf16[6144,16]{0,1:T(8,128)(2,1)} %param.15) | copy-start | bytes 589828
  33.7 42.0 %collective-permute-start.16 = (bf16[240,768]{1,0:T(8,128)(2,1)S(1)}, bf16[240,768]{1,0:T(8,128)(2,1)S(1)}, u32[]{:S(2)}, u32[]{:S(2)}) collective-permute-start(bf16[240,768]{1,0:T(8,128)(2,1)S(1)} %get-tuple-element.100), channel_id=1, source_target_pairs={{0,8},{4,12},{8,0},{12,4},{16,24},{20,28},{24,16},{28,20},{1,9},{5... | collective-permute-start | bytes 1105928 | tf_op jit(solution)/shard_map/ppermute | solution.py:342
  35.3 40.4 %collective-permute-start.17 = (bf16[240,768]{1,0:T(8,128)(2,1)S(1)}, bf16[240,768]{1,0:T(8,128)(2,1)S(1)}, u32[]{:S(2)}, u32[]{:S(2)}) collective-permute-start(bf16[240,768]{1,0:T(8,128)(2,1)S(1)} %get-tuple-element.101), channel_id=1, source_target_pairs={{0,16},{4,20},{8,24},{12,28},{16,0},{20,4},{24,8},{28,12},{1,17},{... | collective-permute-start | bytes 1105928 | tf_op jit(solution)/shard_map/ppermute | solution.py:342
  37.9 37.8 %collective-permute-start.18 = (bf16[240,768]{1,0:T(8,128)(2,1)S(1)}, bf16[240,768]{1,0:T(8,128)(2,1)S(1)}, u32[]{:S(2)}, u32[]{:S(2)}) collective-permute-start(bf16[240,768]{1,0:T(8,128)(2,1)S(1)} %get-tuple-element.102), channel_id=1, source_target_pairs={{0,24},{4,28},{8,16},{12,20},{16,8},{20,12},{24,0},{28,4},{1,25},{... | collective-permute-start | bytes 1105928 | tf_op jit(solution)/shard_map/ppermute | solution.py:342
  38.1 9.8 %copy-start.1 = (bf16[80,6144]{1,0:T(8,128)(2,1)S(1)}, bf16[80,6144]{1,0:T(8,128)(2,1)}, u32[]{:S(2)}) copy-start(bf16[80,6144]{1,0:T(8,128)(2,1)} %get-tuple-element.31.gate) | copy-start | bytes 2949124 | tf_op jit(solution)/shard_map/cond
  38.1 9.8 %copy-start.6 = (bf16[128,80]{1,0:T(8,128)(2,1)S(1)}, bf16[128,80]{1,0:T(8,128)(2,1)}, u32[]{:S(2)}) copy-start(bf16[128,80]{1,0:T(8,128)(2,1)} %get-tuple-element.29.tok_gate) | copy-start | bytes 61444 | tf_op jit(solution)/shard_map/cond
  38.1 9.8 %copy-start.7 = (bf16[128,80]{1,0:T(8,128)(2,1)S(1)}, bf16[128,80]{1,0:T(8,128)(2,1)}, u32[]{:S(2)}) copy-start(bf16[128,80]{1,0:T(8,128)(2,1)} %get-tuple-element.30.tok_up) | copy-start | bytes 61444 | tf_op jit(solution)/shard_map/cond
  40.8 1.4 %collective-permute-start.3 = (f32[16,3072]{1,0:T(8,128)S(1)}, f32[16,3072]{1,0:T(8,128)S(1)}, u32[]{:S(2)}, u32[]{:S(2)}) collective-permute-start(f32[16,3072]{1,0:T(8,128)S(1)} %get-tuple-element.40.behind), channel_id=1, source_target_pairs={{0,4},{4,0},{8,12},{12,8},{16,20},{20,16},{24,28},{28,24},{1,5},{5... | collective-permute-start | bytes 589832 | tf_op jit(solution)/shard_map/cond/branch_1_fun/ppermute | solution.py:339
  42.3 4.9 %collective-permute-start.4 = (bf16[16,3072]{1,0:T(8,128)(2,1)S(1)}, bf16[16,3072]{1,0:T(8,128)(2,1)S(1)}, u32[]{:S(2)}, u32[]{:S(2)}) collective-permute-start(bf16[16,3072]{1,0:T(8,128)(2,1)S(1)} %add_terms.7.refs_0_), channel_id=1, source_target_pairs={{0,1},{1,0},{2,3},{3,2},{4,5},{5,4},{6,7},{7,6},{8,9},{9,8},{10,11... | collective-permute-start | bytes 294920 | tf_op jit(solution)/shard_map/cond/branch_1_fun/ppermute | solution.py:336
  47.2 4.7 %collective-permute-start.5 = (bf16[16,3072]{1,0:T(8,128)(2,1)S(1)}, bf16[16,3072]{1,0:T(8,128)(2,1)S(1)}, u32[]{:S(2)}, u32[]{:S(2)}) collective-permute-start(bf16[16,3072]{1,0:T(8,128)(2,1)S(1)} %add_terms.8.refs_0_), channel_id=1, source_target_pairs={{0,2},{1,3},{2,0},{3,1},{4,6},{5,7},{6,4},{7,5},{8,10},{9,11},{10,... | collective-permute-start | bytes 294920 | tf_op jit(solution)/shard_map/cond/branch_1_fun/ppermute | solution.py:336
  52.0 23.7 %all-to-all-start = ((bf16[4,32,6144]{2,1,0:T(8,128)(2,1)}), bf16[4,32,6144]{2,1,0:T(8,128)(2,1)}, u32[]{:S(2)}, u32[]{:S(2)}) async-start(bf16[4,32,6144]{2,1,0:T(8,128)(2,1)} %row_terms.1.refs_2_), calls=%async_computation | async-start | bytes 3145728 | tf_op jit(solution)/shard_map/cond/branch_1_fun/all_to_all | solution.py:494
  56.3 8.0 %collective-permute-start = (bf16[16,3072]{1,0:T(8,128)(2,1)S(1)}, bf16[16,3072]{1,0:T(8,128)(2,1)S(1)}, u32[]{:S(2)}, u32[]{:S(2)}) collective-permute-start(bf16[16,3072]{1,0:T(8,128)(2,1)S(1)} %refs_0_), channel_id=1, source_target_pairs={{0,8},{4,12},{8,0},{12,4},{16,24},{20,28},{24,16},{28,20},{1,9},{5... | collective-permute-start | bytes 294920 | tf_op jit(solution)/shard_map/cond/branch_1_fun/cond/branch_1_fun/ppermute | solution.py:342
  64.4 8.8 %collective-permute-start.1 = (bf16[16,3072]{1,0:T(8,128)(2,1)S(1)}, bf16[16,3072]{1,0:T(8,128)(2,1)S(1)}, u32[]{:S(2)}, u32[]{:S(2)}) collective-permute-start(bf16[16,3072]{1,0:T(8,128)(2,1)S(1)} %add_terms.5.refs_0_), channel_id=1, source_target_pairs={{0,16},{4,20},{8,24},{12,28},{16,0},{20,4},{24,8},{28,12},{1,17},{... | collective-permute-start | bytes 294920 | tf_op jit(solution)/shard_map/cond/branch_1_fun/cond/branch_1_fun/ppermute | solution.py:342
  73.9 1.8 %collective-permute-start.2 = (f32[16,3072]{1,0:T(8,128)}, f32[16,3072]{1,0:T(8,128)}, u32[]{:S(2)}, u32[]{:S(2)}) collective-permute-start(f32[16,3072]{1,0:T(8,128)} %add_terms.6), channel_id=1, source_target_pairs={{0,4},{4,0},{8,12},{12,8},{16,20},{20,16},{24,28},{28,24},{1,5},{5... | collective-permute-start | bytes 589832 | tf_op jit(solution)/shard_map/cond/branch_1_fun/cond/branch_1_fun/ppermute | solution.py:339

commit v4 on v3

v4 whole, which is shorter than its diff:
```python
import functools

import jax
import jax.numpy as jnp
from jax import lax
from jax.experimental import pallas as pl
from jax.experimental.pallas import tpu as pltpu
from jax.sharding import PartitionSpec as P

F32 = jnp.float32
BF16 = jnp.bfloat16
LANES = 128
VMEM_BYTES = 16 * 2**20


def dot(left, right, contract):
    return lax.dot_general(
        left,
        right,
        ((contract[:1], contract[1:]), ((), ())),
        preferred_element_type=F32,
    )


def iota(shape, dim):
    return lax.broadcasted_iota(jnp.int32, shape, dim)


def split_high_low(value):
    high = value.astype(BF16)
    return high, (value - high.astype(F32)).astype(BF16)


def route_kernel(experts, *refs):
    sources, (first, packed, ids, normed, router, upstream, sems) = refs[:4], refs[4:]
    tokens, width = normed.shape
    half = width // 2
    copies = [
        pltpu.make_async_copy(source, target, sems.at[k])
        for k, (source, target) in enumerate(zip(sources, (ids, normed, router, upstream)))
    ]
    for copy in copies:
        copy.start()
    copies[0].wait()
    expert = iota((experts, tokens), 0)
    named_t = expert < 0
    for k in range(ids.shape[0]):
        named_t = named_t | (ids[k : k + 1, :] == expert)
    unit = (iota((tokens, tokens), 0) == iota((tokens, tokens), 1)).astype(F32).astype(BF16)
    named_f = dot(unit, named_t.astype(F32).astype(BF16), (1, 1))
    named = named_f > 0.5
    earlier = (iota((tokens, tokens), 1) < iota((tokens, tokens), 0)).astype(F32).astype(BF16)
    slot = dot(earlier, named_f.astype(BF16), (1, 0))
    code = jnp.where(named, slot + 1.0, 0.0)
    copies[1].wait()
    copies[2].wait()
    logits = dot(normed[...], router[...], (1, 1))
    largest = jnp.max(jnp.where(named, logits, -jnp.inf), axis=1, keepdims=True)
    weight = jnp.where(named, jnp.exp(jnp.where(named, logits - largest, 0.0)), 0.0)
    weight = weight / jnp.sum(weight, axis=1, keepdims=True)
    high = weight.astype(BF16).astype(F32)
    middle = (weight - high).astype(BF16).astype(F32)
    low = weight - high - middle
    rest = jnp.zeros((tokens, LANES - 4 * experts), F32)
    packed[:, half:] = jnp.concatenate([high, middle, low, code, rest], axis=1).astype(BF16)
    copies[3].wait()
    first[...] = upstream[:, :half]
    packed[:, :half] = upstream[:, half:]


def prepare_kernel(blocks, *refs):
    sources, refs = refs[:4], refs[4:]
    scratch, sems, refs = refs[-5:-1], refs[-1], refs[:-5]
    inputs, gate_rows, up_rows, down_rows, pre_gate, pre_up = refs
    step = inputs.shape[1] // blocks
    copies = []
    for j in range(blocks):
        lanes = pl.ds(j * step, step)
        for k in range(4):
            copy = pltpu.make_async_copy(sources[k].at[:, :, lanes], scratch[k].at[:, :, lanes], sems.at[4 * j + k])
            copy.start()
            copies.append(copy)
    pre_gate[...] = jnp.zeros_like(pre_gate)
    pre_up[...] = jnp.zeros_like(pre_up)
    for j in range(blocks):
        lanes = slice(j * step, (j + 1) * step)
        for k, target in enumerate((inputs, gate_rows, up_rows, down_rows)):
            copies[4 * j + k].wait()
            target[:, lanes] = scratch[k][:, :, lanes].reshape(target.shape[0], step)
        pre_gate[...] += dot(inputs[:, lanes], gate_rows[:, lanes], (1, 1))
        pre_up[...] += dot(inputs[:, lanes], up_rows[:, lanes], (1, 1))


def pick(expert_of_column, experts, groups, columns):
    lane = iota((LANES, columns), 0)
    out = lane < 0
    for g in groups:
        out = out | (lane == expert_of_column + g * experts)
    return out.astype(F32).astype(BF16)


def block_terms(turned, inputs, arrived, start, piece):
    gate, up, hidden = turned
    at = pl.ds(pl.multiple_of(start, LANES), piece)
    return [dot(gate, inputs[:, at], (1, 0)), dot(up, inputs[:, at], (1, 0)), dot(hidden, arrived[:, at], (1, 0))]


def expert_kernel(sizes, at, *refs):
    n_expert, exp_dev, capacity, tokens_here = sizes
    firsts, seconds, rest = refs[:n_expert], refs[n_expert : 2 * n_expert], refs[2 * n_expert :]
    down, pre_gate, pre_up = rest[:3]
    scores = rest[3 : 3 + n_expert]
    place, slot_gate, slot_up, slot_hidden, arrived = rest[3 + n_expert :]
    me = at[0]
    experts = exp_dev * n_expert
    tokens = tokens_here * n_expert
    hidden_all, width = down.shape
    half = width // 2
    slots = exp_dev * capacity * n_expert
    packed = jnp.concatenate([u[:, half:] for u in seconds], axis=0)
    for r in range(n_expert):
        rows = slice(r * tokens_here, (r + 1) * tokens_here)
        arrived[rows, :half] = firsts[r][...]
        arrived[rows, half:] = seconds[r][:, :half]
    grad_hidden_raw = dot(arrived[...], down[...], (1, 1))

    expert_of_hidden = me * exp_dev + iota((LANES, hidden_all), 1) % exp_dev
    weight_hidden = dot(packed, pick(expert_of_hidden, experts, (0, 1, 2), hidden_all), (1, 0))
    expert_of_slot = me * exp_dev + iota((LANES, slots), 1) // (capacity * n_expert)
    code_at = dot(packed, pick(expert_of_slot, experts, (3,), slots), (1, 0))
    column = iota((tokens, slots), 1)
    source = me ^ (iota((tokens, slots), 0) // tokens_here)
    slot_code = ((column // n_expert) % capacity + 1).astype(F32)
    chosen = (source == column % n_expert) & (jnp.abs(code_at - slot_code) < 0.5)
    placed = chosen.astype(F32).astype(BF16)
    place[...] = placed

    high, low = split_high_low(grad_hidden_raw * weight_hidden)
    grad_hidden = dot(placed, high, (0, 0)) + dot(placed, low, (0, 0))
    same = iota((slots, hidden_all), 1) % exp_dev == iota((slots, hidden_all), 0) // (capacity * n_expert)
    v = pre_gate[...]
    logistic = jax.nn.sigmoid(v)
    activated = v * logistic
    hidden = jnp.where(same, activated * pre_up[...], 0.0).astype(BF16)
    slope = logistic * (1.0 + v * (1.0 - logistic))
    slot_hidden[...] = hidden
    slot_gate[...] = jnp.where(same, grad_hidden * pre_up[...] * slope, 0.0).astype(BF16)
    slot_up[...] = jnp.where(same, grad_hidden * activated, 0.0).astype(BF16)
    score = jnp.sum(hidden.astype(F32) * grad_hidden, axis=1, keepdims=True)
    expert_of_row = me * exp_dev + iota((slots, LANES), 0) // (capacity * n_expert)
    score = jnp.where(iota((slots, LANES), 1) == expert_of_row, score, 0.0)
    high, low = split_high_low(score)
    picked = dot(placed, high, (1, 0)) + dot(placed, low, (1, 0))
    for r in range(n_expert):
        scores[r][...] = picked[r * tokens_here : (r + 1) * tokens_here]


def core_kernel(sizes, at, *refs):
    n_expert, exp_dev, n_chip, piece, even = sizes
    seconds, rest = refs[:n_expert], refs[n_expert:]
    place, slot_gate, slot_up, slot_hidden, arrived, inputs = rest[:6]
    tok_gate, tok_up, turned_gate, turned_up, turned_hidden = rest[6:11]
    me, chip, core = at[0], at[1], at[2]
    experts = exp_dev * n_expert
    hidden_all = slot_gate.shape[1]
    hidden_units = hidden_all // exp_dev
    half = arrived.shape[1] // 2
    packed = jnp.concatenate([u[:, half:] for u in seconds], axis=0)
    expert_of_hidden = me * exp_dev + iota((LANES, hidden_all), 1) % exp_dev
    weight_hidden = dot(packed, pick(expert_of_hidden, experts, (0, 1, 2), hidden_all), (1, 0))
    scaled_hidden = (dot(place[...], slot_hidden[...], (1, 0)) * weight_hidden).astype(BF16)
    row, column = iota((hidden_all, hidden_all), 0), iota((hidden_all, hidden_all), 1)
    order = row == (column % exp_dev) * hidden_units + column // exp_dev
    order = order.astype(F32).astype(BF16)
    turned = [dot(order, value, (1, 1)).astype(BF16) for value in (slot_gate[...], slot_up[...], scaled_hidden)]
    turned_gate[...], turned_up[...], turned_hidden[...] = turned
    if even:
        theirs = rest[11]
        for r in range(n_chip):
            terms = block_terms(turned, inputs, arrived, (2 * (chip ^ r) + 1 - core) * piece, piece)
            for k in range(3):
                theirs[r, k * hidden_all : (k + 1) * hidden_all] = terms[k].astype(BF16)
    tok_gate[...] = dot(place[...], slot_gate[...], (1, 0)).astype(BF16)
    tok_up[...] = dot(place[...], slot_up[...], (1, 0)).astype(BF16)


def weight_kernel(sizes, at, arrived, inputs, gate, up, hidden, mine):
    n_chip, piece = sizes
    chip, core = at[1], at[2]
    n = gate.shape[0]
    for r in range(n_chip):
        start = (2 * (chip ^ r) + core) * piece
        terms = block_terms((gate[...], up[...], hidden[...]), inputs, arrived, start, piece)
        for k in range(3):
            mine[r, k * n : (k + 1) * n] = terms[k]


def add_kernel(mine, theirs, *outs):
    for r in range(len(outs)):
        outs[r][...] = (mine[r] + theirs[r].astype(F32)).astype(outs[r].dtype)


def row_kernel(n_expert, blocks, at, tok_gate, tok_up, gate, up, behind, out):
    del behind
    size = tok_gate.shape[0] // n_expert
    step = gate.shape[1] // blocks
    for j in range(blocks):
        lanes = slice(j * step, (j + 1) * step)
        total = dot(tok_gate[...], gate[:, lanes], (1, 0)) + dot(tok_up[...], up[:, lanes], (1, 0))
        for r in range(n_expert):
            out[at[0] ^ r, :, lanes] = total[r * size : (r + 1) * size].astype(out.dtype)


def router_kernel(experts, n_expert, at, *refs):
    scores, (packed, normed, router, other, own, through) = refs[:n_expert], refs[n_expert:]
    picked = scores[0][...]
    for s in scores[1:]:
        picked = picked + s[...]
    picked = picked[:, :experts]
    half = normed.shape[1] // 2
    tail = packed[:, half:].astype(F32)
    weight = tail[:, :experts] + tail[:, experts : 2 * experts] + tail[:, 2 * experts : 3 * experts]
    code = tail[:, 3 * experts : 4 * experts]
    grad = jnp.where(code > 0.5, picked - weight * jnp.sum(picked, axis=1, keepdims=True), 0.0)
    high, low = split_high_low(grad)
    core = at[2]
    for out, part in ((other, 1 - core), (own, core)):
        values = normed[:, pl.ds(pl.multiple_of(part * half, LANES), half)]
        out[...] = dot(high, values, (0, 0)) + dot(low, values, (0, 0))
    through[...] = dot(high, router[...], (1, 0)) + dot(low, router[...], (1, 0))


def terms_kernel(count, *refs):
    terms, out = refs[:count], refs[-1]
    while len(terms) > 1:
        terms = [terms[k][...].astype(F32) + terms[k + 1][...].astype(F32) for k in range(0, len(terms), 2)]
    out[...] = terms[0].astype(out.dtype)


def finish_kernel(sizes, at, *refs):
    exp_dev, hidden_units = sizes
    pieces, (mine, theirs, through, back) = refs[:-9], refs[-9:-5]
    grad_normed, router_grad, *outs = refs[-5:]
    core = at[2]
    half = mine.shape[1]
    router_grad[:, pl.ds(pl.multiple_of(core * half, LANES), half)] = mine[...]
    router_grad[:, pl.ds(pl.multiple_of((1 - core) * half, LANES), half)] = theirs[...]
    rows_total = through[...]
    for r in range(back.shape[0]):
        rows_total = rows_total + back[r].astype(F32)
    grad_normed[...] = rows_total.astype(grad_normed.dtype)
    total = pieces[0][...]
    for piece in pieces[1:]:
        total = total + piece[...].astype(F32)
    for k in range(3):
        for e in range(exp_dev):
            first = (k * exp_dev + e) * hidden_units
            outs[k][:, e, :] = total[first : first + hidden_units]


def on_device(normed, upstream, expert_ids, router_weight, gate_weight, up_weight, down_weight, saved_inputs):
    n_expert = lax.axis_size("expert")
    n_dp = lax.axis_size("dp")
    n_chip = n_dp // 2
    me = lax.axis_index("expert")
    dp = lax.axis_index("dp")
    core = dp & 1
    chip = dp >> 1
    exp_dev, hidden_units, width = gate_weight.shape
    capacity = saved_inputs.shape[3]
    experts = exp_dev * n_expert
    tokens_here = normed.shape[0]
    tokens = tokens_here * n_expert
    slots = exp_dev * capacity * n_expert
    hidden_all = exp_dev * hidden_units
    piece = width // n_dp
    half = width // 2
    even = piece % LANES == 0
    shape = jax.ShapeDtypeStruct

    def over_expert(value, k):
        return lax.ppermute(value, "expert", [(i, i ^ k) for i in range(n_expert)])

    def over_core(value):
        return lax.ppermute(value, "dp", [(i, i ^ 1) for i in range(n_dp)])

    def over_chip(value, k):
        return lax.ppermute(value, "dp", [(i, i ^ (2 * k)) for i in range(n_dp)])

    def in_hbm(*values):
        return [pltpu.with_memory_space_constraint(value, pltpu.HBM) for value in values]

    def call(kernel, name, outs, args, scalars=False, behind=0):
        specs = [pl.BlockSpec(memory_space=pltpu.VMEM)] * len(args)
        if scalars:
            specs[0] = pl.BlockSpec(memory_space=pltpu.SMEM)
        for k in range(behind):
            specs[-1 - k] = pl.BlockSpec(memory_space=pl.ANY)
        return pl.pallas_call(
            kernel,
            out_shape=outs,
            in_specs=specs,
            out_specs=[pl.BlockSpec(memory_space=pltpu.VMEM)] * len(outs),
            compiler_params=pltpu.CompilerParams(vmem_limit_bytes=VMEM_BYTES),
            cost_estimate=pl.CostEstimate(flops=0, bytes_accessed=0, transcendentals=0),
            name=name,
        )(*args)

    at = jnp.stack([me, chip, core]).astype(jnp.int32)
    router = router_weight.T
    first, packed = pl.pallas_call(
        functools.partial(route_kernel, experts),
        out_shape=[shape((tokens_here, half), BF16), shape((tokens_here, half + LANES), BF16)],
        in_specs=[pl.BlockSpec(memory_space=pltpu.HBM)] * 4,
        out_specs=[pl.BlockSpec(memory_space=pltpu.VMEM)] * 2,
        scratch_shapes=[
            pltpu.VMEM(expert_ids.shape[::-1], jnp.int32),
            pltpu.VMEM((tokens_here, width), BF16),
            pltpu.VMEM((experts, width), BF16),
            pltpu.VMEM((tokens_here, width), BF16),
            pltpu.SemaphoreType.DMA((4,)),
        ],
        compiler_params=pltpu.CompilerParams(vmem_limit_bytes=VMEM_BYTES),
        cost_estimate=pl.CostEstimate(flops=0, bytes_accessed=0, transcendentals=0),
        name="route",
    )(*in_hbm(expert_ids.T, normed, router, upstream))
    if n_expert == 4:
        first_1, second_2 = over_expert(first, 1), over_expert(packed, 2)
        second_1, first_2 = over_expert(packed, 1), over_expert(first, 2)
        firsts = [first, first_1, first_2, over_expert(first_1, 2)]
        seconds = [packed, second_1, second_2, over_expert(second_2, 1)]
    else:
        firsts = [first] + [over_expert(first, k) for k in range(1, n_expert)]
        seconds = [packed] + [over_expert(packed, k) for k in range(1, n_expert)]

    blocks = n_dp if even else 8
    sources = [jnp.transpose(saved_inputs[0], (0, 2, 1, 3)).reshape(exp_dev * capacity, n_expert, width)]
    sources += [jnp.transpose(w, (1, 0, 2)) for w in (gate_weight, up_weight, down_weight)]
    results = (
        [shape((slots, width), BF16)]
        + [shape((hidden_all, width), BF16)] * 3
        + [shape((slots, hidden_all), F32)] * 2
    )
    inputs, gate, up, down, pre_gate, pre_up = pl.pallas_call(
        functools.partial(prepare_kernel, blocks),
        out_shape=results,
        in_specs=[pl.BlockSpec(memory_space=pltpu.HBM)] * 4,
        out_specs=[pl.BlockSpec(memory_space=pltpu.VMEM)] * len(results),
        scratch_shapes=[pltpu.VMEM(source.shape, BF16) for source in sources]
        + [pltpu.SemaphoreType.DMA((4 * blocks,))],
        compiler_params=pltpu.CompilerParams(vmem_limit_bytes=VMEM_BYTES),
        cost_estimate=pl.CostEstimate(flops=0, bytes_accessed=0, transcendentals=0),
        name="prepare",
    )(*in_hbm(*sources))

    outs = call(
        functools.partial(expert_kernel, (n_expert, exp_dev, capacity, tokens_here)),
        "experts",
        [shape((tokens_here, LANES), F32)] * n_expert
        + [shape((tokens, slots), BF16)]
        + [shape((slots, hidden_all), BF16)] * 3
        + [shape((tokens, width), BF16)],
        (at, *firsts, *seconds, down, pre_gate, pre_up),
        scalars=True,
    )
    scores, by_slot, arrived = outs[:n_expert], outs[n_expert:-1], outs[-1]
    back_scores = [scores[0]] + [over_expert(scores[k], k) for k in range(1, n_expert)]
    tok_gate, tok_up, *turned = call(
        functools.partial(core_kernel, (n_expert, exp_dev, n_chip, piece, even)),
        "core_terms",
        [shape((tokens, hidden_all), BF16)] * 2
        + [shape((hidden_all, slots), BF16)] * 2
        + [shape((hidden_all, tokens), BF16)]
        + [shape((n_chip, 3 * hidden_all, piece), BF16)] * even,
        (at, *seconds, *by_slot, arrived, inputs),
        scalars=True,
    )
    turned, theirs = turned[:3], turned[3:]
    if even:
        from_core = over_core(theirs[0])
        (mine,) = call(
            functools.partial(weight_kernel, (n_chip, piece)),
            "weight_terms",
            [shape((n_chip, 3 * hidden_all, piece), F32)],
            (at, arrived, inputs, *turned),
            scalars=True,
        )
    if even:
        chip_sums = call(
            add_kernel,
            "core_sum",
            [shape((3 * hidden_all, piece), BF16 if k else F32) for k in range(n_chip)],
            (mine, from_core),
        )
    else:
        terms = [dot(turned[0], inputs, (1, 0)), dot(turned[1], inputs, (1, 0)), dot(turned[2], arrived, (1, 0))]
        terms = jnp.concatenate(terms, axis=0).reshape(3 * hidden_all, n_chip, 2, piece)
        terms = jnp.transpose(terms, (2, 1, 0, 3))
        from_core = over_core(terms[1 - core].astype(BF16))
        terms = terms[core] + from_core.astype(F32)
        chip_sums = [terms[chip ^ k].astype(BF16 if k else F32) for k in range(n_chip)]
    chip_sums, back_scores = lax.optimization_barrier((chip_sums, back_scores))
    moved = {k: over_chip(chip_sums[k], k) for k in range(n_chip - 1, 1, -1)}

    always = dp < n_dp

    def add_terms(terms, dtype, *behind):
        kernel = functools.partial(terms_kernel, len(terms))
        return call(kernel, "add_terms", [shape(terms[0].shape, dtype)], (*terms, *behind), behind=len(behind))[0]

    def add_pair(total, move, k, dtype=BF16):
        return add_terms([total, move(total, 1 << k)], dtype)

    expert_rounds, chip_rounds = n_expert.bit_length() - 1, n_chip.bit_length() - 1

    def sum_chips(values):
        total, near = values
        for k in range(chip_rounds):
            total = add_pair(total, over_chip, k, F32 if k == chip_rounds - 1 else BF16)
            if k == 0:
                near, total = lax.optimization_barrier((near, total))
                near = over_chip(near, 1)
        return near, total, over_core(total)

    def as_one(function, values):
        outs = jax.eval_shape(function, values)
        return lax.cond(always, function, lambda values: jax.tree.map(lambda o: jnp.zeros(o.shape, o.dtype), outs), values)

    def way_back(values):
        back_scores, packed, normed, router, tok_gate, tok_up, gate, up, near = values
        other, own, through = call(
            functools.partial(router_kernel, experts, n_expert),
            "router_terms",
            [shape((experts, half), F32)] * 2 + [shape((tokens_here, width), F32)],
            (at, *back_scores, packed, normed, router),
            scalars=True,
        )
        (row_pieces,) = call(
            functools.partial(row_kernel, n_expert, 8),
            "row_terms",
            [shape((n_expert, tokens_here, width), BF16)],
            (at, tok_gate, tok_up, gate, up, other),
            scalars=True,
            behind=1,
        )
        total = add_terms([own, over_core(other)], BF16)
        if n_expert == 4:
            total = add_terms([total] + [over_expert(total, k) for k in range(1, n_expert)], BF16)
        else:
            for k in range(expert_rounds):
                total = add_pair(total, over_expert, k)
        row_pieces, total = lax.optimization_barrier((row_pieces, total))
        back_rows = lax.all_to_all(row_pieces, "expert", 0, 0, tiled=True)
        return *as_one(sum_chips, (total, near)), through, back_rows

    near, *back = as_one(way_back, (back_scores, packed, normed, router, tok_gate, tok_up, gate, up, chip_sums[1]))
    chip_pieces = [chip_sums[0], near] + [moved[k] for k in range(2, n_chip)]
    grad_normed, router_grad, *grads = call(
        functools.partial(finish_kernel, (exp_dev, hidden_units)),
        "finish",
        [shape((tokens_here, width), BF16), shape((experts, width), F32)]
        + [shape((hidden_units, exp_dev, piece), F32)] * 3,
        (at, *chip_pieces, *back),
        scalars=True,
    )
    grads = [jnp.transpose(g, (1, 0, 2)) for g in grads]
    return (grad_normed, router_grad.T, *grads)


def solution(mesh):
    placed = (
        P(("dp", "expert"), None),
        P(("dp", "expert"), None),
        P(("dp", "expert"), None),
        P(),
        P("expert", None, None),
        P("expert", None, None),
        P("expert", None, None),
        P("dp", "expert", None, None, None),
    )
    return jax.shard_map(
        on_device,
        mesh=mesh,
        in_specs=placed,
        out_specs=(
            P(("dp", "expert"), None),
            P(),
            P("expert", None, "dp"),
            P("expert", None, "dp"),
            P("expert", None, "dp"),
        ),
        check_vma=False,
    )
```

time: 79.2 us -> 78.2 us (0.987)
  the two profiles are of different devices: /device:TPU:0 before, /device:TPU:8 now
where the time goes in v4:
time: 78.2 us; the launch traced here: 77.6 us
  waiting for transfers between devices  28.1 us (36%)
  starting transfers between devices  27.8 us (36%)
  Pallas kernels  20.8 us (27%)
    ppermute x5, waiting for transfers between devices, over_chip(): return lax.ppermute(value, 'dp', [(i, i ^ 2 * k) for i in range(n_dp)])  17 us
    ppermute x12, starting transfers between devices, over_expert(): return lax.ppermute(value, 'expert', [(i, i ^ k) for i in range(n_expert)])  14.2 us
    pallas_call x11, Pallas kernels, call(): pl.pallas_call(kernel, out_shape=outs, in_specs=specs, out_specs=[pl.Bloc...  14.1 us
    ppermute x5, starting transfers between devices, over_chip(): return lax.ppermute(value, 'dp', [(i, i ^ 2 * k) for i in range(n_dp)])  9.09 us
    ppermute x12, waiting for transfers between devices, over_expert(): return lax.ppermute(value, 'expert', [(i, i ^ k) for i in range(n_expert)])  7.88 us
    pallas_call x1, Pallas kernels, on_device(): pl.pallas_call(functools.partial(prepare_kernel, blocks), out_shape=resul...  5.12 us
    all_to_all x1, starting transfers between devices, way_back(): back_rows = lax.all_to_all(row_pieces, 'expert', 0, 0, tiled=True)  4.36 us
    ppermute x3, waiting for transfers between devices, over_core(): return lax.ppermute(value, 'dp', [(i, i ^ 1) for i in range(n_dp)])  3.21 us
  transfers between devices with their start and end apart: 21, of which 9 were waited for; matrix products, arithmetic and copies ran while one was open for 0% of the time, Pallas kernels for 17%

profile of v4, /device:TPU:8, one launch (start us, length us, event | category | flops | bytes accessed | tf_op | source)
XLA Modules:
  0.0 77.6 jit_solution(1566579243935557182)
XLA Ops:
  0.6 1.6 %route.1 = (bf16[32,3072]{1,0:T(8,128)(2,1)S(1)}, bf16[32,3200]{1,0:T(8,128)(2,1)S(1)}) custom-call(s32[4,32]{1,0:T(4,128)} %bitcast.23, bf16[32,6144]{1,0:T(8,128)(2,1)} %refs_1_.1, bf16[16,6144]{1,0:T(8,128)(2,1)} %bitcast.21, bf16[32,6144]{1,0:T(8,128)(2,1)} %refs_3_.1), custom_call_target="tpu_custom_call" | custom-call | tf_op jit(solution)/shard_map/route/pallas_call | solution.py:311
  2.3 1.6 %collective-permute-start.12 = (bf16[32,3200]{1,0:T(8,128)(2,1)S(1)}, bf16[32,3200]{1,0:T(8,128)(2,1)S(1)}, u32[]{:S(2)}, u32[]{:S(2)}) collective-permute-start(bf16[32,3200]{1,0:T(8,128)(2,1)S(1)} %get-tuple-element.109.refs_4_.refs_0_), channel_id=1, source_target_pairs={{0,2},{1,3},{2,0},{3,1},{4,6},{5,7},{6,4},{7,5},{8,10},{9,11},{10,... | collective-permute-start | bytes 614408 | tf_op jit(solution)/shard_map/ppermute | solution.py:282
  3.8 1.5 %collective-permute-start.8 = (bf16[32,3072]{1,0:T(8,128)(2,1)S(1)}, bf16[32,3072]{1,0:T(8,128)(2,1)S(1)}, u32[]{:S(2)}, u32[]{:S(2)}) collective-permute-start(bf16[32,3072]{1,0:T(8,128)(2,1)S(1)} %get-tuple-element.108.refs_0_), channel_id=1, source_target_pairs={{0,1},{1,0},{2,3},{3,2},{4,5},{5,4},{6,7},{7,6},{8,9},{9,8},{10,11... | collective-permute-start | bytes 589832 | tf_op jit(solution)/shard_map/ppermute | solution.py:282
  5.9 3.3 %collective-permute-done.12.refs_6_.refs_2_ = bf16[32,3200]{1,0:T(8,128)(2,1)S(1)} collective-permute-done((bf16[32,3200]{1,0:T(8,128)(2,1)S(1)}, bf16[32,3200]{1,0:T(8,128)(2,1)S(1)}, u32[]{:S(2)}, u32[]{:S(2)}) %collective-permute-start.12) | collective-permute-done | bytes 204832 | tf_op jit(solution)/shard_map/ppermute | solution.py:282
  9.1 1.5 %collective-permute-start.13 = (bf16[32,3200]{1,0:T(8,128)(2,1)S(1)}, bf16[32,3200]{1,0:T(8,128)(2,1)S(1)}, u32[]{:S(2)}, u32[]{:S(2)}) collective-permute-start(bf16[32,3200]{1,0:T(8,128)(2,1)S(1)} %collective-permute-done.12.refs_6_.refs_2_), channel_id=1, source_target_pairs={{0,1},{1,0},{2,3},{3,2},{4,5},{5,4},{6,7},{7,6},{8,9},{9,8},{10,11... | collective-permute-start | bytes 614408 | tf_op jit(solution)/shard_map/ppermute | solution.py:282
  10.6 1.5 %collective-permute-start.9 = (bf16[32,3072]{1,0:T(8,128)(2,1)S(1)}, bf16[32,3072]{1,0:T(8,128)(2,1)S(1)}, u32[]{:S(2)}, u32[]{:S(2)}) collective-permute-start(bf16[32,3072]{1,0:T(8,128)(2,1)S(1)} %get-tuple-element.108.refs_0_), channel_id=1, source_target_pairs={{0,2},{1,3},{2,0},{3,1},{4,6},{5,7},{6,4},{7,5},{8,10},{9,11},{10,... | collective-permute-start | bytes 589832 | tf_op jit(solution)/shard_map/ppermute | solution.py:282
  12.7 5.1 %prepare.1 = (bf16[144,6144]{1,0:T(8,128)(2,1)S(1)}, bf16[80,6144]{1,0:T(8,128)(2,1)}, bf16[80,6144]{1,0:T(8,128)(2,1)}, bf16[80,6144]{1,0:T(8,128)(2,1)S(1)}, f...) custom-call(bf16[36,4,6144]{2,1,0:T(4,128)(2,1)} %bitcast.17, bf16[20,4,6144]{2,1,0:T(4,128)(2,1)} %bitcast.18, ...), custom_call_target="tpu_custom_call" | custom-call | tf_op jit(solution)/shard_map/prepare/pallas_call | solution.py:344
  18.2 2.1 %collective-permute-done.10.refs_3_ = bf16[32,3072]{1,0:T(8,128)(2,1)S(1)} collective-permute-done((bf16[32,3072]{1,0:T(8,128)(2,1)S(1)}, bf16[32,3072]{1,0:T(8,128)(2,1)S(1)}, u32[]{:S(2)}, u32[]{:S(2)}) %collective-permute-start.10) | collective-permute-done | bytes 196640 | tf_op jit(solution)/shard_map/ppermute | solution.py:282
  20.3 1.7 %experts.1 = (f32[32,128]{1,0:T(8,128)S(1)}, f32[32,128]{1,0:T(8,128)S(1)}, f32[32,128]{1,0:T(8,128)S(1)}, f32[32,128]{1,0:T(8,128)S(1)}, bf16[128,144]{1,0:T(8,...) custom-call(s32[3]{0:T(128)S(1)} %pad_add_fusion.at, ...), custom_call_target="tpu_custom_call" | custom-call | tf_op jit(solution)/shard_map/experts/pallas_call | solution.py:299
  22.0 1.4 %core_terms.1 = (bf16[128,80]{1,0:T(8,128)(2,1)S(1)}, bf16[128,80]{1,0:T(8,128)(2,1)S(1)}, bf16[80,144]{1,0:T(8,128)(2,1)S(1)}, bf16[80,144]{1,0:T(8,128)(2,1)S(...) custom-call(s32[3]{0:T(128)S(1)} %pad_add_fusion.at, ...), custom_call_target="tpu_custom_call" | custom-call | tf_op jit(solution)/shard_map/core_terms/pallas_call | solution.py:299
  24.0 1.5 %collective-permute-start.16 = (f32[32,128]{1,0:T(8,128)S(1)}, f32[32,128]{1,0:T(8,128)S(1)}, u32[]{:S(2)}, u32[]{:S(2)}) collective-permute-start(f32[32,128]{1,0:T(8,128)S(1)} %get-tuple-element.129), channel_id=1, source_target_pairs={{0,2},{1,3},{2,0},{3,1},{4,6},{5,7},{6,4},{7,5},{8,10},{9,11},{10,... | collective-permute-start | bytes 49160 | tf_op jit(solution)/shard_map/ppermute | solution.py:282
  25.6 1.4 %collective-permute-start.17 = (f32[32,128]{1,0:T(8,128)S(1)}, f32[32,128]{1,0:T(8,128)S(1)}, u32[]{:S(2)}, u32[]{:S(2)}) collective-permute-start(f32[32,128]{1,0:T(8,128)S(1)} %get-tuple-element.130), channel_id=1, source_target_pairs={{0,3},{1,2},{2,1},{3,0},{4,7},{5,6},{6,5},{7,4},{8,11},{9,10},{10,... | collective-permute-start | bytes 49160 | tf_op jit(solution)/shard_map/ppermute | solution.py:282
  27.0 1.1 %weight_terms.1.mine = f32[4,240,768]{2,1,0:T(8,128)S(1)} custom-call(s32[3]{0:T(128)S(1)} %pad_add_fusion.at, bf16[128,6144]{1,0:T(8,128)(2,1)S(1)} %get-tuple-element.113.refs_8_.arrived, bf16[144,6144]{1,0:T(8,128)(2,1)S(1)} %get-tuple-element.114.refs_9_.inputs, bf16[80,144]{1,0:T(8,128)(2,1)S(1)} %get-tuple-element.119.gate, ...), custom_call_target="tpu_custom_call" | custom-call | tf_op jit(solution)/shard_map/weight_terms/pallas_call | solution.py:299
  28.1 0.9 %core_sum.1 = (f32[240,768]{1,0:T(8,128)S(1)}, bf16[240,768]{1,0:T(8,128)(2,1)}, bf16[240,768]{1,0:T(8,128)(2,1)S(1)}, bf16[240,768]{1,0:T(8,128)(2,1)S(1)}) custom-call(f32[4,240,768]{2,1,0:T(8,128)S(1)} %weight_terms.1.mine, bf16[4,240,768]{2,1,0:T(8,128)(2,1)S(1)} %collective-permute-done.14.theirs), custom_call_target="tpu_custom_call" | custom-call | tf_op jit(solution)/shard_map/core_sum/pallas_call | solution.py:299
  29.1 1.1 %collective-permute-done.17 = f32[32,128]{1,0:T(8,128)S(1)} collective-permute-done((f32[32,128]{1,0:T(8,128)S(1)}, f32[32,128]{1,0:T(8,128)S(1)}, u32[]{:S(2)}, u32[]{:S(2)}) %collective-permute-start.17) | collective-permute-done | bytes 16416 | tf_op jit(solution)/shard_map/ppermute | solution.py:282
  30.2 2.6 %collective-permute-start.18 = (bf16[240,768]{1,0:T(8,128)(2,1)S(1)}, bf16[240,768]{1,0:T(8,128)(2,1)S(1)}, u32[]{:S(2)}, u32[]{:S(2)}) collective-permute-start(bf16[240,768]{1,0:T(8,128)(2,1)S(1)} %get-tuple-element.142), channel_id=1, source_target_pairs={{0,16},{4,20},{8,24},{12,28},{16,0},{20,4},{24,8},{28,12},{1,17},{... | collective-permute-start | bytes 1105928 | tf_op jit(solution)/shard_map/ppermute | solution.py:288
  32.8 41.7 %conditional.2 = (bf16[240,768]{1,0:T(8,128)(2,1)}, f32[16,3072]{1,0:T(8,128)}, f32[16,3072]{1,0:T(8,128)}, f32[32,6144]{1,0:T(8,128)S(1)}, bf16[4,32,6144]{2,1,0:T(8,128)(2,1)}) conditional(s32[]{:T(128)} %convert_element_type.6, () %tuple.28, (pred[]{:T(512)}, s32[3]{0:T(128)S(1)}, f32[32,128]{1,0:T(8,128)S(1)}, f32[32,128]{1,0:T(8,128)S(1)}, ...), branch_computations={%region_0.0_spmd, %region_1.0_spmd} | conditional | flops 1 | bytes 13664721 | solution.py:427
  32.8 1.8 %router_terms.1 = (f32[16,3072]{1,0:T(8,128)S(1)}, f32[16,3072]{1,0:T(8,128)S(1)}, f32[32,6144]{1,0:T(8,128)S(1)}) custom-call(s32[3]{0:T(128)S(1)} %get-tuple-element.37.at, f32[32,128]{1,0:T(8,128)S(1)} %get-tuple-element.42.refs_0_, f32[32,128]{1,0:T(8,128)S(1)} %get-tuple-element.43.refs_1_, f32[32,128]{1,0:T(8,128)S(1)} %get-tuple-element.44.refs_2_, ...), custom_call_target="tpu_custom_call" | custom-call | tf_op jit(solution)/shard_map/cond/branch_1_fun/router_terms/pallas_call | solution.py:299
  34.7 1.4 %collective-permute-done.4.refs_1_ = f32[16,3072]{1,0:T(8,128)S(1)} collective-permute-done((f32[16,3072]{1,0:T(8,128)S(1)}, f32[16,3072]{1,0:T(8,128)S(1)}, u32[]{:S(2)}, u32[]{:S(2)}) %collective-permute-start.4) | collective-permute-done | bytes 196640 | tf_op jit(solution)/shard_map/cond/branch_1_fun/ppermute | solution.py:285
  36.2 1.5 %collective-permute-start.7 = (bf16[16,3072]{1,0:T(8,128)(2,1)S(1)}, bf16[16,3072]{1,0:T(8,128)(2,1)S(1)}, u32[]{:S(2)}, u32[]{:S(2)}) collective-permute-start(bf16[16,3072]{1,0:T(8,128)(2,1)S(1)} %add_terms.6.refs_0_), channel_id=1, source_target_pairs={{0,3},{1,2},{2,1},{3,0},{4,7},{5,6},{6,5},{7,4},{8,11},{9,10},{10,... | collective-permute-start | bytes 294920 | tf_op jit(solution)/shard_map/cond/branch_1_fun/ppermute | solution.py:282
  37.7 1.5 %collective-permute-start.6 = (bf16[16,3072]{1,0:T(8,128)(2,1)S(1)}, bf16[16,3072]{1,0:T(8,128)(2,1)S(1)}, u32[]{:S(2)}, u32[]{:S(2)}) collective-permute-start(bf16[16,3072]{1,0:T(8,128)(2,1)S(1)} %add_terms.6.refs_0_), channel_id=1, source_target_pairs={{0,2},{1,3},{2,0},{3,1},{4,6},{5,7},{6,4},{7,5},{8,10},{9,11},{10,... | collective-permute-start | bytes 294920 | tf_op jit(solution)/shard_map/cond/branch_1_fun/ppermute | solution.py:282
  39.7 3.4 %row_terms.1 = bf16[4,32,6144]{2,1,0:T(8,128)(2,1)} custom-call(s32[3]{0:T(128)S(1)} %get-tuple-element.37.at, bf16[128,80]{1,0:T(8,128)(2,1)S(1)} %get-tuple-element.38.tok_gate, bf16[128,80]{1,0:T(8,128)(2,1)S(1)} %get-tuple-element.39.tok_up, bf16[80,6144]{1,0:T(8,128)(2,1)S(1)} %copy-done, bf16[80,6144]{1,0:T(8,128)(2,1)} %get-tuple-element.41.up, ...), custom_call_target="tpu_custom_call" | custom-call | tf_op jit(solution)/shard_map/cond/branch_1_fun/row_terms/pallas_call | solution.py:299
  43.1 1.0 %collective-permute-done.6.refs_2_ = bf16[16,3072]{1,0:T(8,128)(2,1)S(1)} collective-permute-done((bf16[16,3072]{1,0:T(8,128)(2,1)S(1)}, bf16[16,3072]{1,0:T(8,128)(2,1)S(1)}, u32[]{:S(2)}, u32[]{:S(2)}) %collective-permute-start.6) | collective-permute-done | bytes 98336 | tf_op jit(solution)/shard_map/cond/branch_1_fun/ppermute | solution.py:282
  44.1 4.4 %all-to-all-start = ((bf16[4,32,6144]{2,1,0:T(8,128)(2,1)}), bf16[4,32,6144]{2,1,0:T(8,128)(2,1)}, u32[]{:S(2)}, u32[]{:S(2)}) async-start(bf16[4,32,6144]{2,1,0:T(8,128)(2,1)} %row_terms.1), calls=%async_computation | async-start | bytes 3145728 | tf_op jit(solution)/shard_map/cond/branch_1_fun/all_to_all | solution.py:453
  48.5 26.0 %conditional = (bf16[240,768]{1,0:T(8,128)(2,1)}, f32[16,3072]{1,0:T(8,128)}, f32[16,3072]{1,0:T(8,128)}) conditional(s32[]{:T(128)} %convert_element_type.4, () %tuple.18, (bf16[16,3072]{1,0:T(8,128)(2,1)S(1)}, bf16[240,768]{1,0:T(8,128)(2,1)}) %tuple.20), branch_computations={%region_2.0_spmd, %region_3.0_spmd} | conditional | bytes 3047608 | solution.py:427
  48.5 1.9 %collective-permute-start = (bf16[16,3072]{1,0:T(8,128)(2,1)S(1)}, bf16[16,3072]{1,0:T(8,128)(2,1)S(1)}, u32[]{:S(2)}, u32[]{:S(2)}) collective-permute-start(bf16[16,3072]{1,0:T(8,128)(2,1)S(1)} %get-tuple-element.33.refs_0_), channel_id=1, source_target_pairs={{0,8},{4,12},{8,0},{12,4},{16,24},{20,28},{24,16},{28,20},{1,9},{5... | collective-permute-start | bytes 294920 | tf_op jit(solution)/shard_map/cond/branch_1_fun/cond/branch_1_fun/ppermute | solution.py:288
  50.4 5.9 %collective-permute-done.refs_1_ = bf16[16,3072]{1,0:T(8,128)(2,1)S(1)} collective-permute-done((bf16[16,3072]{1,0:T(8,128)(2,1)S(1)}, bf16[16,3072]{1,0:T(8,128)(2,1)S(1)}, u32[]{:S(2)}, u32[]{:S(2)}) %collective-permute-start) | collective-permute-done | bytes 98336 | tf_op jit(solution)/shard_map/cond/branch_1_fun/cond/branch_1_fun/ppermute | solution.py:288
  56.2 2.5 %collective-permute-start.1 = (bf16[240,768]{1,0:T(8,128)(2,1)}, bf16[240,768]{1,0:T(8,128)(2,1)}, u32[]{:S(2)}, u32[]{:S(2)}) collective-permute-start(bf16[240,768]{1,0:T(8,128)(2,1)} %get-tuple-element.34), channel_id=1, source_target_pairs={{0,8},{4,12},{8,0},{12,4},{16,24},{20,28},{24,16},{28,20},{1,9},{5... | collective-permute-start | bytes 1105928 | tf_op jit(solution)/shard_map/cond/branch_1_fun/cond/branch_1_fun/ppermute | solution.py:288
  58.8 2.1 %collective-permute-start.2 = (bf16[16,3072]{1,0:T(8,128)(2,1)S(1)}, bf16[16,3072]{1,0:T(8,128)(2,1)S(1)}, u32[]{:S(2)}, u32[]{:S(2)}) collective-permute-start(bf16[16,3072]{1,0:T(8,128)(2,1)S(1)} %add_terms.4.refs_0_), channel_id=1, source_target_pairs={{0,16},{4,20},{8,24},{12,28},{16,0},{20,4},{24,8},{28,12},{1,17},{... | collective-permute-start | bytes 294920 | tf_op jit(solution)/shard_map/cond/branch_1_fun/cond/branch_1_fun/ppermute | solution.py:288
  60.9 11.1 %collective-permute-done.2.refs_1_ = bf16[16,3072]{1,0:T(8,128)(2,1)S(1)} collective-permute-done((bf16[16,3072]{1,0:T(8,128)(2,1)S(1)}, bf16[16,3072]{1,0:T(8,128)(2,1)S(1)}, u32[]{:S(2)}, u32[]{:S(2)}) %collective-permute-start.2) | collective-permute-done | bytes 98336 | tf_op jit(solution)/shard_map/cond/branch_1_fun/cond/branch_1_fun/ppermute | solution.py:288
  72.7 1.8 %collective-permute-done.3 = f32[16,3072]{1,0:T(8,128)} collective-permute-done((f32[16,3072]{1,0:T(8,128)}, f32[16,3072]{1,0:T(8,128)}, u32[]{:S(2)}, u32[]{:S(2)}) %collective-permute-start.3) | collective-permute-done | bytes 196640 | tf_op jit(solution)/shard_map/cond/branch_1_fun/cond/branch_1_fun/ppermute | solution.py:285
  74.5 3.0 %finish.1 = (bf16[32,6144]{1,0:T(8,128)(2,1)}, f32[16,6144]{1,0:T(8,128)}, f32[20,4,768]{2,1,0:T(4,128)}, f32[20,4,768]{2,1,0:T(4,128)}, f32[20,4,768]{2,1,0:T(4,128)}) custom-call(s32[3]{0:T(128)S(1)} %pad_add_fusion.at, f32[240,768]{1,0:T(8,128)S(1)} %get-tuple-element.131.refs_0_, bf16[240,768]{1,0:T(8,128)(2,1)} %get-tuple-element.141.refs_1_, ...), custom_call_target="tpu_custom_call" | custom-call | tf_op jit(solution)/shard_map/finish/pallas_call | solution.py:299
  (30 shorter events, 3.6 us)
Async XLA Ops:
  2.3 6.9 %collective-permute-start.12 = (bf16[32,3200]{1,0:T(8,128)(2,1)S(1)}, bf16[32,3200]{1,0:T(8,128)(2,1)S(1)}, u32[]{:S(2)}, u32[]{:S(2)}) collective-permute-start(bf16[32,3200]{1,0:T(8,128)(2,1)S(1)} %get-tuple-element.109.refs_4_.refs_0_), channel_id=1, source_target_pairs={{0,2},{1,3},{2,0},{3,1},{4,6},{5,7},{6,4},{7,5},{8,10},{9,11},{10,... | collective-permute-start | bytes 614408 | tf_op jit(solution)/shard_map/ppermute | solution.py:282
  3.8 8.3 %collective-permute-start.8 = (bf16[32,3072]{1,0:T(8,128)(2,1)S(1)}, bf16[32,3072]{1,0:T(8,128)(2,1)S(1)}, u32[]{:S(2)}, u32[]{:S(2)}) collective-permute-start(bf16[32,3072]{1,0:T(8,128)(2,1)S(1)} %get-tuple-element.108.refs_0_), channel_id=1, source_target_pairs={{0,1},{1,0},{2,3},{3,2},{4,5},{5,4},{6,7},{7,6},{8,9},{9,8},{10,11... | collective-permute-start | bytes 589832 | tf_op jit(solution)/shard_map/ppermute | solution.py:282
  5.3 12.9 %collective-permute-start.11 = (bf16[32,3200]{1,0:T(8,128)(2,1)S(1)}, bf16[32,3200]{1,0:T(8,128)(2,1)S(1)}, u32[]{:S(2)}, u32[]{:S(2)}) collective-permute-start(bf16[32,3200]{1,0:T(8,128)(2,1)S(1)} %get-tuple-element.109.refs_4_.refs_0_), channel_id=1, source_target_pairs={{0,1},{1,0},{2,3},{3,2},{4,5},{5,4},{6,7},{7,6},{8,9},{9,8},{10,11... | collective-permute-start | bytes 614408 | tf_op jit(solution)/shard_map/ppermute | solution.py:282
  9.1 11.2 %collective-permute-start.13 = (bf16[32,3200]{1,0:T(8,128)(2,1)S(1)}, bf16[32,3200]{1,0:T(8,128)(2,1)S(1)}, u32[]{:S(2)}, u32[]{:S(2)}) collective-permute-start(bf16[32,3200]{1,0:T(8,128)(2,1)S(1)} %collective-permute-done.12.refs_6_.refs_2_), channel_id=1, source_target_pairs={{0,1},{1,0},{2,3},{3,2},{4,5},{5,4},{6,7},{7,6},{8,9},{9,8},{10,11... | collective-permute-start | bytes 614408 | tf_op jit(solution)/shard_map/ppermute | solution.py:282
  10.6 7.6 %collective-permute-start.9 = (bf16[32,3072]{1,0:T(8,128)(2,1)S(1)}, bf16[32,3072]{1,0:T(8,128)(2,1)S(1)}, u32[]{:S(2)}, u32[]{:S(2)}) collective-permute-start(bf16[32,3072]{1,0:T(8,128)(2,1)S(1)} %get-tuple-element.108.refs_0_), channel_id=1, source_target_pairs={{0,2},{1,3},{2,0},{3,1},{4,6},{5,7},{6,4},{7,5},{8,10},{9,11},{10,... | collective-permute-start | bytes 589832 | tf_op jit(solution)/shard_map/ppermute | solution.py:282
  12.1 8.2 %collective-permute-start.10 = (bf16[32,3072]{1,0:T(8,128)(2,1)S(1)}, bf16[32,3072]{1,0:T(8,128)(2,1)S(1)}, u32[]{:S(2)}, u32[]{:S(2)}) collective-permute-start(bf16[32,3072]{1,0:T(8,128)(2,1)S(1)} %collective-permute-done.8.refs_1_), channel_id=1, source_target_pairs={{0,2},{1,3},{2,0},{3,1},{4,6},{5,7},{6,4},{7,5},{8,10},{9,11},{10,... | collective-permute-start | bytes 589832 | tf_op jit(solution)/shard_map/ppermute | solution.py:282
  23.4 4.7 %collective-permute-start.14 = (bf16[4,240,768]{2,1,0:T(8,128)(2,1)S(1)}, bf16[4,240,768]{2,1,0:T(8,128)(2,1)S(1)}, u32[]{:S(2)}, u32[]{:S(2)}) collective-permute-start(bf16[4,240,768]{2,1,0:T(8,128)(2,1)S(1)} %get-tuple-element.122), channel_id=1, source_target_pairs={{0,4},{4,0},{8,12},{12,8},{16,20},{20,16},{24,28},{28,24},{1,5},{5... | collective-permute-start | bytes 4423688 | tf_op jit(solution)/shard_map/ppermute | solution.py:285
  23.4 5.6 %collective-permute-start.15 = (f32[32,128]{1,0:T(8,128)S(1)}, f32[32,128]{1,0:T(8,128)S(1)}, u32[]{:S(2)}, u32[]{:S(2)}) collective-permute-start(f32[32,128]{1,0:T(8,128)S(1)} %get-tuple-element.128), channel_id=1, source_target_pairs={{0,1},{1,0},{2,3},{3,2},{4,5},{5,4},{6,7},{7,6},{8,9},{9,8},{10,11... | collective-permute-start | bytes 49160 | tf_op jit(solution)/shard_map/ppermute | solution.py:282
  24.0 5.0 %collective-permute-start.16 = (f32[32,128]{1,0:T(8,128)S(1)}, f32[32,128]{1,0:T(8,128)S(1)}, u32[]{:S(2)}, u32[]{:S(2)}) collective-permute-start(f32[32,128]{1,0:T(8,128)S(1)} %get-tuple-element.129), channel_id=1, source_target_pairs={{0,2},{1,3},{2,0},{3,1},{4,6},{5,7},{6,4},{7,5},{8,10},{9,11},{10,... | collective-permute-start | bytes 49160 | tf_op jit(solution)/shard_map/ppermute | solution.py:282
  25.6 4.6 %collective-permute-start.17 = (f32[32,128]{1,0:T(8,128)S(1)}, f32[32,128]{1,0:T(8,128)S(1)}, u32[]{:S(2)}, u32[]{:S(2)}) collective-permute-start(f32[32,128]{1,0:T(8,128)S(1)} %get-tuple-element.130), channel_id=1, source_target_pairs={{0,3},{1,2},{2,1},{3,0},{4,7},{5,6},{6,5},{7,4},{8,11},{9,10},{10,... | collective-permute-start | bytes 49160 | tf_op jit(solution)/shard_map/ppermute | solution.py:282
  28.1 4.7 %copy-start.1 = (bf16[6144,16]{0,1:T(8,128)(2,1)S(1)}, bf16[6144,16]{0,1:T(8,128)(2,1)}, u32[]{:S(2)}) copy-start(bf16[6144,16]{0,1:T(8,128)(2,1)} %param.15) | copy-start | bytes 589828
  30.2 44.3 %collective-permute-start.18 = (bf16[240,768]{1,0:T(8,128)(2,1)S(1)}, bf16[240,768]{1,0:T(8,128)(2,1)S(1)}, u32[]{:S(2)}, u32[]{:S(2)}) collective-permute-start(bf16[240,768]{1,0:T(8,128)(2,1)S(1)} %get-tuple-element.142), channel_id=1, source_target_pairs={{0,16},{4,20},{8,24},{12,28},{16,0},{20,4},{24,8},{28,12},{1,17},{... | collective-permute-start | bytes 1105928 | tf_op jit(solution)/shard_map/ppermute | solution.py:288
  32.8 41.7 %collective-permute-start.19 = (bf16[240,768]{1,0:T(8,128)(2,1)S(1)}, bf16[240,768]{1,0:T(8,128)(2,1)S(1)}, u32[]{:S(2)}, u32[]{:S(2)}) collective-permute-start(bf16[240,768]{1,0:T(8,128)(2,1)S(1)} %get-tuple-element.143), channel_id=1, source_target_pairs={{0,24},{4,28},{8,16},{12,20},{16,8},{20,12},{24,0},{28,4},{1,25},{... | collective-permute-start | bytes 1105928 | tf_op jit(solution)/shard_map/ppermute | solution.py:288
  32.8 6.9 %copy-start = (bf16[80,6144]{1,0:T(8,128)(2,1)S(1)}, bf16[80,6144]{1,0:T(8,128)(2,1)}, u32[]{:S(2)}) copy-start(bf16[80,6144]{1,0:T(8,128)(2,1)} %get-tuple-element.40.gate) | copy-start | bytes 2949124 | tf_op jit(solution)/shard_map/cond
  34.6 1.5 %collective-permute-start.4 = (f32[16,3072]{1,0:T(8,128)S(1)}, f32[16,3072]{1,0:T(8,128)S(1)}, u32[]{:S(2)}, u32[]{:S(2)}) collective-permute-start(f32[16,3072]{1,0:T(8,128)S(1)} %get-tuple-element.49.behind), channel_id=1, source_target_pairs={{0,4},{4,0},{8,12},{12,8},{16,20},{20,16},{24,28},{28,24},{1,5},{5... | collective-permute-start | bytes 589832 | tf_op jit(solution)/shard_map/cond/branch_1_fun/ppermute | solution.py:285
  36.2 6.9 %collective-permute-start.7 = (bf16[16,3072]{1,0:T(8,128)(2,1)S(1)}, bf16[16,3072]{1,0:T(8,128)(2,1)S(1)}, u32[]{:S(2)}, u32[]{:S(2)}) collective-permute-start(bf16[16,3072]{1,0:T(8,128)(2,1)S(1)} %add_terms.6.refs_0_), channel_id=1, source_target_pairs={{0,3},{1,2},{2,1},{3,0},{4,7},{5,6},{6,5},{7,4},{8,11},{9,10},{10,... | collective-permute-start | bytes 294920 | tf_op jit(solution)/shard_map/cond/branch_1_fun/ppermute | solution.py:282
  37.7 6.4 %collective-permute-start.6 = (bf16[16,3072]{1,0:T(8,128)(2,1)S(1)}, bf16[16,3072]{1,0:T(8,128)(2,1)S(1)}, u32[]{:S(2)}, u32[]{:S(2)}) collective-permute-start(bf16[16,3072]{1,0:T(8,128)(2,1)S(1)} %add_terms.6.refs_0_), channel_id=1, source_target_pairs={{0,2},{1,3},{2,0},{3,1},{4,6},{5,7},{6,4},{7,5},{8,10},{9,11},{10,... | collective-permute-start | bytes 294920 | tf_op jit(solution)/shard_map/cond/branch_1_fun/ppermute | solution.py:282
  39.2 4.9 %collective-permute-start.5 = (bf16[16,3072]{1,0:T(8,128)(2,1)S(1)}, bf16[16,3072]{1,0:T(8,128)(2,1)S(1)}, u32[]{:S(2)}, u32[]{:S(2)}) collective-permute-start(bf16[16,3072]{1,0:T(8,128)(2,1)S(1)} %add_terms.6.refs_0_), channel_id=1, source_target_pairs={{0,1},{1,0},{2,3},{3,2},{4,5},{5,4},{6,7},{7,6},{8,9},{9,8},{10,11... | collective-permute-start | bytes 294920 | tf_op jit(solution)/shard_map/cond/branch_1_fun/ppermute | solution.py:282
  44.1 30.4 %all-to-all-start = ((bf16[4,32,6144]{2,1,0:T(8,128)(2,1)}), bf16[4,32,6144]{2,1,0:T(8,128)(2,1)}, u32[]{:S(2)}, u32[]{:S(2)}) async-start(bf16[4,32,6144]{2,1,0:T(8,128)(2,1)} %row_terms.1), calls=%async_computation | async-start | bytes 3145728 | tf_op jit(solution)/shard_map/cond/branch_1_fun/all_to_all | solution.py:453
  48.5 7.7 %collective-permute-start = (bf16[16,3072]{1,0:T(8,128)(2,1)S(1)}, bf16[16,3072]{1,0:T(8,128)(2,1)S(1)}, u32[]{:S(2)}, u32[]{:S(2)}) collective-permute-start(bf16[16,3072]{1,0:T(8,128)(2,1)S(1)} %get-tuple-element.33.refs_0_), channel_id=1, source_target_pairs={{0,8},{4,12},{8,0},{12,4},{16,24},{20,28},{24,16},{28,20},{1,9},{5... | collective-permute-start | bytes 294920 | tf_op jit(solution)/shard_map/cond/branch_1_fun/cond/branch_1_fun/ppermute | solution.py:288
  56.2 18.3 %collective-permute-start.1 = (bf16[240,768]{1,0:T(8,128)(2,1)}, bf16[240,768]{1,0:T(8,128)(2,1)}, u32[]{:S(2)}, u32[]{:S(2)}) collective-permute-start(bf16[240,768]{1,0:T(8,128)(2,1)} %get-tuple-element.34), channel_id=1, source_target_pairs={{0,8},{4,12},{8,0},{12,4},{16,24},{20,28},{24,16},{28,20},{1,9},{5... | collective-permute-start | bytes 1105928 | tf_op jit(solution)/shard_map/cond/branch_1_fun/cond/branch_1_fun/ppermute | solution.py:288
  58.8 13.2 %collective-permute-start.2 = (bf16[16,3072]{1,0:T(8,128)(2,1)S(1)}, bf16[16,3072]{1,0:T(8,128)(2,1)S(1)}, u32[]{:S(2)}, u32[]{:S(2)}) collective-permute-start(bf16[16,3072]{1,0:T(8,128)(2,1)S(1)} %add_terms.4.refs_0_), channel_id=1, source_target_pairs={{0,16},{4,20},{8,24},{12,28},{16,0},{20,4},{24,8},{28,12},{1,17},{... | collective-permute-start | bytes 294920 | tf_op jit(solution)/shard_map/cond/branch_1_fun/cond/branch_1_fun/ppermute | solution.py:288
  72.7 1.8 %collective-permute-start.3 = (f32[16,3072]{1,0:T(8,128)}, f32[16,3072]{1,0:T(8,128)}, u32[]{:S(2)}, u32[]{:S(2)}) collective-permute-start(f32[16,3072]{1,0:T(8,128)} %add_terms.5), channel_id=1, source_target_pairs={{0,4},{4,0},{8,12},{12,8},{16,20},{20,16},{24,28},{28,24},{1,5},{5... | collective-permute-start | bytes 589832 | tf_op jit(solution)/shard_map/cond/branch_1_fun/cond/branch_1_fun/ppermute | solution.py:285

commit v5 on v4

--- a/solution.py
+++ b/solution.py
@@ -239,12 +239,13 @@
 
 def finish_kernel(sizes, at, *refs):
     exp_dev, hidden_units = sizes
-    pieces, (mine, theirs, through, back) = refs[:-9], refs[-9:-5]
+    pieces, halves, (through, back) = refs[:-11], refs[-11:-7], refs[-7:-5]
     grad_normed, router_grad, *outs = refs[-5:]
     core = at[2]
-    half = mine.shape[1]
-    router_grad[:, pl.ds(pl.multiple_of(core * half, LANES), half)] = mine[...]
-    router_grad[:, pl.ds(pl.multiple_of((1 - core) * half, LANES), half)] = theirs[...]
+    half = halves[0].shape[1]
+    for k in range(2):
+        lanes = pl.ds(pl.multiple_of((core ^ k) * half, LANES), half)
+        router_grad[:, lanes] = halves[2 * k][...].astype(F32) + halves[2 * k + 1][...].astype(F32)
     rows_total = through[...]
     for r in range(back.shape[0]):
         rows_total = rows_total + back[r].astype(F32)
@@ -415,12 +416,12 @@
 
     def sum_chips(values):
         total, near = values
-        for k in range(chip_rounds):
-            total = add_pair(total, over_chip, k, F32 if k == chip_rounds - 1 else BF16)
+        for k in range(chip_rounds - 1):
+            total = add_pair(total, over_chip, k)
             if k == 0:
                 near, total = lax.optimization_barrier((near, total))
-                near = over_chip(near, 1)
-        return near, total, over_core(total)
+        last = over_chip(total, 1 << (chip_rounds - 1))
+        return over_chip(near, 1), (total, last), (over_core(total), over_core(last))
 
     def as_one(function, values):
         outs = jax.eval_shape(function, values)
@@ -453,14 +454,14 @@
         back_rows = lax.all_to_all(row_pieces, "expert", 0, 0, tiled=True)
         return *as_one(sum_chips, (total, near)), through, back_rows
 
-    near, *back = as_one(way_back, (back_scores, packed, normed, router, tok_gate, tok_up, gate, up, chip_sums[1]))
+    near, mine, theirs, *back = as_one(way_back, (back_scores, packed, normed, router, tok_gate, tok_up, gate, up, chip_sums[1]))
     chip_pieces = [chip_sums[0], near] + [moved[k] for k in range(2, n_chip)]
     grad_normed, router_grad, *grads = call(
         functools.partial(finish_kernel, (exp_dev, hidden_units)),
         "finish",
         [shape((tokens_here, width), BF16), shape((experts, width), F32)]
         + [shape((hidden_units, exp_dev, piece), F32)] * 3,
-        (at, *chip_pieces, *back),
+        (at, *chip_pieces, *mine, *theirs, *back),
         scalars=True,
     )
     grads = [jnp.transpose(g, (1, 0, 2)) for g in grads]

time: 78.2 us -> 78 us (level)
    pallas_call x11 -> x10, Pallas kernels: 14.1 us -> 13.9 us  [call(): pl.pallas_call(kernel, out_shape=outs, in_specs=specs, out_specs=[pl.Bloc...]
    ppermute x3 -> x4, waiting for transfers between devices: 3.21 us -> 3.07 us  [over_core(): return lax.ppermute(value, 'dp', [(i, i ^ 1) for i in range(n_dp)])]
  transfers between devices with their start and end apart: 21 -> 22, of which waited for: 9 -> 9; matrix products, arithmetic and copies ran while one was open for 0% -> 0% of each run, Pallas kernels for 17% -> 17%
where the time goes in v5:
time: 78 us; the launch traced here: 77.3 us
  waiting for transfers between devices  28.1 us (36%)
  starting transfers between devices  27.7 us (36%)
  Pallas kernels  20.7 us (27%)
    ppermute x5, waiting for transfers between devices, over_chip(): return lax.ppermute(value, 'dp', [(i, i ^ 2 * k) for i in range(n_dp)])  17.2 us
    ppermute x12, starting transfers between devices, over_expert(): return lax.ppermute(value, 'expert', [(i, i ^ k) for i in range(n_expert)])  14.2 us
    pallas_call x10, Pallas kernels, call(): pl.pallas_call(kernel, out_shape=outs, in_specs=specs, out_specs=[pl.Bloc...  13.9 us
    ppermute x5, starting transfers between devices, over_chip(): return lax.ppermute(value, 'dp', [(i, i ^ 2 * k) for i in range(n_dp)])  8.96 us
    ppermute x12, waiting for transfers between devices, over_expert(): return lax.ppermute(value, 'expert', [(i, i ^ k) for i in range(n_expert)])  7.84 us
    pallas_call x1, Pallas kernels, on_device(): pl.pallas_call(functools.partial(prepare_kernel, blocks), out_shape=resul...  5.16 us
    all_to_all x1, starting transfers between devices, way_back(): back_rows = lax.all_to_all(row_pieces, 'expert', 0, 0, tiled=True)  4.35 us
    ppermute x4, waiting for transfers between devices, over_core(): return lax.ppermute(value, 'dp', [(i, i ^ 1) for i in range(n_dp)])  3.07 us
  transfers between devices with their start and end apart: 22, of which 9 were waited for; matrix products, arithmetic and copies ran while one was open for 0% of the time, Pallas kernels for 17%

profile of v5, /device:TPU:8, one launch (start us, length us, event | category | flops | bytes accessed | tf_op | source)
XLA Modules:
  0.0 77.3 jit_solution(15487888288198449755)
XLA Ops:
  0.6 1.6 %route.1 = (bf16[32,3072]{1,0:T(8,128)(2,1)S(1)}, bf16[32,3200]{1,0:T(8,128)(2,1)S(1)}) custom-call(s32[4,32]{1,0:T(4,128)} %bitcast.23, bf16[32,6144]{1,0:T(8,128)(2,1)} %refs_1_.1, bf16[16,6144]{1,0:T(8,128)(2,1)} %bitcast.21, bf16[32,6144]{1,0:T(8,128)(2,1)} %refs_3_.1), custom_call_target="tpu_custom_call" | custom-call | tf_op jit(solution)/shard_map/route/pallas_call | solution.py:312
  2.3 1.6 %collective-permute-start.13 = (bf16[32,3200]{1,0:T(8,128)(2,1)S(1)}, bf16[32,3200]{1,0:T(8,128)(2,1)S(1)}, u32[]{:S(2)}, u32[]{:S(2)}) collective-permute-start(bf16[32,3200]{1,0:T(8,128)(2,1)S(1)} %get-tuple-element.113.refs_4_.refs_0_), channel_id=1, source_target_pairs={{0,2},{1,3},{2,0},{3,1},{4,6},{5,7},{6,4},{7,5},{8,10},{9,11},{10,... | collective-permute-start | bytes 614408 | tf_op jit(solution)/shard_map/ppermute | solution.py:283
  3.8 1.5 %collective-permute-start.9 = (bf16[32,3072]{1,0:T(8,128)(2,1)S(1)}, bf16[32,3072]{1,0:T(8,128)(2,1)S(1)}, u32[]{:S(2)}, u32[]{:S(2)}) collective-permute-start(bf16[32,3072]{1,0:T(8,128)(2,1)S(1)} %get-tuple-element.112.refs_0_), channel_id=1, source_target_pairs={{0,1},{1,0},{2,3},{3,2},{4,5},{5,4},{6,7},{7,6},{8,9},{9,8},{10,11... | collective-permute-start | bytes 589832 | tf_op jit(solution)/shard_map/ppermute | solution.py:283
  5.9 3.3 %collective-permute-done.13.refs_6_.refs_2_ = bf16[32,3200]{1,0:T(8,128)(2,1)S(1)} collective-permute-done((bf16[32,3200]{1,0:T(8,128)(2,1)S(1)}, bf16[32,3200]{1,0:T(8,128)(2,1)S(1)}, u32[]{:S(2)}, u32[]{:S(2)}) %collective-permute-start.13) | collective-permute-done | bytes 204832 | tf_op jit(solution)/shard_map/ppermute | solution.py:283
  9.1 1.5 %collective-permute-start.14 = (bf16[32,3200]{1,0:T(8,128)(2,1)S(1)}, bf16[32,3200]{1,0:T(8,128)(2,1)S(1)}, u32[]{:S(2)}, u32[]{:S(2)}) collective-permute-start(bf16[32,3200]{1,0:T(8,128)(2,1)S(1)} %collective-permute-done.13.refs_6_.refs_2_), channel_id=1, source_target_pairs={{0,1},{1,0},{2,3},{3,2},{4,5},{5,4},{6,7},{7,6},{8,9},{9,8},{10,11... | collective-permute-start | bytes 614408 | tf_op jit(solution)/shard_map/ppermute | solution.py:283
  10.6 1.5 %collective-permute-start.10 = (bf16[32,3072]{1,0:T(8,128)(2,1)S(1)}, bf16[32,3072]{1,0:T(8,128)(2,1)S(1)}, u32[]{:S(2)}, u32[]{:S(2)}) collective-permute-start(bf16[32,3072]{1,0:T(8,128)(2,1)S(1)} %get-tuple-element.112.refs_0_), channel_id=1, source_target_pairs={{0,2},{1,3},{2,0},{3,1},{4,6},{5,7},{6,4},{7,5},{8,10},{9,11},{10,... | collective-permute-start | bytes 589832 | tf_op jit(solution)/shard_map/ppermute | solution.py:283
  12.7 5.2 %prepare.1 = (bf16[144,6144]{1,0:T(8,128)(2,1)S(1)}, bf16[80,6144]{1,0:T(8,128)(2,1)}, bf16[80,6144]{1,0:T(8,128)(2,1)}, bf16[80,6144]{1,0:T(8,128)(2,1)S(1)}, f...) custom-call(bf16[36,4,6144]{2,1,0:T(4,128)(2,1)} %bitcast.17, bf16[20,4,6144]{2,1,0:T(4,128)(2,1)} %bitcast.18, ...), custom_call_target="tpu_custom_call" | custom-call | tf_op jit(solution)/shard_map/prepare/pallas_call | solution.py:345
  18.2 2.1 %collective-permute-done.11.refs_3_ = bf16[32,3072]{1,0:T(8,128)(2,1)S(1)} collective-permute-done((bf16[32,3072]{1,0:T(8,128)(2,1)S(1)}, bf16[32,3072]{1,0:T(8,128)(2,1)S(1)}, u32[]{:S(2)}, u32[]{:S(2)}) %collective-permute-start.11) | collective-permute-done | bytes 196640 | tf_op jit(solution)/shard_map/ppermute | solution.py:283
  20.3 1.7 %experts.1 = (f32[32,128]{1,0:T(8,128)S(1)}, f32[32,128]{1,0:T(8,128)S(1)}, f32[32,128]{1,0:T(8,128)S(1)}, f32[32,128]{1,0:T(8,128)S(1)}, bf16[128,144]{1,0:T(8,...) custom-call(s32[3]{0:T(128)S(1)} %pad_add_fusion.at, ...), custom_call_target="tpu_custom_call" | custom-call | tf_op jit(solution)/shard_map/experts/pallas_call | solution.py:300
  22.0 1.4 %core_terms.1 = (bf16[128,80]{1,0:T(8,128)(2,1)S(1)}, bf16[128,80]{1,0:T(8,128)(2,1)S(1)}, bf16[80,144]{1,0:T(8,128)(2,1)S(1)}, bf16[80,144]{1,0:T(8,128)(2,1)S(...) custom-call(s32[3]{0:T(128)S(1)} %pad_add_fusion.at, ...), custom_call_target="tpu_custom_call" | custom-call | tf_op jit(solution)/shard_map/core_terms/pallas_call | solution.py:300
  24.0 1.5 %collective-permute-start.17 = (f32[32,128]{1,0:T(8,128)S(1)}, f32[32,128]{1,0:T(8,128)S(1)}, u32[]{:S(2)}, u32[]{:S(2)}) collective-permute-start(f32[32,128]{1,0:T(8,128)S(1)} %get-tuple-element.133), channel_id=1, source_target_pairs={{0,2},{1,3},{2,0},{3,1},{4,6},{5,7},{6,4},{7,5},{8,10},{9,11},{10,... | collective-permute-start | bytes 49160 | tf_op jit(solution)/shard_map/ppermute | solution.py:283
  25.6 1.4 %collective-permute-start.18 = (f32[32,128]{1,0:T(8,128)S(1)}, f32[32,128]{1,0:T(8,128)S(1)}, u32[]{:S(2)}, u32[]{:S(2)}) collective-permute-start(f32[32,128]{1,0:T(8,128)S(1)} %get-tuple-element.134), channel_id=1, source_target_pairs={{0,3},{1,2},{2,1},{3,0},{4,7},{5,6},{6,5},{7,4},{8,11},{9,10},{10,... | collective-permute-start | bytes 49160 | tf_op jit(solution)/shard_map/ppermute | solution.py:283
  27.0 1.1 %weight_terms.1.mine = f32[4,240,768]{2,1,0:T(8,128)S(1)} custom-call(s32[3]{0:T(128)S(1)} %pad_add_fusion.at, bf16[128,6144]{1,0:T(8,128)(2,1)S(1)} %get-tuple-element.117.refs_8_.arrived, bf16[144,6144]{1,0:T(8,128)(2,1)S(1)} %get-tuple-element.118.refs_9_.inputs, bf16[80,144]{1,0:T(8,128)(2,1)S(1)} %get-tuple-element.123.gate, ...), custom_call_target="tpu_custom_call" | custom-call | tf_op jit(solution)/shard_map/weight_terms/pallas_call | solution.py:300
  28.1 0.9 %core_sum.1 = (f32[240,768]{1,0:T(8,128)S(1)}, bf16[240,768]{1,0:T(8,128)(2,1)}, bf16[240,768]{1,0:T(8,128)(2,1)S(1)}, bf16[240,768]{1,0:T(8,128)(2,1)S(1)}) custom-call(f32[4,240,768]{2,1,0:T(8,128)S(1)} %weight_terms.1.mine, bf16[4,240,768]{2,1,0:T(8,128)(2,1)S(1)} %collective-permute-done.15.theirs), custom_call_target="tpu_custom_call" | custom-call | tf_op jit(solution)/shard_map/core_sum/pallas_call | solution.py:300
  29.1 1.1 %collective-permute-done.18 = f32[32,128]{1,0:T(8,128)S(1)} collective-permute-done((f32[32,128]{1,0:T(8,128)S(1)}, f32[32,128]{1,0:T(8,128)S(1)}, u32[]{:S(2)}, u32[]{:S(2)}) %collective-permute-start.18) | collective-permute-done | bytes 16416 | tf_op jit(solution)/shard_map/ppermute | solution.py:283
  30.2 2.6 %collective-permute-start.19 = (bf16[240,768]{1,0:T(8,128)(2,1)S(1)}, bf16[240,768]{1,0:T(8,128)(2,1)S(1)}, u32[]{:S(2)}, u32[]{:S(2)}) collective-permute-start(bf16[240,768]{1,0:T(8,128)(2,1)S(1)} %get-tuple-element.146), channel_id=1, source_target_pairs={{0,16},{4,20},{8,24},{12,28},{16,0},{20,4},{24,8},{28,12},{1,17},{... | collective-permute-start | bytes 1105928 | tf_op jit(solution)/shard_map/ppermute | solution.py:289
  32.8 41.5 %conditional.2 = (bf16[240,768]{1,0:T(8,128)(2,1)}, bf16[16,3072]{1,0:T(8,128)(2,1)}, bf16[16,3072]{1,0:T(8,128)(2,1)}, bf16[16,3072]{1,0:T(8,128)(2,1)}, bf16[1...) conditional(s32[]{:T(128)} %convert_element_type.6, () %tuple.28, (pred[]{:T(512)}, ...), branch_computations={%region_0.0_spmd, %region_1.0_spmd} | conditional | flops 1 | bytes 13664793 | solution.py:428
  32.8 1.8 %router_terms.1 = (f32[16,3072]{1,0:T(8,128)S(1)}, f32[16,3072]{1,0:T(8,128)S(1)}, f32[32,6144]{1,0:T(8,128)S(1)}) custom-call(s32[3]{0:T(128)S(1)} %get-tuple-element.37.at, f32[32,128]{1,0:T(8,128)S(1)} %get-tuple-element.42.refs_0_, f32[32,128]{1,0:T(8,128)S(1)} %get-tuple-element.43.refs_1_, f32[32,128]{1,0:T(8,128)S(1)} %get-tuple-element.44.refs_2_, ...), custom_call_target="tpu_custom_call" | custom-call | tf_op jit(solution)/shard_map/cond/branch_1_fun/router_terms/pallas_call | solution.py:300
  34.7 1.4 %collective-permute-done.5.refs_1_ = f32[16,3072]{1,0:T(8,128)S(1)} collective-permute-done((f32[16,3072]{1,0:T(8,128)S(1)}, f32[16,3072]{1,0:T(8,128)S(1)}, u32[]{:S(2)}, u32[]{:S(2)}) %collective-permute-start.5) | collective-permute-done | bytes 196640 | tf_op jit(solution)/shard_map/cond/branch_1_fun/ppermute | solution.py:286
  36.2 1.5 %collective-permute-start.8 = (bf16[16,3072]{1,0:T(8,128)(2,1)S(1)}, bf16[16,3072]{1,0:T(8,128)(2,1)S(1)}, u32[]{:S(2)}, u32[]{:S(2)}) collective-permute-start(bf16[16,3072]{1,0:T(8,128)(2,1)S(1)} %add_terms.4.refs_0_), channel_id=1, source_target_pairs={{0,3},{1,2},{2,1},{3,0},{4,7},{5,6},{6,5},{7,4},{8,11},{9,10},{10,... | collective-permute-start | bytes 294920 | tf_op jit(solution)/shard_map/cond/branch_1_fun/ppermute | solution.py:283
  37.7 1.5 %collective-permute-start.7 = (bf16[16,3072]{1,0:T(8,128)(2,1)S(1)}, bf16[16,3072]{1,0:T(8,128)(2,1)S(1)}, u32[]{:S(2)}, u32[]{:S(2)}) collective-permute-start(bf16[16,3072]{1,0:T(8,128)(2,1)S(1)} %add_terms.4.refs_0_), channel_id=1, source_target_pairs={{0,2},{1,3},{2,0},{3,1},{4,6},{5,7},{6,4},{7,5},{8,10},{9,11},{10,... | collective-permute-start | bytes 294920 | tf_op jit(solution)/shard_map/cond/branch_1_fun/ppermute | solution.py:283
  39.7 3.4 %row_terms.1 = bf16[4,32,6144]{2,1,0:T(8,128)(2,1)} custom-call(s32[3]{0:T(128)S(1)} %get-tuple-element.37.at, bf16[128,80]{1,0:T(8,128)(2,1)S(1)} %get-tuple-element.38.tok_gate, bf16[128,80]{1,0:T(8,128)(2,1)S(1)} %get-tuple-element.39.tok_up, bf16[80,6144]{1,0:T(8,128)(2,1)S(1)} %copy-done, bf16[80,6144]{1,0:T(8,128)(2,1)} %get-tuple-element.41.up, ...), custom_call_target="tpu_custom_call" | custom-call | tf_op jit(solution)/shard_map/cond/branch_1_fun/row_terms/pallas_call | solution.py:300
  43.1 1.0 %collective-permute-done.7.refs_2_ = bf16[16,3072]{1,0:T(8,128)(2,1)S(1)} collective-permute-done((bf16[16,3072]{1,0:T(8,128)(2,1)S(1)}, bf16[16,3072]{1,0:T(8,128)(2,1)S(1)}, u32[]{:S(2)}, u32[]{:S(2)}) %collective-permute-start.7) | collective-permute-done | bytes 98336 | tf_op jit(solution)/shard_map/cond/branch_1_fun/ppermute | solution.py:283
  44.1 4.4 %all-to-all-start = ((bf16[4,32,6144]{2,1,0:T(8,128)(2,1)}), bf16[4,32,6144]{2,1,0:T(8,128)(2,1)}, u32[]{:S(2)}, u32[]{:S(2)}) async-start(bf16[4,32,6144]{2,1,0:T(8,128)(2,1)} %row_terms.1), calls=%async_computation | async-start | bytes 3145728 | tf_op jit(solution)/shard_map/cond/branch_1_fun/all_to_all | solution.py:454
  48.5 25.8 %conditional = (bf16[240,768]{1,0:T(8,128)(2,1)}, bf16[16,3072]{1,0:T(8,128)(2,1)}, bf16[16,3072]{1,0:T(8,128)(2,1)}, bf16[16,3072]{1,0:T(8,128)(2,1)}, bf16[16,3072]{1,0:T(8,128)(2,1)}) conditional(s32[]{:T(128)} %convert_element_type.4, () %tuple.18, (bf16[16,3072]{1,0:T(8,128)(2,1)S(1)}, bf16[240,768]{1,0:T(8,128)(2,1)}) %tuple.20), branch_computations={%region_2.0_spmd, %region_3.0_spmd} | conditional | bytes 3047664 | solution.py:428
  48.5 1.9 %collective-permute-start = (bf16[16,3072]{1,0:T(8,128)(2,1)S(1)}, bf16[16,3072]{1,0:T(8,128)(2,1)S(1)}, u32[]{:S(2)}, u32[]{:S(2)}) collective-permute-start(bf16[16,3072]{1,0:T(8,128)(2,1)S(1)} %get-tuple-element.33.refs_0_), channel_id=1, source_target_pairs={{0,8},{4,12},{8,0},{12,4},{16,24},{20,28},{24,16},{28,20},{1,9},{5... | collective-permute-start | bytes 294920 | tf_op jit(solution)/shard_map/cond/branch_1_fun/cond/branch_1_fun/ppermute | solution.py:289
  50.3 5.9 %collective-permute-done.refs_1_ = bf16[16,3072]{1,0:T(8,128)(2,1)S(1)} collective-permute-done((bf16[16,3072]{1,0:T(8,128)(2,1)S(1)}, bf16[16,3072]{1,0:T(8,128)(2,1)S(1)}, u32[]{:S(2)}, u32[]{:S(2)}) %collective-permute-start) | collective-permute-done | bytes 98336 | tf_op jit(solution)/shard_map/cond/branch_1_fun/cond/branch_1_fun/ppermute | solution.py:289
  56.9 2.5 %collective-permute-start.1 = (bf16[240,768]{1,0:T(8,128)(2,1)}, bf16[240,768]{1,0:T(8,128)(2,1)}, u32[]{:S(2)}, u32[]{:S(2)}) collective-permute-start(bf16[240,768]{1,0:T(8,128)(2,1)} %get-tuple-element.34), channel_id=1, source_target_pairs={{0,8},{4,12},{8,0},{12,4},{16,24},{20,28},{24,16},{28,20},{1,9},{5... | collective-permute-start | bytes 1105928 | tf_op jit(solution)/shard_map/cond/branch_1_fun/cond/branch_1_fun/ppermute | solution.py:289
  59.3 2.0 %collective-permute-start.2 = (bf16[16,3072]{1,0:T(8,128)(2,1)}, bf16[16,3072]{1,0:T(8,128)(2,1)}, u32[]{:S(2)}, u32[]{:S(2)}) collective-permute-start(bf16[16,3072]{1,0:T(8,128)(2,1)} %add_terms.3), channel_id=1, source_target_pairs={{0,16},{4,20},{8,24},{12,28},{16,0},{20,4},{24,8},{28,12},{1,17},{... | collective-permute-start | bytes 294920 | tf_op jit(solution)/shard_map/cond/branch_1_fun/cond/branch_1_fun/ppermute | solution.py:289
  61.4 11.3 %collective-permute-done.2 = bf16[16,3072]{1,0:T(8,128)(2,1)} collective-permute-done((bf16[16,3072]{1,0:T(8,128)(2,1)}, bf16[16,3072]{1,0:T(8,128)(2,1)}, u32[]{:S(2)}, u32[]{:S(2)}) %collective-permute-start.2) | collective-permute-done | bytes 98336 | tf_op jit(solution)/shard_map/cond/branch_1_fun/cond/branch_1_fun/ppermute | solution.py:289
  72.7 1.6 %collective-permute-done.4 = bf16[16,3072]{1,0:T(8,128)(2,1)} collective-permute-done((bf16[16,3072]{1,0:T(8,128)(2,1)}, bf16[16,3072]{1,0:T(8,128)(2,1)}, u32[]{:S(2)}, u32[]{:S(2)}) %collective-permute-start.4) | collective-permute-done | bytes 98336 | tf_op jit(solution)/shard_map/cond/branch_1_fun/cond/branch_1_fun/ppermute | solution.py:286
  74.3 3.0 %finish.1 = (bf16[32,6144]{1,0:T(8,128)(2,1)}, f32[16,6144]{1,0:T(8,128)}, f32[20,4,768]{2,1,0:T(4,128)}, f32[20,4,768]{2,1,0:T(4,128)}, f32[20,4,768]{2,1,0:T(4,128)}) custom-call(s32[3]{0:T(128)S(1)} %pad_add_fusion.at, f32[240,768]{1,0:T(8,128)S(1)} %get-tuple-element.135.refs_0_, bf16[240,768]{1,0:T(8,128)(2,1)} %get-tuple-element.145.refs_1_, ...), custom_call_target="tpu_custom_call" | custom-call | tf_op jit(solution)/shard_map/finish/pallas_call | solution.py:300
  (31 shorter events, 3.5 us)
Async XLA Ops:
  2.3 6.9 %collective-permute-start.13 = (bf16[32,3200]{1,0:T(8,128)(2,1)S(1)}, bf16[32,3200]{1,0:T(8,128)(2,1)S(1)}, u32[]{:S(2)}, u32[]{:S(2)}) collective-permute-start(bf16[32,3200]{1,0:T(8,128)(2,1)S(1)} %get-tuple-element.113.refs_4_.refs_0_), channel_id=1, source_target_pairs={{0,2},{1,3},{2,0},{3,1},{4,6},{5,7},{6,4},{7,5},{8,10},{9,11},{10,... | collective-permute-start | bytes 614408 | tf_op jit(solution)/shard_map/ppermute | solution.py:283
  3.8 8.3 %collective-permute-start.9 = (bf16[32,3072]{1,0:T(8,128)(2,1)S(1)}, bf16[32,3072]{1,0:T(8,128)(2,1)S(1)}, u32[]{:S(2)}, u32[]{:S(2)}) collective-permute-start(bf16[32,3072]{1,0:T(8,128)(2,1)S(1)} %get-tuple-element.112.refs_0_), channel_id=1, source_target_pairs={{0,1},{1,0},{2,3},{3,2},{4,5},{5,4},{6,7},{7,6},{8,9},{9,8},{10,11... | collective-permute-start | bytes 589832 | tf_op jit(solution)/shard_map/ppermute | solution.py:283
  5.3 12.9 %collective-permute-start.12 = (bf16[32,3200]{1,0:T(8,128)(2,1)S(1)}, bf16[32,3200]{1,0:T(8,128)(2,1)S(1)}, u32[]{:S(2)}, u32[]{:S(2)}) collective-permute-start(bf16[32,3200]{1,0:T(8,128)(2,1)S(1)} %get-tuple-element.113.refs_4_.refs_0_), channel_id=1, source_target_pairs={{0,1},{1,0},{2,3},{3,2},{4,5},{5,4},{6,7},{7,6},{8,9},{9,8},{10,11... | collective-permute-start | bytes 614408 | tf_op jit(solution)/shard_map/ppermute | solution.py:283
  9.1 11.2 %collective-permute-start.14 = (bf16[32,3200]{1,0:T(8,128)(2,1)S(1)}, bf16[32,3200]{1,0:T(8,128)(2,1)S(1)}, u32[]{:S(2)}, u32[]{:S(2)}) collective-permute-start(bf16[32,3200]{1,0:T(8,128)(2,1)S(1)} %collective-permute-done.13.refs_6_.refs_2_), channel_id=1, source_target_pairs={{0,1},{1,0},{2,3},{3,2},{4,5},{5,4},{6,7},{7,6},{8,9},{9,8},{10,11... | collective-permute-start | bytes 614408 | tf_op jit(solution)/shard_map/ppermute | solution.py:283
  10.6 7.6 %collective-permute-start.10 = (bf16[32,3072]{1,0:T(8,128)(2,1)S(1)}, bf16[32,3072]{1,0:T(8,128)(2,1)S(1)}, u32[]{:S(2)}, u32[]{:S(2)}) collective-permute-start(bf16[32,3072]{1,0:T(8,128)(2,1)S(1)} %get-tuple-element.112.refs_0_), channel_id=1, source_target_pairs={{0,2},{1,3},{2,0},{3,1},{4,6},{5,7},{6,4},{7,5},{8,10},{9,11},{10,... | collective-permute-start | bytes 589832 | tf_op jit(solution)/shard_map/ppermute | solution.py:283
  12.1 8.2 %collective-permute-start.11 = (bf16[32,3072]{1,0:T(8,128)(2,1)S(1)}, bf16[32,3072]{1,0:T(8,128)(2,1)S(1)}, u32[]{:S(2)}, u32[]{:S(2)}) collective-permute-start(bf16[32,3072]{1,0:T(8,128)(2,1)S(1)} %collective-permute-done.9.refs_1_), channel_id=1, source_target_pairs={{0,2},{1,3},{2,0},{3,1},{4,6},{5,7},{6,4},{7,5},{8,10},{9,11},{10,... | collective-permute-start | bytes 589832 | tf_op jit(solution)/shard_map/ppermute | solution.py:283
  23.4 4.7 %collective-permute-start.15 = (bf16[4,240,768]{2,1,0:T(8,128)(2,1)S(1)}, bf16[4,240,768]{2,1,0:T(8,128)(2,1)S(1)}, u32[]{:S(2)}, u32[]{:S(2)}) collective-permute-start(bf16[4,240,768]{2,1,0:T(8,128)(2,1)S(1)} %get-tuple-element.126), channel_id=1, source_target_pairs={{0,4},{4,0},{8,12},{12,8},{16,20},{20,16},{24,28},{28,24},{1,5},{5... | collective-permute-start | bytes 4423688 | tf_op jit(solution)/shard_map/ppermute | solution.py:286
  23.4 5.6 %collective-permute-start.16 = (f32[32,128]{1,0:T(8,128)S(1)}, f32[32,128]{1,0:T(8,128)S(1)}, u32[]{:S(2)}, u32[]{:S(2)}) collective-permute-start(f32[32,128]{1,0:T(8,128)S(1)} %get-tuple-element.132), channel_id=1, source_target_pairs={{0,1},{1,0},{2,3},{3,2},{4,5},{5,4},{6,7},{7,6},{8,9},{9,8},{10,11... | collective-permute-start | bytes 49160 | tf_op jit(solution)/shard_map/ppermute | solution.py:283
  24.0 5.0 %collective-permute-start.17 = (f32[32,128]{1,0:T(8,128)S(1)}, f32[32,128]{1,0:T(8,128)S(1)}, u32[]{:S(2)}, u32[]{:S(2)}) collective-permute-start(f32[32,128]{1,0:T(8,128)S(1)} %get-tuple-element.133), channel_id=1, source_target_pairs={{0,2},{1,3},{2,0},{3,1},{4,6},{5,7},{6,4},{7,5},{8,10},{9,11},{10,... | collective-permute-start | bytes 49160 | tf_op jit(solution)/shard_map/ppermute | solution.py:283
  25.6 4.6 %collective-permute-start.18 = (f32[32,128]{1,0:T(8,128)S(1)}, f32[32,128]{1,0:T(8,128)S(1)}, u32[]{:S(2)}, u32[]{:S(2)}) collective-permute-start(f32[32,128]{1,0:T(8,128)S(1)} %get-tuple-element.134), channel_id=1, source_target_pairs={{0,3},{1,2},{2,1},{3,0},{4,7},{5,6},{6,5},{7,4},{8,11},{9,10},{10,... | collective-permute-start | bytes 49160 | tf_op jit(solution)/shard_map/ppermute | solution.py:283
  28.1 4.7 %copy-start.1 = (bf16[6144,16]{0,1:T(8,128)(2,1)S(1)}, bf16[6144,16]{0,1:T(8,128)(2,1)}, u32[]{:S(2)}) copy-start(bf16[6144,16]{0,1:T(8,128)(2,1)} %param.15) | copy-start | bytes 589828
  30.2 44.1 %collective-permute-start.19 = (bf16[240,768]{1,0:T(8,128)(2,1)S(1)}, bf16[240,768]{1,0:T(8,128)(2,1)S(1)}, u32[]{:S(2)}, u32[]{:S(2)}) collective-permute-start(bf16[240,768]{1,0:T(8,128)(2,1)S(1)} %get-tuple-element.146), channel_id=1, source_target_pairs={{0,16},{4,20},{8,24},{12,28},{16,0},{20,4},{24,8},{28,12},{1,17},{... | collective-permute-start | bytes 1105928 | tf_op jit(solution)/shard_map/ppermute | solution.py:289
  32.8 41.5 %collective-permute-start.20 = (bf16[240,768]{1,0:T(8,128)(2,1)S(1)}, bf16[240,768]{1,0:T(8,128)(2,1)S(1)}, u32[]{:S(2)}, u32[]{:S(2)}) collective-permute-start(bf16[240,768]{1,0:T(8,128)(2,1)S(1)} %get-tuple-element.147), channel_id=1, source_target_pairs={{0,24},{4,28},{8,16},{12,20},{16,8},{20,12},{24,0},{28,4},{1,25},{... | collective-permute-start | bytes 1105928 | tf_op jit(solution)/shard_map/ppermute | solution.py:289
  32.8 6.9 %copy-start = (bf16[80,6144]{1,0:T(8,128)(2,1)S(1)}, bf16[80,6144]{1,0:T(8,128)(2,1)}, u32[]{:S(2)}) copy-start(bf16[80,6144]{1,0:T(8,128)(2,1)} %get-tuple-element.40.gate) | copy-start | bytes 2949124 | tf_op jit(solution)/shard_map/cond
  34.6 1.5 %collective-permute-start.5 = (f32[16,3072]{1,0:T(8,128)S(1)}, f32[16,3072]{1,0:T(8,128)S(1)}, u32[]{:S(2)}, u32[]{:S(2)}) collective-permute-start(f32[16,3072]{1,0:T(8,128)S(1)} %get-tuple-element.49.behind), channel_id=1, source_target_pairs={{0,4},{4,0},{8,12},{12,8},{16,20},{20,16},{24,28},{28,24},{1,5},{5... | collective-permute-start | bytes 589832 | tf_op jit(solution)/shard_map/cond/branch_1_fun/ppermute | solution.py:286
  36.2 6.9 %collective-permute-start.8 = (bf16[16,3072]{1,0:T(8,128)(2,1)S(1)}, bf16[16,3072]{1,0:T(8,128)(2,1)S(1)}, u32[]{:S(2)}, u32[]{:S(2)}) collective-permute-start(bf16[16,3072]{1,0:T(8,128)(2,1)S(1)} %add_terms.4.refs_0_), channel_id=1, source_target_pairs={{0,3},{1,2},{2,1},{3,0},{4,7},{5,6},{6,5},{7,4},{8,11},{9,10},{10,... | collective-permute-start | bytes 294920 | tf_op jit(solution)/shard_map/cond/branch_1_fun/ppermute | solution.py:283
  37.7 6.4 %collective-permute-start.7 = (bf16[16,3072]{1,0:T(8,128)(2,1)S(1)}, bf16[16,3072]{1,0:T(8,128)(2,1)S(1)}, u32[]{:S(2)}, u32[]{:S(2)}) collective-permute-start(bf16[16,3072]{1,0:T(8,128)(2,1)S(1)} %add_terms.4.refs_0_), channel_id=1, source_target_pairs={{0,2},{1,3},{2,0},{3,1},{4,6},{5,7},{6,4},{7,5},{8,10},{9,11},{10,... | collective-permute-start | bytes 294920 | tf_op jit(solution)/shard_map/cond/branch_1_fun/ppermute | solution.py:283
  39.2 4.9 %collective-permute-start.6 = (bf16[16,3072]{1,0:T(8,128)(2,1)S(1)}, bf16[16,3072]{1,0:T(8,128)(2,1)S(1)}, u32[]{:S(2)}, u32[]{:S(2)}) collective-permute-start(bf16[16,3072]{1,0:T(8,128)(2,1)S(1)} %add_terms.4.refs_0_), channel_id=1, source_target_pairs={{0,1},{1,0},{2,3},{3,2},{4,5},{5,4},{6,7},{7,6},{8,9},{9,8},{10,11... | collective-permute-start | bytes 294920 | tf_op jit(solution)/shard_map/cond/branch_1_fun/ppermute | solution.py:283
  44.1 30.2 %all-to-all-start = ((bf16[4,32,6144]{2,1,0:T(8,128)(2,1)}), bf16[4,32,6144]{2,1,0:T(8,128)(2,1)}, u32[]{:S(2)}, u32[]{:S(2)}) async-start(bf16[4,32,6144]{2,1,0:T(8,128)(2,1)} %row_terms.1), calls=%async_computation | async-start | bytes 3145728 | tf_op jit(solution)/shard_map/cond/branch_1_fun/all_to_all | solution.py:454
  48.5 7.7 %collective-permute-start = (bf16[16,3072]{1,0:T(8,128)(2,1)S(1)}, bf16[16,3072]{1,0:T(8,128)(2,1)S(1)}, u32[]{:S(2)}, u32[]{:S(2)}) collective-permute-start(bf16[16,3072]{1,0:T(8,128)(2,1)S(1)} %get-tuple-element.33.refs_0_), channel_id=1, source_target_pairs={{0,8},{4,12},{8,0},{12,4},{16,24},{20,28},{24,16},{28,20},{1,9},{5... | collective-permute-start | bytes 294920 | tf_op jit(solution)/shard_map/cond/branch_1_fun/cond/branch_1_fun/ppermute | solution.py:289
  56.9 17.5 %collective-permute-start.1 = (bf16[240,768]{1,0:T(8,128)(2,1)}, bf16[240,768]{1,0:T(8,128)(2,1)}, u32[]{:S(2)}, u32[]{:S(2)}) collective-permute-start(bf16[240,768]{1,0:T(8,128)(2,1)} %get-tuple-element.34), channel_id=1, source_target_pairs={{0,8},{4,12},{8,0},{12,4},{16,24},{20,28},{24,16},{28,20},{1,9},{5... | collective-permute-start | bytes 1105928 | tf_op jit(solution)/shard_map/cond/branch_1_fun/cond/branch_1_fun/ppermute | solution.py:289
  59.3 13.3 %collective-permute-start.2 = (bf16[16,3072]{1,0:T(8,128)(2,1)}, bf16[16,3072]{1,0:T(8,128)(2,1)}, u32[]{:S(2)}, u32[]{:S(2)}) collective-permute-start(bf16[16,3072]{1,0:T(8,128)(2,1)} %add_terms.3), channel_id=1, source_target_pairs={{0,16},{4,20},{8,24},{12,28},{16,0},{20,4},{24,8},{28,12},{1,17},{... | collective-permute-start | bytes 294920 | tf_op jit(solution)/shard_map/cond/branch_1_fun/cond/branch_1_fun/ppermute | solution.py:289
  61.4 11.3 %collective-permute-start.3 = (bf16[16,3072]{1,0:T(8,128)(2,1)}, bf16[16,3072]{1,0:T(8,128)(2,1)}, u32[]{:S(2)}, u32[]{:S(2)}) collective-permute-start(bf16[16,3072]{1,0:T(8,128)(2,1)} %add_terms.3), channel_id=1, source_target_pairs={{0,4},{4,0},{8,12},{12,8},{16,20},{20,16},{24,28},{28,24},{1,5},{5... | collective-permute-start | bytes 294920 | tf_op jit(solution)/shard_map/cond/branch_1_fun/cond/branch_1_fun/ppermute | solution.py:286
  72.7 1.6 %collective-permute-start.4 = (bf16[16,3072]{1,0:T(8,128)(2,1)}, bf16[16,3072]{1,0:T(8,128)(2,1)}, u32[]{:S(2)}, u32[]{:S(2)}) collective-permute-start(bf16[16,3072]{1,0:T(8,128)(2,1)} %collective-permute-done.2), channel_id=1, source_target_pairs={{0,4},{4,0},{8,12},{12,8},{16,20},{20,16},{24,28},{28,24},{1,5},{5... | collective-permute-start | bytes 294920 | tf_op jit(solution)/shard_map/cond/branch_1_fun/cond/branch_1_fun/ppermute | solution.py:286

commit v6 on v5

--- a/solution.py
+++ b/solution.py
@@ -200,19 +200,21 @@
         outs[r][...] = (mine[r] + theirs[r].astype(F32)).astype(outs[r].dtype)
 
 
-def row_kernel(n_expert, blocks, at, tok_gate, tok_up, gate, up, behind, out):
-    del behind
+def row_kernel(n_expert, blocks, at, tok_gate, tok_up, gate, up, grad_logits, router, out):
+    high, low = split_high_low(grad_logits[...])
     size = tok_gate.shape[0] // n_expert
     step = gate.shape[1] // blocks
     for j in range(blocks):
         lanes = slice(j * step, (j + 1) * step)
         total = dot(tok_gate[...], gate[:, lanes], (1, 0)) + dot(tok_up[...], up[:, lanes], (1, 0))
+        through = dot(high, router[:, lanes], (1, 0)) + dot(low, router[:, lanes], (1, 0))
         for r in range(n_expert):
-            out[at[0] ^ r, :, lanes] = total[r * size : (r + 1) * size].astype(out.dtype)
+            piece = total[r * size : (r + 1) * size]
+            out[at[0] ^ r, :, lanes] = (piece if r else piece + through).astype(out.dtype)
 
 
 def router_kernel(experts, n_expert, at, *refs):
-    scores, (packed, normed, router, other, own, through) = refs[:n_expert], refs[n_expert:]
+    scores, (packed, normed, other, own, kept) = refs[:n_expert], refs[n_expert:]
     picked = scores[0][...]
     for s in scores[1:]:
         picked = picked + s[...]
@@ -227,7 +229,7 @@
     for out, part in ((other, 1 - core), (own, core)):
         values = normed[:, pl.ds(pl.multiple_of(part * half, LANES), half)]
         out[...] = dot(high, values, (0, 0)) + dot(low, values, (0, 0))
-    through[...] = dot(high, router[...], (1, 0)) + dot(low, router[...], (1, 0))
+    kept[...] = grad
 
 
 def terms_kernel(count, *refs):
@@ -239,15 +241,15 @@
 
 def finish_kernel(sizes, at, *refs):
     exp_dev, hidden_units = sizes
-    pieces, halves, (through, back) = refs[:-11], refs[-11:-7], refs[-7:-5]
+    pieces, halves, back = refs[:-10], refs[-10:-6], refs[-6]
     grad_normed, router_grad, *outs = refs[-5:]
     core = at[2]
     half = halves[0].shape[1]
     for k in range(2):
         lanes = pl.ds(pl.multiple_of((core ^ k) * half, LANES), half)
         router_grad[:, lanes] = halves[2 * k][...].astype(F32) + halves[2 * k + 1][...].astype(F32)
-    rows_total = through[...]
-    for r in range(back.shape[0]):
+    rows_total = back[0].astype(F32)
+    for r in range(1, back.shape[0]):
         rows_total = rows_total + back[r].astype(F32)
     grad_normed[...] = rows_total.astype(grad_normed.dtype)
     total = pieces[0][...]
@@ -429,20 +431,19 @@
 
     def way_back(values):
         back_scores, packed, normed, router, tok_gate, tok_up, gate, up, near = values
-        other, own, through = call(
+        other, own, grad_logits = call(
             functools.partial(router_kernel, experts, n_expert),
             "router_terms",
-            [shape((experts, half), F32)] * 2 + [shape((tokens_here, width), F32)],
-            (at, *back_scores, packed, normed, router),
+            [shape((experts, half), F32)] * 2 + [shape((tokens_here, experts), F32)],
+            (at, *back_scores, packed, normed),
             scalars=True,
         )
         (row_pieces,) = call(
             functools.partial(row_kernel, n_expert, 8),
             "row_terms",
             [shape((n_expert, tokens_here, width), BF16)],
-            (at, tok_gate, tok_up, gate, up, other),
+            (at, tok_gate, tok_up, gate, up, grad_logits, router),
             scalars=True,
-            behind=1,
         )
         total = add_terms([own, over_core(other)], BF16)
         if n_expert == 4:
@@ -452,7 +453,7 @@
                 total = add_pair(total, over_expert, k)
         row_pieces, total = lax.optimization_barrier((row_pieces, total))
         back_rows = lax.all_to_all(row_pieces, "expert", 0, 0, tiled=True)
-        return *as_one(sum_chips, (total, near)), through, back_rows
+        return *as_one(sum_chips, (total, near)), back_rows
 
     near, mine, theirs, *back = as_one(way_back, (back_scores, packed, normed, router, tok_gate, tok_up, gate, up, chip_sums[1]))
     chip_pieces = [chip_sums[0], near] + [moved[k] for k in range(2, n_chip)]

time: 78 us -> 77.7 us (level)
  Pallas kernels: 20.7 us -> 19.5 us
  waiting for transfers between devices: 28.1 us -> 29 us
    pallas_call x10, Pallas kernels: 13.9 us -> 12.7 us  [call(): pl.pallas_call(kernel, out_shape=outs, in_specs=specs, out_specs=[pl.Bloc...]
  transfers between devices with their start and end apart: 22 -> 22, of which waited for: 9 -> 9; matrix products, arithmetic and copies ran while one was open for 0% -> 0% of each run, Pallas kernels for 17% -> 15%
where the time goes in v6:
time: 77.7 us; the launch traced here: 77.1 us
  waiting for transfers between devices  29 us (37%)
  starting transfers between devices  27.7 us (36%)
  Pallas kernels  19.5 us (25%)
    ppermute x5, waiting for transfers between devices, over_chip(): return lax.ppermute(value, 'dp', [(i, i ^ 2 * k) for i in range(n_dp)])  17.3 us
    ppermute x12, starting transfers between devices, over_expert(): return lax.ppermute(value, 'expert', [(i, i ^ k) for i in range(n_expert)])  14.2 us
    pallas_call x10, Pallas kernels, call(): pl.pallas_call(kernel, out_shape=outs, in_specs=specs, out_specs=[pl.Bloc...  12.7 us
    ppermute x5, starting transfers between devices, over_chip(): return lax.ppermute(value, 'dp', [(i, i ^ 2 * k) for i in range(n_dp)])  8.93 us
    ppermute x12, waiting for transfers between devices, over_expert(): return lax.ppermute(value, 'expert', [(i, i ^ k) for i in range(n_expert)])  8.59 us
    pallas_call x1, Pallas kernels, on_device(): pl.pallas_call(functools.partial(prepare_kernel, blocks), out_shape=resul...  5.17 us
    all_to_all x1, starting transfers between devices, way_back(): back_rows = lax.all_to_all(row_pieces, 'expert', 0, 0, tiled=True)  4.35 us
    ppermute x4, waiting for transfers between devices, over_core(): return lax.ppermute(value, 'dp', [(i, i ^ 1) for i in range(n_dp)])  3.07 us
  transfers between devices with their start and end apart: 22, of which 9 were waited for; matrix products, arithmetic and copies ran while one was open for 0% of the time, Pallas kernels for 15%

profile of v6, /device:TPU:8, one launch (start us, length us, event | category | flops | bytes accessed | tf_op | source)
XLA Modules:
  0.0 77.1 jit_solution(7363665331223109223)
XLA Ops:
  0.6 1.6 %route.1 = (bf16[32,3072]{1,0:T(8,128)(2,1)S(1)}, bf16[32,3200]{1,0:T(8,128)(2,1)S(1)}) custom-call(s32[4,32]{1,0:T(4,128)} %bitcast.23, bf16[32,6144]{1,0:T(8,128)(2,1)} %refs_1_.1, bf16[16,6144]{1,0:T(8,128)(2,1)} %bitcast.21, bf16[32,6144]{1,0:T(8,128)(2,1)} %refs_3_.1), custom_call_target="tpu_custom_call" | custom-call | tf_op jit(solution)/shard_map/route/pallas_call | solution.py:314
  2.3 1.6 %collective-permute-start.13 = (bf16[32,3200]{1,0:T(8,128)(2,1)S(1)}, bf16[32,3200]{1,0:T(8,128)(2,1)S(1)}, u32[]{:S(2)}, u32[]{:S(2)}) collective-permute-start(bf16[32,3200]{1,0:T(8,128)(2,1)S(1)} %get-tuple-element.112.refs_4_.refs_0_), channel_id=1, source_target_pairs={{0,2},{1,3},{2,0},{3,1},{4,6},{5,7},{6,4},{7,5},{8,10},{9,11},{10,... | collective-permute-start | bytes 614408 | tf_op jit(solution)/shard_map/ppermute | solution.py:285
  3.8 1.5 %collective-permute-start.9 = (bf16[32,3072]{1,0:T(8,128)(2,1)S(1)}, bf16[32,3072]{1,0:T(8,128)(2,1)S(1)}, u32[]{:S(2)}, u32[]{:S(2)}) collective-permute-start(bf16[32,3072]{1,0:T(8,128)(2,1)S(1)} %get-tuple-element.111.refs_0_), channel_id=1, source_target_pairs={{0,1},{1,0},{2,3},{3,2},{4,5},{5,4},{6,7},{7,6},{8,9},{9,8},{10,11... | collective-permute-start | bytes 589832 | tf_op jit(solution)/shard_map/ppermute | solution.py:285
  5.9 3.3 %collective-permute-done.13.refs_6_.refs_2_ = bf16[32,3200]{1,0:T(8,128)(2,1)S(1)} collective-permute-done((bf16[32,3200]{1,0:T(8,128)(2,1)S(1)}, bf16[32,3200]{1,0:T(8,128)(2,1)S(1)}, u32[]{:S(2)}, u32[]{:S(2)}) %collective-permute-start.13) | collective-permute-done | bytes 204832 | tf_op jit(solution)/shard_map/ppermute | solution.py:285
  9.1 1.5 %collective-permute-start.14 = (bf16[32,3200]{1,0:T(8,128)(2,1)S(1)}, bf16[32,3200]{1,0:T(8,128)(2,1)S(1)}, u32[]{:S(2)}, u32[]{:S(2)}) collective-permute-start(bf16[32,3200]{1,0:T(8,128)(2,1)S(1)} %collective-permute-done.13.refs_6_.refs_2_), channel_id=1, source_target_pairs={{0,1},{1,0},{2,3},{3,2},{4,5},{5,4},{6,7},{7,6},{8,9},{9,8},{10,11... | collective-permute-start | bytes 614408 | tf_op jit(solution)/shard_map/ppermute | solution.py:285
  10.6 1.5 %collective-permute-start.10 = (bf16[32,3072]{1,0:T(8,128)(2,1)S(1)}, bf16[32,3072]{1,0:T(8,128)(2,1)S(1)}, u32[]{:S(2)}, u32[]{:S(2)}) collective-permute-start(bf16[32,3072]{1,0:T(8,128)(2,1)S(1)} %get-tuple-element.111.refs_0_), channel_id=1, source_target_pairs={{0,2},{1,3},{2,0},{3,1},{4,6},{5,7},{6,4},{7,5},{8,10},{9,11},{10,... | collective-permute-start | bytes 589832 | tf_op jit(solution)/shard_map/ppermute | solution.py:285
  12.7 5.2 %prepare.1 = (bf16[144,6144]{1,0:T(8,128)(2,1)S(1)}, bf16[80,6144]{1,0:T(8,128)(2,1)}, bf16[80,6144]{1,0:T(8,128)(2,1)}, bf16[80,6144]{1,0:T(8,128)(2,1)S(1)}, f...) custom-call(bf16[36,4,6144]{2,1,0:T(4,128)(2,1)} %bitcast.17, bf16[20,4,6144]{2,1,0:T(4,128)(2,1)} %bitcast.18, ...), custom_call_target="tpu_custom_call" | custom-call | tf_op jit(solution)/shard_map/prepare/pallas_call | solution.py:347
  18.2 2.1 %collective-permute-done.11.refs_3_ = bf16[32,3072]{1,0:T(8,128)(2,1)S(1)} collective-permute-done((bf16[32,3072]{1,0:T(8,128)(2,1)S(1)}, bf16[32,3072]{1,0:T(8,128)(2,1)S(1)}, u32[]{:S(2)}, u32[]{:S(2)}) %collective-permute-start.11) | collective-permute-done | bytes 196640 | tf_op jit(solution)/shard_map/ppermute | solution.py:285
  20.3 1.7 %experts.1 = (f32[32,128]{1,0:T(8,128)S(1)}, f32[32,128]{1,0:T(8,128)S(1)}, f32[32,128]{1,0:T(8,128)S(1)}, f32[32,128]{1,0:T(8,128)S(1)}, bf16[128,144]{1,0:T(8,...) custom-call(s32[3]{0:T(128)S(1)} %pad_add_fusion.at, ...), custom_call_target="tpu_custom_call" | custom-call | tf_op jit(solution)/shard_map/experts/pallas_call | solution.py:302
  22.0 1.4 %core_terms.1 = (bf16[128,80]{1,0:T(8,128)(2,1)S(1)}, bf16[128,80]{1,0:T(8,128)(2,1)S(1)}, bf16[80,144]{1,0:T(8,128)(2,1)S(1)}, bf16[80,144]{1,0:T(8,128)(2,1)S(...) custom-call(s32[3]{0:T(128)S(1)} %pad_add_fusion.at, ...), custom_call_target="tpu_custom_call" | custom-call | tf_op jit(solution)/shard_map/core_terms/pallas_call | solution.py:302
  24.1 1.5 %collective-permute-start.17 = (f32[32,128]{1,0:T(8,128)S(1)}, f32[32,128]{1,0:T(8,128)S(1)}, u32[]{:S(2)}, u32[]{:S(2)}) collective-permute-start(f32[32,128]{1,0:T(8,128)S(1)} %get-tuple-element.132), channel_id=1, source_target_pairs={{0,2},{1,3},{2,0},{3,1},{4,6},{5,7},{6,4},{7,5},{8,10},{9,11},{10,... | collective-permute-start | bytes 49160 | tf_op jit(solution)/shard_map/ppermute | solution.py:285
  25.6 1.4 %collective-permute-start.18 = (f32[32,128]{1,0:T(8,128)S(1)}, f32[32,128]{1,0:T(8,128)S(1)}, u32[]{:S(2)}, u32[]{:S(2)}) collective-permute-start(f32[32,128]{1,0:T(8,128)S(1)} %get-tuple-element.133), channel_id=1, source_target_pairs={{0,3},{1,2},{2,1},{3,0},{4,7},{5,6},{6,5},{7,4},{8,11},{9,10},{10,... | collective-permute-start | bytes 49160 | tf_op jit(solution)/shard_map/ppermute | solution.py:285
  27.0 1.1 %weight_terms.1.mine = f32[4,240,768]{2,1,0:T(8,128)S(1)} custom-call(s32[3]{0:T(128)S(1)} %pad_add_fusion.at, bf16[128,6144]{1,0:T(8,128)(2,1)S(1)} %get-tuple-element.116.refs_8_.arrived, bf16[144,6144]{1,0:T(8,128)(2,1)S(1)} %get-tuple-element.117.refs_9_.inputs, bf16[80,144]{1,0:T(8,128)(2,1)S(1)} %get-tuple-element.122.gate, ...), custom_call_target="tpu_custom_call" | custom-call | tf_op jit(solution)/shard_map/weight_terms/pallas_call | solution.py:302
  28.4 1.8 %collective-permute-done.18 = f32[32,128]{1,0:T(8,128)S(1)} collective-permute-done((f32[32,128]{1,0:T(8,128)S(1)}, f32[32,128]{1,0:T(8,128)S(1)}, u32[]{:S(2)}, u32[]{:S(2)}) %collective-permute-start.18) | collective-permute-done | bytes 16416 | tf_op jit(solution)/shard_map/ppermute | solution.py:285
  30.2 2.6 %collective-permute-start.19 = (bf16[240,768]{1,0:T(8,128)(2,1)S(1)}, bf16[240,768]{1,0:T(8,128)(2,1)S(1)}, u32[]{:S(2)}, u32[]{:S(2)}) collective-permute-start(bf16[240,768]{1,0:T(8,128)(2,1)S(1)} %get-tuple-element.145), channel_id=1, source_target_pairs={{0,16},{4,20},{8,24},{12,28},{16,0},{20,4},{24,8},{28,12},{1,17},{... | collective-permute-start | bytes 1105928 | tf_op jit(solution)/shard_map/ppermute | solution.py:291
  32.8 41.3 %conditional.2 = (bf16[240,768]{1,0:T(8,128)(2,1)}, bf16[16,3072]{1,0:T(8,128)(2,1)}, bf16[16,3072]{1,0:T(8,128)(2,1)}, bf16[16,3072]{1,0:T(8,128)(2,1)}, bf16[1...) conditional(s32[]{:T(128)} %convert_element_type.6, () %tuple.28, (pred[]{:T(512)}, s32[3]{0:T(128)S(1)}, ...), branch_computations={%region_0.0_spmd, %region_1.0_spmd} | conditional | flops 1 | bytes 13664785 | solution.py:430
  32.8 1.1 %router_terms.1 = (f32[16,3072]{1,0:T(8,128)S(1)}, f32[16,3072]{1,0:T(8,128)S(1)}, f32[32,16]{1,0:T(8,128)S(1)}) custom-call(s32[3]{0:T(128)S(1)} %get-tuple-element.37.at, f32[32,128]{1,0:T(8,128)S(1)} %get-tuple-element.42.refs_0_, f32[32,128]{1,0:T(8,128)S(1)} %get-tuple-element.43.refs_1_, f32[32,128]{1,0:T(8,128)S(1)} %get-tuple-element.44.refs_2_, ...), custom_call_target="tpu_custom_call" | custom-call | tf_op jit(solution)/shard_map/cond/branch_1_fun/router_terms/pallas_call | solution.py:302
  34.0 1.4 %collective-permute-done.5.refs_1_ = f32[16,3072]{1,0:T(8,128)S(1)} collective-permute-done((f32[16,3072]{1,0:T(8,128)S(1)}, f32[16,3072]{1,0:T(8,128)S(1)}, u32[]{:S(2)}, u32[]{:S(2)}) %collective-permute-start.5) | collective-permute-done | bytes 196640 | tf_op jit(solution)/shard_map/cond/branch_1_fun/ppermute | solution.py:288
  35.4 1.6 %collective-permute-start.6 = (bf16[16,3072]{1,0:T(8,128)(2,1)S(1)}, bf16[16,3072]{1,0:T(8,128)(2,1)S(1)}, u32[]{:S(2)}, u32[]{:S(2)}) collective-permute-start(bf16[16,3072]{1,0:T(8,128)(2,1)S(1)} %add_terms.4.refs_0_), channel_id=1, source_target_pairs={{0,1},{1,0},{2,3},{3,2},{4,5},{5,4},{6,7},{7,6},{8,9},{9,8},{10,11... | collective-permute-start | bytes 294920 | tf_op jit(solution)/shard_map/cond/branch_1_fun/ppermute | solution.py:285
  37.5 1.5 %collective-permute-start.8 = (bf16[16,3072]{1,0:T(8,128)(2,1)S(1)}, bf16[16,3072]{1,0:T(8,128)(2,1)S(1)}, u32[]{:S(2)}, u32[]{:S(2)}) collective-permute-start(bf16[16,3072]{1,0:T(8,128)(2,1)S(1)} %add_terms.4.refs_0_), channel_id=1, source_target_pairs={{0,3},{1,2},{2,1},{3,0},{4,7},{5,6},{6,5},{7,4},{8,11},{9,10},{10,... | collective-permute-start | bytes 294920 | tf_op jit(solution)/shard_map/cond/branch_1_fun/ppermute | solution.py:285
  39.0 3.6 %row_terms.1 = bf16[4,32,6144]{2,1,0:T(8,128)(2,1)} custom-call(s32[3]{0:T(128)S(1)} %get-tuple-element.37.at, bf16[128,80]{1,0:T(8,128)(2,1)S(1)} %get-tuple-element.38.tok_gate, bf16[128,80]{1,0:T(8,128)(2,1)S(1)} %get-tuple-element.39.tok_up, bf16[80,6144]{1,0:T(8,128)(2,1)S(1)} %copy-done.1, bf16[80,6144]{1,0:T(8,128)(2,1)} %get-tuple-element.41.up, ...), custom_call_target="tpu_custom_call" | custom-call | tf_op jit(solution)/shard_map/cond/branch_1_fun/row_terms/pallas_call | solution.py:302
  42.6 1.1 %collective-permute-done.7.refs_2_ = bf16[16,3072]{1,0:T(8,128)(2,1)S(1)} collective-permute-done((bf16[16,3072]{1,0:T(8,128)(2,1)S(1)}, bf16[16,3072]{1,0:T(8,128)(2,1)S(1)}, u32[]{:S(2)}, u32[]{:S(2)}) %collective-permute-start.7) | collective-permute-done | bytes 98336 | tf_op jit(solution)/shard_map/cond/branch_1_fun/ppermute | solution.py:285
  43.8 4.3 %all-to-all-start = ((bf16[4,32,6144]{2,1,0:T(8,128)(2,1)}), bf16[4,32,6144]{2,1,0:T(8,128)(2,1)}, u32[]{:S(2)}, u32[]{:S(2)}) async-start(bf16[4,32,6144]{2,1,0:T(8,128)(2,1)} %row_terms.1), calls=%async_computation | async-start | bytes 3145728 | tf_op jit(solution)/shard_map/cond/branch_1_fun/all_to_all | solution.py:455
  48.1 26.0 %conditional = (bf16[240,768]{1,0:T(8,128)(2,1)}, bf16[16,3072]{1,0:T(8,128)(2,1)}, bf16[16,3072]{1,0:T(8,128)(2,1)}, bf16[16,3072]{1,0:T(8,128)(2,1)}, bf16[16,3072]{1,0:T(8,128)(2,1)}) conditional(s32[]{:T(128)} %convert_element_type.4, () %tuple.18, (bf16[16,3072]{1,0:T(8,128)(2,1)S(1)}, bf16[240,768]{1,0:T(8,128)(2,1)S(1)}) %tuple.20), branch_computations={%region_2.0_spmd, %region_3.0_spmd} | conditional | bytes 3047664 | solution.py:430
  48.1 1.8 %collective-permute-start = (bf16[16,3072]{1,0:T(8,128)(2,1)S(1)}, bf16[16,3072]{1,0:T(8,128)(2,1)S(1)}, u32[]{:S(2)}, u32[]{:S(2)}) collective-permute-start(bf16[16,3072]{1,0:T(8,128)(2,1)S(1)} %get-tuple-element.33.refs_0_), channel_id=1, source_target_pairs={{0,8},{4,12},{8,0},{12,4},{16,24},{20,28},{24,16},{28,20},{1,9},{5... | collective-permute-start | bytes 294920 | tf_op jit(solution)/shard_map/cond/branch_1_fun/cond/branch_1_fun/ppermute | solution.py:291
  50.0 6.3 %collective-permute-done.refs_1_ = bf16[16,3072]{1,0:T(8,128)(2,1)S(1)} collective-permute-done((bf16[16,3072]{1,0:T(8,128)(2,1)S(1)}, bf16[16,3072]{1,0:T(8,128)(2,1)S(1)}, u32[]{:S(2)}, u32[]{:S(2)}) %collective-permute-start) | collective-permute-done | bytes 98336 | tf_op jit(solution)/shard_map/cond/branch_1_fun/cond/branch_1_fun/ppermute | solution.py:291
  56.2 0.7 add_terms.3
  56.9 2.5 %collective-permute-start.1 = (bf16[240,768]{1,0:T(8,128)(2,1)S(1)}, bf16[240,768]{1,0:T(8,128)(2,1)}, u32[]{:S(2)}, u32[]{:S(2)}) collective-permute-start(bf16[240,768]{1,0:T(8,128)(2,1)S(1)} %get-tuple-element.34), channel_id=1, source_target_pairs={{0,8},{4,12},{8,0},{12,4},{16,24},{20,28},{24,16},{28,20},{1,9},{5... | collective-permute-start | bytes 1105928 | tf_op jit(solution)/shard_map/cond/branch_1_fun/cond/branch_1_fun/ppermute | solution.py:291
  59.4 2.0 %collective-permute-start.2 = (bf16[16,3072]{1,0:T(8,128)(2,1)}, bf16[16,3072]{1,0:T(8,128)(2,1)}, u32[]{:S(2)}, u32[]{:S(2)}) collective-permute-start(bf16[16,3072]{1,0:T(8,128)(2,1)} %add_terms.3), channel_id=1, source_target_pairs={{0,16},{4,20},{8,24},{12,28},{16,0},{20,4},{24,8},{28,12},{1,17},{... | collective-permute-start | bytes 294920 | tf_op jit(solution)/shard_map/cond/branch_1_fun/cond/branch_1_fun/ppermute | solution.py:291
  61.4 11.1 %collective-permute-done.2 = bf16[16,3072]{1,0:T(8,128)(2,1)} collective-permute-done((bf16[16,3072]{1,0:T(8,128)(2,1)}, bf16[16,3072]{1,0:T(8,128)(2,1)}, u32[]{:S(2)}, u32[]{:S(2)}) %collective-permute-start.2) | collective-permute-done | bytes 98336 | tf_op jit(solution)/shard_map/cond/branch_1_fun/cond/branch_1_fun/ppermute | solution.py:291
  72.5 1.6 %collective-permute-done.4 = bf16[16,3072]{1,0:T(8,128)(2,1)} collective-permute-done((bf16[16,3072]{1,0:T(8,128)(2,1)}, bf16[16,3072]{1,0:T(8,128)(2,1)}, u32[]{:S(2)}, u32[]{:S(2)}) %collective-permute-start.4) | collective-permute-done | bytes 98336 | tf_op jit(solution)/shard_map/cond/branch_1_fun/cond/branch_1_fun/ppermute | solution.py:288
  74.2 2.9 %finish.1 = (bf16[32,6144]{1,0:T(8,128)(2,1)}, f32[16,6144]{1,0:T(8,128)}, f32[20,4,768]{2,1,0:T(4,128)}, f32[20,4,768]{2,1,0:T(4,128)}, f32[20,4,768]{2,1,0:T(4,128)}) custom-call(s32[3]{0:T(128)S(1)} %pad_add_fusion.at, f32[240,768]{1,0:T(8,128)S(1)} %get-tuple-element.134.refs_0_, bf16[240,768]{1,0:T(8,128)(2,1)} %get-tuple-element.144.refs_1_, ...), custom_call_target="tpu_custom_call" | custom-call | tf_op jit(solution)/shard_map/finish/pallas_call | solution.py:302
  (33 shorter events, 3.1 us)
Async XLA Ops:
  2.3 6.9 %collective-permute-start.13 = (bf16[32,3200]{1,0:T(8,128)(2,1)S(1)}, bf16[32,3200]{1,0:T(8,128)(2,1)S(1)}, u32[]{:S(2)}, u32[]{:S(2)}) collective-permute-start(bf16[32,3200]{1,0:T(8,128)(2,1)S(1)} %get-tuple-element.112.refs_4_.refs_0_), channel_id=1, source_target_pairs={{0,2},{1,3},{2,0},{3,1},{4,6},{5,7},{6,4},{7,5},{8,10},{9,11},{10,... | collective-permute-start | bytes 614408 | tf_op jit(solution)/shard_map/ppermute | solution.py:285
  3.8 8.3 %collective-permute-start.9 = (bf16[32,3072]{1,0:T(8,128)(2,1)S(1)}, bf16[32,3072]{1,0:T(8,128)(2,1)S(1)}, u32[]{:S(2)}, u32[]{:S(2)}) collective-permute-start(bf16[32,3072]{1,0:T(8,128)(2,1)S(1)} %get-tuple-element.111.refs_0_), channel_id=1, source_target_pairs={{0,1},{1,0},{2,3},{3,2},{4,5},{5,4},{6,7},{7,6},{8,9},{9,8},{10,11... | collective-permute-start | bytes 589832 | tf_op jit(solution)/shard_map/ppermute | solution.py:285
  5.3 12.9 %collective-permute-start.12 = (bf16[32,3200]{1,0:T(8,128)(2,1)S(1)}, bf16[32,3200]{1,0:T(8,128)(2,1)S(1)}, u32[]{:S(2)}, u32[]{:S(2)}) collective-permute-start(bf16[32,3200]{1,0:T(8,128)(2,1)S(1)} %get-tuple-element.112.refs_4_.refs_0_), channel_id=1, source_target_pairs={{0,1},{1,0},{2,3},{3,2},{4,5},{5,4},{6,7},{7,6},{8,9},{9,8},{10,11... | collective-permute-start | bytes 614408 | tf_op jit(solution)/shard_map/ppermute | solution.py:285
  9.1 11.2 %collective-permute-start.14 = (bf16[32,3200]{1,0:T(8,128)(2,1)S(1)}, bf16[32,3200]{1,0:T(8,128)(2,1)S(1)}, u32[]{:S(2)}, u32[]{:S(2)}) collective-permute-start(bf16[32,3200]{1,0:T(8,128)(2,1)S(1)} %collective-permute-done.13.refs_6_.refs_2_), channel_id=1, source_target_pairs={{0,1},{1,0},{2,3},{3,2},{4,5},{5,4},{6,7},{7,6},{8,9},{9,8},{10,11... | collective-permute-start | bytes 614408 | tf_op jit(solution)/shard_map/ppermute | solution.py:285
  10.6 7.6 %collective-permute-start.10 = (bf16[32,3072]{1,0:T(8,128)(2,1)S(1)}, bf16[32,3072]{1,0:T(8,128)(2,1)S(1)}, u32[]{:S(2)}, u32[]{:S(2)}) collective-permute-start(bf16[32,3072]{1,0:T(8,128)(2,1)S(1)} %get-tuple-element.111.refs_0_), channel_id=1, source_target_pairs={{0,2},{1,3},{2,0},{3,1},{4,6},{5,7},{6,4},{7,5},{8,10},{9,11},{10,... | collective-permute-start | bytes 589832 | tf_op jit(solution)/shard_map/ppermute | solution.py:285
  12.1 8.2 %collective-permute-start.11 = (bf16[32,3072]{1,0:T(8,128)(2,1)S(1)}, bf16[32,3072]{1,0:T(8,128)(2,1)S(1)}, u32[]{:S(2)}, u32[]{:S(2)}) collective-permute-start(bf16[32,3072]{1,0:T(8,128)(2,1)S(1)} %collective-permute-done.9.refs_1_), channel_id=1, source_target_pairs={{0,2},{1,3},{2,0},{3,1},{4,6},{5,7},{6,4},{7,5},{8,10},{9,11},{10,... | collective-permute-start | bytes 589832 | tf_op jit(solution)/shard_map/ppermute | solution.py:285
  23.4 4.8 %collective-permute-start.15 = (bf16[4,240,768]{2,1,0:T(8,128)(2,1)S(1)}, bf16[4,240,768]{2,1,0:T(8,128)(2,1)S(1)}, u32[]{:S(2)}, u32[]{:S(2)}) collective-permute-start(bf16[4,240,768]{2,1,0:T(8,128)(2,1)S(1)} %get-tuple-element.125), channel_id=1, source_target_pairs={{0,4},{4,0},{8,12},{12,8},{16,20},{20,16},{24,28},{28,24},{1,5},{5... | collective-permute-start | bytes 4423688 | tf_op jit(solution)/shard_map/ppermute | solution.py:288
  23.5 4.9 %collective-permute-start.16 = (f32[32,128]{1,0:T(8,128)S(1)}, f32[32,128]{1,0:T(8,128)S(1)}, u32[]{:S(2)}, u32[]{:S(2)}) collective-permute-start(f32[32,128]{1,0:T(8,128)S(1)} %get-tuple-element.131), channel_id=1, source_target_pairs={{0,1},{1,0},{2,3},{3,2},{4,5},{5,4},{6,7},{7,6},{8,9},{9,8},{10,11... | collective-permute-start | bytes 49160 | tf_op jit(solution)/shard_map/ppermute | solution.py:285
  24.1 4.3 %collective-permute-start.17 = (f32[32,128]{1,0:T(8,128)S(1)}, f32[32,128]{1,0:T(8,128)S(1)}, u32[]{:S(2)}, u32[]{:S(2)}) collective-permute-start(f32[32,128]{1,0:T(8,128)S(1)} %get-tuple-element.132), channel_id=1, source_target_pairs={{0,2},{1,3},{2,0},{3,1},{4,6},{5,7},{6,4},{7,5},{8,10},{9,11},{10,... | collective-permute-start | bytes 49160 | tf_op jit(solution)/shard_map/ppermute | solution.py:285
  25.6 4.6 %collective-permute-start.18 = (f32[32,128]{1,0:T(8,128)S(1)}, f32[32,128]{1,0:T(8,128)S(1)}, u32[]{:S(2)}, u32[]{:S(2)}) collective-permute-start(f32[32,128]{1,0:T(8,128)S(1)} %get-tuple-element.133), channel_id=1, source_target_pairs={{0,3},{1,2},{2,1},{3,0},{4,7},{5,6},{6,5},{7,4},{8,11},{9,10},{10,... | collective-permute-start | bytes 49160 | tf_op jit(solution)/shard_map/ppermute | solution.py:285
  28.1 4.7 %copy-start = (bf16[32,6144]{1,0:T(8,128)(2,1)S(1)}, bf16[32,6144]{1,0:T(8,128)(2,1)}, u32[]{:S(2)}) copy-start(bf16[32,6144]{1,0:T(8,128)(2,1)} %refs_1_.1) | copy-start | bytes 1179652
  28.1 4.7 %copy-start.2 = (bf16[6144,16]{0,1:T(8,128)(2,1)S(1)}, bf16[6144,16]{0,1:T(8,128)(2,1)}, u32[]{:S(2)}) copy-start(bf16[6144,16]{0,1:T(8,128)(2,1)} %param.15) | copy-start | bytes 589828
  30.2 43.9 %collective-permute-start.19 = (bf16[240,768]{1,0:T(8,128)(2,1)S(1)}, bf16[240,768]{1,0:T(8,128)(2,1)S(1)}, u32[]{:S(2)}, u32[]{:S(2)}) collective-permute-start(bf16[240,768]{1,0:T(8,128)(2,1)S(1)} %get-tuple-element.145), channel_id=1, source_target_pairs={{0,16},{4,20},{8,24},{12,28},{16,0},{20,4},{24,8},{28,12},{1,17},{... | collective-permute-start | bytes 1105928 | tf_op jit(solution)/shard_map/ppermute | solution.py:291
  32.8 41.3 %collective-permute-start.20 = (bf16[240,768]{1,0:T(8,128)(2,1)S(1)}, bf16[240,768]{1,0:T(8,128)(2,1)S(1)}, u32[]{:S(2)}, u32[]{:S(2)}) collective-permute-start(bf16[240,768]{1,0:T(8,128)(2,1)S(1)} %get-tuple-element.146), channel_id=1, source_target_pairs={{0,24},{4,28},{8,16},{12,20},{16,8},{20,12},{24,0},{28,4},{1,25},{... | collective-permute-start | bytes 1105928 | tf_op jit(solution)/shard_map/ppermute | solution.py:291
  32.8 6.2 %copy-start.1 = (bf16[80,6144]{1,0:T(8,128)(2,1)S(1)}, bf16[80,6144]{1,0:T(8,128)(2,1)}, u32[]{:S(2)}) copy-start(bf16[80,6144]{1,0:T(8,128)(2,1)} %get-tuple-element.40.gate) | copy-start | bytes 2949124 | tf_op jit(solution)/shard_map/cond
  33.9 1.5 %collective-permute-start.5 = (f32[16,3072]{1,0:T(8,128)S(1)}, f32[16,3072]{1,0:T(8,128)S(1)}, u32[]{:S(2)}, u32[]{:S(2)}) collective-permute-start(f32[16,3072]{1,0:T(8,128)S(1)} %get-tuple-element.51), channel_id=1, source_target_pairs={{0,4},{4,0},{8,12},{12,8},{16,20},{20,16},{24,28},{28,24},{1,5},{5... | collective-permute-start | bytes 589832 | tf_op jit(solution)/shard_map/cond/branch_1_fun/ppermute | solution.py:288
  35.4 7.2 %collective-permute-start.6 = (bf16[16,3072]{1,0:T(8,128)(2,1)S(1)}, bf16[16,3072]{1,0:T(8,128)(2,1)S(1)}, u32[]{:S(2)}, u32[]{:S(2)}) collective-permute-start(bf16[16,3072]{1,0:T(8,128)(2,1)S(1)} %add_terms.4.refs_0_), channel_id=1, source_target_pairs={{0,1},{1,0},{2,3},{3,2},{4,5},{5,4},{6,7},{7,6},{8,9},{9,8},{10,11... | collective-permute-start | bytes 294920 | tf_op jit(solution)/shard_map/cond/branch_1_fun/ppermute | solution.py:285
  37.0 6.7 %collective-permute-start.7 = (bf16[16,3072]{1,0:T(8,128)(2,1)S(1)}, bf16[16,3072]{1,0:T(8,128)(2,1)S(1)}, u32[]{:S(2)}, u32[]{:S(2)}) collective-permute-start(bf16[16,3072]{1,0:T(8,128)(2,1)S(1)} %add_terms.4.refs_0_), channel_id=1, source_target_pairs={{0,2},{1,3},{2,0},{3,1},{4,6},{5,7},{6,4},{7,5},{8,10},{9,11},{10,... | collective-permute-start | bytes 294920 | tf_op jit(solution)/shard_map/cond/branch_1_fun/ppermute | solution.py:285
  37.5 6.2 %collective-permute-start.8 = (bf16[16,3072]{1,0:T(8,128)(2,1)S(1)}, bf16[16,3072]{1,0:T(8,128)(2,1)S(1)}, u32[]{:S(2)}, u32[]{:S(2)}) collective-permute-start(bf16[16,3072]{1,0:T(8,128)(2,1)S(1)} %add_terms.4.refs_0_), channel_id=1, source_target_pairs={{0,3},{1,2},{2,1},{3,0},{4,7},{5,6},{6,5},{7,4},{8,11},{9,10},{10,... | collective-permute-start | bytes 294920 | tf_op jit(solution)/shard_map/cond/branch_1_fun/ppermute | solution.py:285
  43.8 30.4 %all-to-all-start = ((bf16[4,32,6144]{2,1,0:T(8,128)(2,1)}), bf16[4,32,6144]{2,1,0:T(8,128)(2,1)}, u32[]{:S(2)}, u32[]{:S(2)}) async-start(bf16[4,32,6144]{2,1,0:T(8,128)(2,1)} %row_terms.1), calls=%async_computation | async-start | bytes 3145728 | tf_op jit(solution)/shard_map/cond/branch_1_fun/all_to_all | solution.py:455
  48.1 8.1 %collective-permute-start = (bf16[16,3072]{1,0:T(8,128)(2,1)S(1)}, bf16[16,3072]{1,0:T(8,128)(2,1)S(1)}, u32[]{:S(2)}, u32[]{:S(2)}) collective-permute-start(bf16[16,3072]{1,0:T(8,128)(2,1)S(1)} %get-tuple-element.33.refs_0_), channel_id=1, source_target_pairs={{0,8},{4,12},{8,0},{12,4},{16,24},{20,28},{24,16},{28,20},{1,9},{5... | collective-permute-start | bytes 294920 | tf_op jit(solution)/shard_map/cond/branch_1_fun/cond/branch_1_fun/ppermute | solution.py:291
  56.9 17.2 %collective-permute-start.1 = (bf16[240,768]{1,0:T(8,128)(2,1)S(1)}, bf16[240,768]{1,0:T(8,128)(2,1)}, u32[]{:S(2)}, u32[]{:S(2)}) collective-permute-start(bf16[240,768]{1,0:T(8,128)(2,1)S(1)} %get-tuple-element.34), channel_id=1, source_target_pairs={{0,8},{4,12},{8,0},{12,4},{16,24},{20,28},{24,16},{28,20},{1,9},{5... | collective-permute-start | bytes 1105928 | tf_op jit(solution)/shard_map/cond/branch_1_fun/cond/branch_1_fun/ppermute | solution.py:291
  59.4 13.1 %collective-permute-start.2 = (bf16[16,3072]{1,0:T(8,128)(2,1)}, bf16[16,3072]{1,0:T(8,128)(2,1)}, u32[]{:S(2)}, u32[]{:S(2)}) collective-permute-start(bf16[16,3072]{1,0:T(8,128)(2,1)} %add_terms.3), channel_id=1, source_target_pairs={{0,16},{4,20},{8,24},{12,28},{16,0},{20,4},{24,8},{28,12},{1,17},{... | collective-permute-start | bytes 294920 | tf_op jit(solution)/shard_map/cond/branch_1_fun/cond/branch_1_fun/ppermute | solution.py:291
  61.4 11.1 %collective-permute-start.3 = (bf16[16,3072]{1,0:T(8,128)(2,1)}, bf16[16,3072]{1,0:T(8,128)(2,1)}, u32[]{:S(2)}, u32[]{:S(2)}) collective-permute-start(bf16[16,3072]{1,0:T(8,128)(2,1)} %add_terms.3), channel_id=1, source_target_pairs={{0,4},{4,0},{8,12},{12,8},{16,20},{20,16},{24,28},{28,24},{1,5},{5... | collective-permute-start | bytes 294920 | tf_op jit(solution)/shard_map/cond/branch_1_fun/cond/branch_1_fun/ppermute | solution.py:288
  72.5 1.6 %collective-permute-start.4 = (bf16[16,3072]{1,0:T(8,128)(2,1)}, bf16[16,3072]{1,0:T(8,128)(2,1)}, u32[]{:S(2)}, u32[]{:S(2)}) collective-permute-start(bf16[16,3072]{1,0:T(8,128)(2,1)} %collective-permute-done.2), channel_id=1, source_target_pairs={{0,4},{4,0},{8,12},{12,8},{16,20},{20,16},{24,28},{28,24},{1,5},{5... | collective-permute-start | bytes 294920 | tf_op jit(solution)/shard_map/cond/branch_1_fun/cond/branch_1_fun/ppermute | solution.py:288

commit v7 on v6

--- a/solution.py
+++ b/solution.py
@@ -419,9 +419,10 @@
     def sum_chips(values):
         total, near = values
         for k in range(chip_rounds - 1):
-            total = add_pair(total, over_chip, k)
+            partner = over_chip(total, 1 << k)
             if k == 0:
-                near, total = lax.optimization_barrier((near, total))
+                near, partner = lax.optimization_barrier((near, partner))
+            total = add_terms([total, partner], BF16)
         last = over_chip(total, 1 << (chip_rounds - 1))
         return over_chip(near, 1), (total, last), (over_core(total), over_core(last))
 

time: 77.7 us -> 77 us (level)
  transfers between devices with their start and end apart: 22 -> 22, of which waited for: 9 -> 9; matrix products, arithmetic and copies ran while one was open for 0% -> 0% of each run, Pallas kernels for 15% -> 16%
where the time goes in v7:
time: 77 us; the launch traced here: 76.4 us
  waiting for transfers between devices  28.3 us (37%)
  starting transfers between devices  27.7 us (36%)
  Pallas kernels  19.5 us (25%)
    ppermute x5, waiting for transfers between devices, over_chip(): return lax.ppermute(value, 'dp', [(i, i ^ 2 * k) for i in range(n_dp)])  16.7 us
    ppermute x12, starting transfers between devices, over_expert(): return lax.ppermute(value, 'expert', [(i, i ^ k) for i in range(n_expert)])  14.2 us
    pallas_call x10, Pallas kernels, call(): pl.pallas_call(kernel, out_shape=outs, in_specs=specs, out_specs=[pl.Bloc...  12.7 us
    ppermute x5, starting transfers between devices, over_chip(): return lax.ppermute(value, 'dp', [(i, i ^ 2 * k) for i in range(n_dp)])  8.93 us
    ppermute x12, waiting for transfers between devices, over_expert(): return lax.ppermute(value, 'expert', [(i, i ^ k) for i in range(n_expert)])  8.59 us
    pallas_call x1, Pallas kernels, on_device(): pl.pallas_call(functools.partial(prepare_kernel, blocks), out_shape=resul...  5.17 us
    all_to_all x1, starting transfers between devices, way_back(): back_rows = lax.all_to_all(row_pieces, 'expert', 0, 0, tiled=True)  4.35 us
    ppermute x4, waiting for transfers between devices, over_core(): return lax.ppermute(value, 'dp', [(i, i ^ 1) for i in range(n_dp)])  3.07 us
  transfers between devices with their start and end apart: 22, of which 9 were waited for; matrix products, arithmetic and copies ran while one was open for 0% of the time, Pallas kernels for 16%

profile of v7, /device:TPU:8, one launch (start us, length us, event | category | flops | bytes accessed | tf_op | source)
XLA Modules:
  0.0 76.4 jit_solution(16491634346490099198)
XLA Ops:
  0.6 1.6 %route.1 = (bf16[32,3072]{1,0:T(8,128)(2,1)S(1)}, bf16[32,3200]{1,0:T(8,128)(2,1)S(1)}) custom-call(s32[4,32]{1,0:T(4,128)} %bitcast.23, bf16[32,6144]{1,0:T(8,128)(2,1)} %refs_1_.1, bf16[16,6144]{1,0:T(8,128)(2,1)} %bitcast.21, bf16[32,6144]{1,0:T(8,128)(2,1)} %refs_3_.1), custom_call_target="tpu_custom_call" | custom-call | tf_op jit(solution)/shard_map/route/pallas_call | solution.py:314
  2.3 1.6 %collective-permute-start.13 = (bf16[32,3200]{1,0:T(8,128)(2,1)S(1)}, bf16[32,3200]{1,0:T(8,128)(2,1)S(1)}, u32[]{:S(2)}, u32[]{:S(2)}) collective-permute-start(bf16[32,3200]{1,0:T(8,128)(2,1)S(1)} %get-tuple-element.112.refs_4_.refs_0_), channel_id=1, source_target_pairs={{0,2},{1,3},{2,0},{3,1},{4,6},{5,7},{6,4},{7,5},{8,10},{9,11},{10,... | collective-permute-start | bytes 614408 | tf_op jit(solution)/shard_map/ppermute | solution.py:285
  3.8 1.5 %collective-permute-start.9 = (bf16[32,3072]{1,0:T(8,128)(2,1)S(1)}, bf16[32,3072]{1,0:T(8,128)(2,1)S(1)}, u32[]{:S(2)}, u32[]{:S(2)}) collective-permute-start(bf16[32,3072]{1,0:T(8,128)(2,1)S(1)} %get-tuple-element.111.refs_0_), channel_id=1, source_target_pairs={{0,1},{1,0},{2,3},{3,2},{4,5},{5,4},{6,7},{7,6},{8,9},{9,8},{10,11... | collective-permute-start | bytes 589832 | tf_op jit(solution)/shard_map/ppermute | solution.py:285
  5.9 3.3 %collective-permute-done.13.refs_6_.refs_2_ = bf16[32,3200]{1,0:T(8,128)(2,1)S(1)} collective-permute-done((bf16[32,3200]{1,0:T(8,128)(2,1)S(1)}, bf16[32,3200]{1,0:T(8,128)(2,1)S(1)}, u32[]{:S(2)}, u32[]{:S(2)}) %collective-permute-start.13) | collective-permute-done | bytes 204832 | tf_op jit(solution)/shard_map/ppermute | solution.py:285
  9.1 1.5 %collective-permute-start.14 = (bf16[32,3200]{1,0:T(8,128)(2,1)S(1)}, bf16[32,3200]{1,0:T(8,128)(2,1)S(1)}, u32[]{:S(2)}, u32[]{:S(2)}) collective-permute-start(bf16[32,3200]{1,0:T(8,128)(2,1)S(1)} %collective-permute-done.13.refs_6_.refs_2_), channel_id=1, source_target_pairs={{0,1},{1,0},{2,3},{3,2},{4,5},{5,4},{6,7},{7,6},{8,9},{9,8},{10,11... | collective-permute-start | bytes 614408 | tf_op jit(solution)/shard_map/ppermute | solution.py:285
  10.6 1.5 %collective-permute-start.10 = (bf16[32,3072]{1,0:T(8,128)(2,1)S(1)}, bf16[32,3072]{1,0:T(8,128)(2,1)S(1)}, u32[]{:S(2)}, u32[]{:S(2)}) collective-permute-start(bf16[32,3072]{1,0:T(8,128)(2,1)S(1)} %get-tuple-element.111.refs_0_), channel_id=1, source_target_pairs={{0,2},{1,3},{2,0},{3,1},{4,6},{5,7},{6,4},{7,5},{8,10},{9,11},{10,... | collective-permute-start | bytes 589832 | tf_op jit(solution)/shard_map/ppermute | solution.py:285
  12.7 5.2 %prepare.1 = (bf16[144,6144]{1,0:T(8,128)(2,1)S(1)}, bf16[80,6144]{1,0:T(8,128)(2,1)}, bf16[80,6144]{1,0:T(8,128)(2,1)}, bf16[80,6144]{1,0:T(8,128)(2,1)S(1)}, f...) custom-call(bf16[36,4,6144]{2,1,0:T(4,128)(2,1)} %bitcast.17, bf16[20,4,6144]{2,1,0:T(4,128)(2,1)} %bitcast.18, ...), custom_call_target="tpu_custom_call" | custom-call | tf_op jit(solution)/shard_map/prepare/pallas_call | solution.py:347
  18.2 2.1 %collective-permute-done.11.refs_3_ = bf16[32,3072]{1,0:T(8,128)(2,1)S(1)} collective-permute-done((bf16[32,3072]{1,0:T(8,128)(2,1)S(1)}, bf16[32,3072]{1,0:T(8,128)(2,1)S(1)}, u32[]{:S(2)}, u32[]{:S(2)}) %collective-permute-start.11) | collective-permute-done | bytes 196640 | tf_op jit(solution)/shard_map/ppermute | solution.py:285
  20.3 1.7 %experts.1 = (f32[32,128]{1,0:T(8,128)S(1)}, f32[32,128]{1,0:T(8,128)S(1)}, f32[32,128]{1,0:T(8,128)S(1)}, f32[32,128]{1,0:T(8,128)S(1)}, bf16[128,144]{1,0:T(8,...) custom-call(s32[3]{0:T(128)S(1)} %pad_add_fusion.at, ...), custom_call_target="tpu_custom_call" | custom-call | tf_op jit(solution)/shard_map/experts/pallas_call | solution.py:302
  22.0 1.4 %core_terms.1 = (bf16[128,80]{1,0:T(8,128)(2,1)S(1)}, bf16[128,80]{1,0:T(8,128)(2,1)S(1)}, bf16[80,144]{1,0:T(8,128)(2,1)S(1)}, bf16[80,144]{1,0:T(8,128)(2,1)S(...) custom-call(s32[3]{0:T(128)S(1)} %pad_add_fusion.at, ...), custom_call_target="tpu_custom_call" | custom-call | tf_op jit(solution)/shard_map/core_terms/pallas_call | solution.py:302
  24.1 1.5 %collective-permute-start.17 = (f32[32,128]{1,0:T(8,128)S(1)}, f32[32,128]{1,0:T(8,128)S(1)}, u32[]{:S(2)}, u32[]{:S(2)}) collective-permute-start(f32[32,128]{1,0:T(8,128)S(1)} %get-tuple-element.132), channel_id=1, source_target_pairs={{0,2},{1,3},{2,0},{3,1},{4,6},{5,7},{6,4},{7,5},{8,10},{9,11},{10,... | collective-permute-start | bytes 49160 | tf_op jit(solution)/shard_map/ppermute | solution.py:285
  25.6 1.4 %collective-permute-start.18 = (f32[32,128]{1,0:T(8,128)S(1)}, f32[32,128]{1,0:T(8,128)S(1)}, u32[]{:S(2)}, u32[]{:S(2)}) collective-permute-start(f32[32,128]{1,0:T(8,128)S(1)} %get-tuple-element.133), channel_id=1, source_target_pairs={{0,3},{1,2},{2,1},{3,0},{4,7},{5,6},{6,5},{7,4},{8,11},{9,10},{10,... | collective-permute-start | bytes 49160 | tf_op jit(solution)/shard_map/ppermute | solution.py:285
  27.0 1.1 %weight_terms.1.mine = f32[4,240,768]{2,1,0:T(8,128)S(1)} custom-call(s32[3]{0:T(128)S(1)} %pad_add_fusion.at, bf16[128,6144]{1,0:T(8,128)(2,1)S(1)} %get-tuple-element.116.refs_8_.arrived, bf16[144,6144]{1,0:T(8,128)(2,1)S(1)} %get-tuple-element.117.refs_9_.inputs, bf16[80,144]{1,0:T(8,128)(2,1)S(1)} %get-tuple-element.122.gate, ...), custom_call_target="tpu_custom_call" | custom-call | tf_op jit(solution)/shard_map/weight_terms/pallas_call | solution.py:302
  28.4 1.8 %collective-permute-done.18 = f32[32,128]{1,0:T(8,128)S(1)} collective-permute-done((f32[32,128]{1,0:T(8,128)S(1)}, f32[32,128]{1,0:T(8,128)S(1)}, u32[]{:S(2)}, u32[]{:S(2)}) %collective-permute-start.18) | collective-permute-done | bytes 16416 | tf_op jit(solution)/shard_map/ppermute | solution.py:285
  30.2 2.6 %collective-permute-start.19 = (bf16[240,768]{1,0:T(8,128)(2,1)S(1)}, bf16[240,768]{1,0:T(8,128)(2,1)S(1)}, u32[]{:S(2)}, u32[]{:S(2)}) collective-permute-start(bf16[240,768]{1,0:T(8,128)(2,1)S(1)} %get-tuple-element.145), channel_id=1, source_target_pairs={{0,16},{4,20},{8,24},{12,28},{16,0},{20,4},{24,8},{28,12},{1,17},{... | collective-permute-start | bytes 1105928 | tf_op jit(solution)/shard_map/ppermute | solution.py:291
  32.8 40.7 %conditional.2 = (bf16[240,768]{1,0:T(8,128)(2,1)}, bf16[16,3072]{1,0:T(8,128)(2,1)}, bf16[16,3072]{1,0:T(8,128)(2,1)}, bf16[16,3072]{1,0:T(8,128)(2,1)}, bf16[1...) conditional(s32[]{:T(128)} %convert_element_type.6, () %tuple.28, (pred[]{:T(512)}, s32[3]{0:T(128)S(1)}, ...), branch_computations={%region_0.0_spmd, %region_1.0_spmd} | conditional | flops 1 | bytes 13664785 | solution.py:431
  32.8 1.1 %router_terms.1 = (f32[16,3072]{1,0:T(8,128)S(1)}, f32[16,3072]{1,0:T(8,128)S(1)}, f32[32,16]{1,0:T(8,128)S(1)}) custom-call(s32[3]{0:T(128)S(1)} %get-tuple-element.37.at, f32[32,128]{1,0:T(8,128)S(1)} %get-tuple-element.42.refs_0_, f32[32,128]{1,0:T(8,128)S(1)} %get-tuple-element.43.refs_1_, f32[32,128]{1,0:T(8,128)S(1)} %get-tuple-element.44.refs_2_, ...), custom_call_target="tpu_custom_call" | custom-call | tf_op jit(solution)/shard_map/cond/branch_1_fun/router_terms/pallas_call | solution.py:302
  34.0 1.4 %collective-permute-done.5.refs_1_ = f32[16,3072]{1,0:T(8,128)S(1)} collective-permute-done((f32[16,3072]{1,0:T(8,128)S(1)}, f32[16,3072]{1,0:T(8,128)S(1)}, u32[]{:S(2)}, u32[]{:S(2)}) %collective-permute-start.5) | collective-permute-done | bytes 196640 | tf_op jit(solution)/shard_map/cond/branch_1_fun/ppermute | solution.py:288
  35.4 1.6 %collective-permute-start.6 = (bf16[16,3072]{1,0:T(8,128)(2,1)S(1)}, bf16[16,3072]{1,0:T(8,128)(2,1)S(1)}, u32[]{:S(2)}, u32[]{:S(2)}) collective-permute-start(bf16[16,3072]{1,0:T(8,128)(2,1)S(1)} %add_terms.4.refs_0_), channel_id=1, source_target_pairs={{0,1},{1,0},{2,3},{3,2},{4,5},{5,4},{6,7},{7,6},{8,9},{9,8},{10,11... | collective-permute-start | bytes 294920 | tf_op jit(solution)/shard_map/cond/branch_1_fun/ppermute | solution.py:285
  37.5 1.5 %collective-permute-start.8 = (bf16[16,3072]{1,0:T(8,128)(2,1)S(1)}, bf16[16,3072]{1,0:T(8,128)(2,1)S(1)}, u32[]{:S(2)}, u32[]{:S(2)}) collective-permute-start(bf16[16,3072]{1,0:T(8,128)(2,1)S(1)} %add_terms.4.refs_0_), channel_id=1, source_target_pairs={{0,3},{1,2},{2,1},{3,0},{4,7},{5,6},{6,5},{7,4},{8,11},{9,10},{10,... | collective-permute-start | bytes 294920 | tf_op jit(solution)/shard_map/cond/branch_1_fun/ppermute | solution.py:285
  39.0 3.6 %row_terms.1 = bf16[4,32,6144]{2,1,0:T(8,128)(2,1)} custom-call(s32[3]{0:T(128)S(1)} %get-tuple-element.37.at, bf16[128,80]{1,0:T(8,128)(2,1)S(1)} %get-tuple-element.38.tok_gate, bf16[128,80]{1,0:T(8,128)(2,1)S(1)} %get-tuple-element.39.tok_up, bf16[80,6144]{1,0:T(8,128)(2,1)S(1)} %copy-done.1, bf16[80,6144]{1,0:T(8,128)(2,1)} %get-tuple-element.41.up, ...), custom_call_target="tpu_custom_call" | custom-call | tf_op jit(solution)/shard_map/cond/branch_1_fun/row_terms/pallas_call | solution.py:302
  42.6 1.1 %collective-permute-done.7.refs_2_ = bf16[16,3072]{1,0:T(8,128)(2,1)S(1)} collective-permute-done((bf16[16,3072]{1,0:T(8,128)(2,1)S(1)}, bf16[16,3072]{1,0:T(8,128)(2,1)S(1)}, u32[]{:S(2)}, u32[]{:S(2)}) %collective-permute-start.7) | collective-permute-done | bytes 98336 | tf_op jit(solution)/shard_map/cond/branch_1_fun/ppermute | solution.py:285
  43.8 4.3 %all-to-all-start = ((bf16[4,32,6144]{2,1,0:T(8,128)(2,1)}), bf16[4,32,6144]{2,1,0:T(8,128)(2,1)}, u32[]{:S(2)}, u32[]{:S(2)}) async-start(bf16[4,32,6144]{2,1,0:T(8,128)(2,1)} %row_terms.1), calls=%async_computation | async-start | bytes 3145728 | tf_op jit(solution)/shard_map/cond/branch_1_fun/all_to_all | solution.py:456
  48.1 25.3 %conditional = (bf16[240,768]{1,0:T(8,128)(2,1)}, bf16[16,3072]{1,0:T(8,128)(2,1)}, bf16[16,3072]{1,0:T(8,128)(2,1)}, bf16[16,3072]{1,0:T(8,128)(2,1)}, bf16[16,3072]{1,0:T(8,128)(2,1)}) conditional(s32[]{:T(128)} %convert_element_type.4, () %tuple.18, (bf16[16,3072]{1,0:T(8,128)(2,1)S(1)}, bf16[240,768]{1,0:T(8,128)(2,1)S(1)}) %tuple.20), branch_computations={%region_2.0_spmd, %region_3.0_spmd} | conditional | bytes 3047664 | solution.py:431
  48.1 1.8 %collective-permute-start = (bf16[16,3072]{1,0:T(8,128)(2,1)S(1)}, bf16[16,3072]{1,0:T(8,128)(2,1)S(1)}, u32[]{:S(2)}, u32[]{:S(2)}) collective-permute-start(bf16[16,3072]{1,0:T(8,128)(2,1)S(1)} %get-tuple-element.33.refs_0_), channel_id=1, source_target_pairs={{0,8},{4,12},{8,0},{12,4},{16,24},{20,28},{24,16},{28,20},{1,9},{5... | collective-permute-start | bytes 294920 | tf_op jit(solution)/shard_map/cond/branch_1_fun/cond/branch_1_fun/ppermute | solution.py:291
  50.0 6.3 %collective-permute-done.refs_1_ = bf16[16,3072]{1,0:T(8,128)(2,1)S(1)} collective-permute-done((bf16[16,3072]{1,0:T(8,128)(2,1)S(1)}, bf16[16,3072]{1,0:T(8,128)(2,1)S(1)}, u32[]{:S(2)}, u32[]{:S(2)}) %collective-permute-start) | collective-permute-done | bytes 98336 | tf_op jit(solution)/shard_map/cond/branch_1_fun/cond/branch_1_fun/ppermute | solution.py:291
  56.2 2.5 %collective-permute-start.1 = (bf16[240,768]{1,0:T(8,128)(2,1)S(1)}, bf16[240,768]{1,0:T(8,128)(2,1)}, u32[]{:S(2)}, u32[]{:S(2)}) collective-permute-start(bf16[240,768]{1,0:T(8,128)(2,1)S(1)} %get-tuple-element.34), channel_id=1, source_target_pairs={{0,8},{4,12},{8,0},{12,4},{16,24},{20,28},{24,16},{28,20},{1,9},{5... | collective-permute-start | bytes 1105928 | tf_op jit(solution)/shard_map/cond/branch_1_fun/cond/branch_1_fun/ppermute | solution.py:291
  58.7 0.7 add_terms.3
  59.4 2.0 %collective-permute-start.2 = (bf16[16,3072]{1,0:T(8,128)(2,1)}, bf16[16,3072]{1,0:T(8,128)(2,1)}, u32[]{:S(2)}, u32[]{:S(2)}) collective-permute-start(bf16[16,3072]{1,0:T(8,128)(2,1)} %add_terms.3), channel_id=1, source_target_pairs={{0,16},{4,20},{8,24},{12,28},{16,0},{20,4},{24,8},{28,12},{1,17},{... | collective-permute-start | bytes 294920 | tf_op jit(solution)/shard_map/cond/branch_1_fun/cond/branch_1_fun/ppermute | solution.py:291
  61.4 10.4 %collective-permute-done.2 = bf16[16,3072]{1,0:T(8,128)(2,1)} collective-permute-done((bf16[16,3072]{1,0:T(8,128)(2,1)}, bf16[16,3072]{1,0:T(8,128)(2,1)}, u32[]{:S(2)}, u32[]{:S(2)}) %collective-permute-start.2) | collective-permute-done | bytes 98336 | tf_op jit(solution)/shard_map/cond/branch_1_fun/cond/branch_1_fun/ppermute | solution.py:291
  71.8 1.6 %collective-permute-done.4 = bf16[16,3072]{1,0:T(8,128)(2,1)} collective-permute-done((bf16[16,3072]{1,0:T(8,128)(2,1)}, bf16[16,3072]{1,0:T(8,128)(2,1)}, u32[]{:S(2)}, u32[]{:S(2)}) %collective-permute-start.4) | collective-permute-done | bytes 98336 | tf_op jit(solution)/shard_map/cond/branch_1_fun/cond/branch_1_fun/ppermute | solution.py:288
  73.5 2.9 %finish.1 = (bf16[32,6144]{1,0:T(8,128)(2,1)}, f32[16,6144]{1,0:T(8,128)}, f32[20,4,768]{2,1,0:T(4,128)}, f32[20,4,768]{2,1,0:T(4,128)}, f32[20,4,768]{2,1,0:T(4,128)}) custom-call(s32[3]{0:T(128)S(1)} %pad_add_fusion.at, f32[240,768]{1,0:T(8,128)S(1)} %get-tuple-element.134.refs_0_, bf16[240,768]{1,0:T(8,128)(2,1)} %get-tuple-element.144.refs_1_, ...), custom_call_target="tpu_custom_call" | custom-call | tf_op jit(solution)/shard_map/finish/pallas_call | solution.py:302
  (33 shorter events, 3.1 us)
Async XLA Ops:
  2.3 6.9 %collective-permute-start.13 = (bf16[32,3200]{1,0:T(8,128)(2,1)S(1)}, bf16[32,3200]{1,0:T(8,128)(2,1)S(1)}, u32[]{:S(2)}, u32[]{:S(2)}) collective-permute-start(bf16[32,3200]{1,0:T(8,128)(2,1)S(1)} %get-tuple-element.112.refs_4_.refs_0_), channel_id=1, source_target_pairs={{0,2},{1,3},{2,0},{3,1},{4,6},{5,7},{6,4},{7,5},{8,10},{9,11},{10,... | collective-permute-start | bytes 614408 | tf_op jit(solution)/shard_map/ppermute | solution.py:285
  3.8 8.3 %collective-permute-start.9 = (bf16[32,3072]{1,0:T(8,128)(2,1)S(1)}, bf16[32,3072]{1,0:T(8,128)(2,1)S(1)}, u32[]{:S(2)}, u32[]{:S(2)}) collective-permute-start(bf16[32,3072]{1,0:T(8,128)(2,1)S(1)} %get-tuple-element.111.refs_0_), channel_id=1, source_target_pairs={{0,1},{1,0},{2,3},{3,2},{4,5},{5,4},{6,7},{7,6},{8,9},{9,8},{10,11... | collective-permute-start | bytes 589832 | tf_op jit(solution)/shard_map/ppermute | solution.py:285
  5.3 12.9 %collective-permute-start.12 = (bf16[32,3200]{1,0:T(8,128)(2,1)S(1)}, bf16[32,3200]{1,0:T(8,128)(2,1)S(1)}, u32[]{:S(2)}, u32[]{:S(2)}) collective-permute-start(bf16[32,3200]{1,0:T(8,128)(2,1)S(1)} %get-tuple-element.112.refs_4_.refs_0_), channel_id=1, source_target_pairs={{0,1},{1,0},{2,3},{3,2},{4,5},{5,4},{6,7},{7,6},{8,9},{9,8},{10,11... | collective-permute-start | bytes 614408 | tf_op jit(solution)/shard_map/ppermute | solution.py:285
  9.1 11.2 %collective-permute-start.14 = (bf16[32,3200]{1,0:T(8,128)(2,1)S(1)}, bf16[32,3200]{1,0:T(8,128)(2,1)S(1)}, u32[]{:S(2)}, u32[]{:S(2)}) collective-permute-start(bf16[32,3200]{1,0:T(8,128)(2,1)S(1)} %collective-permute-done.13.refs_6_.refs_2_), channel_id=1, source_target_pairs={{0,1},{1,0},{2,3},{3,2},{4,5},{5,4},{6,7},{7,6},{8,9},{9,8},{10,11... | collective-permute-start | bytes 614408 | tf_op jit(solution)/shard_map/ppermute | solution.py:285
  10.6 7.6 %collective-permute-start.10 = (bf16[32,3072]{1,0:T(8,128)(2,1)S(1)}, bf16[32,3072]{1,0:T(8,128)(2,1)S(1)}, u32[]{:S(2)}, u32[]{:S(2)}) collective-permute-start(bf16[32,3072]{1,0:T(8,128)(2,1)S(1)} %get-tuple-element.111.refs_0_), channel_id=1, source_target_pairs={{0,2},{1,3},{2,0},{3,1},{4,6},{5,7},{6,4},{7,5},{8,10},{9,11},{10,... | collective-permute-start | bytes 589832 | tf_op jit(solution)/shard_map/ppermute | solution.py:285
  12.1 8.2 %collective-permute-start.11 = (bf16[32,3072]{1,0:T(8,128)(2,1)S(1)}, bf16[32,3072]{1,0:T(8,128)(2,1)S(1)}, u32[]{:S(2)}, u32[]{:S(2)}) collective-permute-start(bf16[32,3072]{1,0:T(8,128)(2,1)S(1)} %collective-permute-done.9.refs_1_), channel_id=1, source_target_pairs={{0,2},{1,3},{2,0},{3,1},{4,6},{5,7},{6,4},{7,5},{8,10},{9,11},{10,... | collective-permute-start | bytes 589832 | tf_op jit(solution)/shard_map/ppermute | solution.py:285
  23.4 4.8 %collective-permute-start.15 = (bf16[4,240,768]{2,1,0:T(8,128)(2,1)S(1)}, bf16[4,240,768]{2,1,0:T(8,128)(2,1)S(1)}, u32[]{:S(2)}, u32[]{:S(2)}) collective-permute-start(bf16[4,240,768]{2,1,0:T(8,128)(2,1)S(1)} %get-tuple-element.125), channel_id=1, source_target_pairs={{0,4},{4,0},{8,12},{12,8},{16,20},{20,16},{24,28},{28,24},{1,5},{5... | collective-permute-start | bytes 4423688 | tf_op jit(solution)/shard_map/ppermute | solution.py:288
  23.5 4.9 %collective-permute-start.16 = (f32[32,128]{1,0:T(8,128)S(1)}, f32[32,128]{1,0:T(8,128)S(1)}, u32[]{:S(2)}, u32[]{:S(2)}) collective-permute-start(f32[32,128]{1,0:T(8,128)S(1)} %get-tuple-element.131), channel_id=1, source_target_pairs={{0,1},{1,0},{2,3},{3,2},{4,5},{5,4},{6,7},{7,6},{8,9},{9,8},{10,11... | collective-permute-start | bytes 49160 | tf_op jit(solution)/shard_map/ppermute | solution.py:285
  24.1 4.3 %collective-permute-start.17 = (f32[32,128]{1,0:T(8,128)S(1)}, f32[32,128]{1,0:T(8,128)S(1)}, u32[]{:S(2)}, u32[]{:S(2)}) collective-permute-start(f32[32,128]{1,0:T(8,128)S(1)} %get-tuple-element.132), channel_id=1, source_target_pairs={{0,2},{1,3},{2,0},{3,1},{4,6},{5,7},{6,4},{7,5},{8,10},{9,11},{10,... | collective-permute-start | bytes 49160 | tf_op jit(solution)/shard_map/ppermute | solution.py:285
  25.6 4.6 %collective-permute-start.18 = (f32[32,128]{1,0:T(8,128)S(1)}, f32[32,128]{1,0:T(8,128)S(1)}, u32[]{:S(2)}, u32[]{:S(2)}) collective-permute-start(f32[32,128]{1,0:T(8,128)S(1)} %get-tuple-element.133), channel_id=1, source_target_pairs={{0,3},{1,2},{2,1},{3,0},{4,7},{5,6},{6,5},{7,4},{8,11},{9,10},{10,... | collective-permute-start | bytes 49160 | tf_op jit(solution)/shard_map/ppermute | solution.py:285
  28.1 4.7 %copy-start = (bf16[32,6144]{1,0:T(8,128)(2,1)S(1)}, bf16[32,6144]{1,0:T(8,128)(2,1)}, u32[]{:S(2)}) copy-start(bf16[32,6144]{1,0:T(8,128)(2,1)} %refs_1_.1) | copy-start | bytes 1179652
  28.1 4.7 %copy-start.2 = (bf16[6144,16]{0,1:T(8,128)(2,1)S(1)}, bf16[6144,16]{0,1:T(8,128)(2,1)}, u32[]{:S(2)}) copy-start(bf16[6144,16]{0,1:T(8,128)(2,1)} %param.15) | copy-start | bytes 589828
  30.2 43.3 %collective-permute-start.19 = (bf16[240,768]{1,0:T(8,128)(2,1)S(1)}, bf16[240,768]{1,0:T(8,128)(2,1)S(1)}, u32[]{:S(2)}, u32[]{:S(2)}) collective-permute-start(bf16[240,768]{1,0:T(8,128)(2,1)S(1)} %get-tuple-element.145), channel_id=1, source_target_pairs={{0,16},{4,20},{8,24},{12,28},{16,0},{20,4},{24,8},{28,12},{1,17},{... | collective-permute-start | bytes 1105928 | tf_op jit(solution)/shard_map/ppermute | solution.py:291
  32.8 40.7 %collective-permute-start.20 = (bf16[240,768]{1,0:T(8,128)(2,1)S(1)}, bf16[240,768]{1,0:T(8,128)(2,1)S(1)}, u32[]{:S(2)}, u32[]{:S(2)}) collective-permute-start(bf16[240,768]{1,0:T(8,128)(2,1)S(1)} %get-tuple-element.146), channel_id=1, source_target_pairs={{0,24},{4,28},{8,16},{12,20},{16,8},{20,12},{24,0},{28,4},{1,25},{... | collective-permute-start | bytes 1105928 | tf_op jit(solution)/shard_map/ppermute | solution.py:291
  32.8 6.2 %copy-start.1 = (bf16[80,6144]{1,0:T(8,128)(2,1)S(1)}, bf16[80,6144]{1,0:T(8,128)(2,1)}, u32[]{:S(2)}) copy-start(bf16[80,6144]{1,0:T(8,128)(2,1)} %get-tuple-element.40.gate) | copy-start | bytes 2949124 | tf_op jit(solution)/shard_map/cond
  33.9 1.5 %collective-permute-start.5 = (f32[16,3072]{1,0:T(8,128)S(1)}, f32[16,3072]{1,0:T(8,128)S(1)}, u32[]{:S(2)}, u32[]{:S(2)}) collective-permute-start(f32[16,3072]{1,0:T(8,128)S(1)} %get-tuple-element.51), channel_id=1, source_target_pairs={{0,4},{4,0},{8,12},{12,8},{16,20},{20,16},{24,28},{28,24},{1,5},{5... | collective-permute-start | bytes 589832 | tf_op jit(solution)/shard_map/cond/branch_1_fun/ppermute | solution.py:288
  35.4 7.2 %collective-permute-start.6 = (bf16[16,3072]{1,0:T(8,128)(2,1)S(1)}, bf16[16,3072]{1,0:T(8,128)(2,1)S(1)}, u32[]{:S(2)}, u32[]{:S(2)}) collective-permute-start(bf16[16,3072]{1,0:T(8,128)(2,1)S(1)} %add_terms.4.refs_0_), channel_id=1, source_target_pairs={{0,1},{1,0},{2,3},{3,2},{4,5},{5,4},{6,7},{7,6},{8,9},{9,8},{10,11... | collective-permute-start | bytes 294920 | tf_op jit(solution)/shard_map/cond/branch_1_fun/ppermute | solution.py:285
  37.0 6.7 %collective-permute-start.7 = (bf16[16,3072]{1,0:T(8,128)(2,1)S(1)}, bf16[16,3072]{1,0:T(8,128)(2,1)S(1)}, u32[]{:S(2)}, u32[]{:S(2)}) collective-permute-start(bf16[16,3072]{1,0:T(8,128)(2,1)S(1)} %add_terms.4.refs_0_), channel_id=1, source_target_pairs={{0,2},{1,3},{2,0},{3,1},{4,6},{5,7},{6,4},{7,5},{8,10},{9,11},{10,... | collective-permute-start | bytes 294920 | tf_op jit(solution)/shard_map/cond/branch_1_fun/ppermute | solution.py:285
  37.5 6.2 %collective-permute-start.8 = (bf16[16,3072]{1,0:T(8,128)(2,1)S(1)}, bf16[16,3072]{1,0:T(8,128)(2,1)S(1)}, u32[]{:S(2)}, u32[]{:S(2)}) collective-permute-start(bf16[16,3072]{1,0:T(8,128)(2,1)S(1)} %add_terms.4.refs_0_), channel_id=1, source_target_pairs={{0,3},{1,2},{2,1},{3,0},{4,7},{5,6},{6,5},{7,4},{8,11},{9,10},{10,... | collective-permute-start | bytes 294920 | tf_op jit(solution)/shard_map/cond/branch_1_fun/ppermute | solution.py:285
  43.8 29.7 %all-to-all-start = ((bf16[4,32,6144]{2,1,0:T(8,128)(2,1)}), bf16[4,32,6144]{2,1,0:T(8,128)(2,1)}, u32[]{:S(2)}, u32[]{:S(2)}) async-start(bf16[4,32,6144]{2,1,0:T(8,128)(2,1)} %row_terms.1), calls=%async_computation | async-start | bytes 3145728 | tf_op jit(solution)/shard_map/cond/branch_1_fun/all_to_all | solution.py:456
  48.1 8.1 %collective-permute-start = (bf16[16,3072]{1,0:T(8,128)(2,1)S(1)}, bf16[16,3072]{1,0:T(8,128)(2,1)S(1)}, u32[]{:S(2)}, u32[]{:S(2)}) collective-permute-start(bf16[16,3072]{1,0:T(8,128)(2,1)S(1)} %get-tuple-element.33.refs_0_), channel_id=1, source_target_pairs={{0,8},{4,12},{8,0},{12,4},{16,24},{20,28},{24,16},{28,20},{1,9},{5... | collective-permute-start | bytes 294920 | tf_op jit(solution)/shard_map/cond/branch_1_fun/cond/branch_1_fun/ppermute | solution.py:291
  56.2 17.2 %collective-permute-start.1 = (bf16[240,768]{1,0:T(8,128)(2,1)S(1)}, bf16[240,768]{1,0:T(8,128)(2,1)}, u32[]{:S(2)}, u32[]{:S(2)}) collective-permute-start(bf16[240,768]{1,0:T(8,128)(2,1)S(1)} %get-tuple-element.34), channel_id=1, source_target_pairs={{0,8},{4,12},{8,0},{12,4},{16,24},{20,28},{24,16},{28,20},{1,9},{5... | collective-permute-start | bytes 1105928 | tf_op jit(solution)/shard_map/cond/branch_1_fun/cond/branch_1_fun/ppermute | solution.py:291
  59.4 12.4 %collective-permute-start.2 = (bf16[16,3072]{1,0:T(8,128)(2,1)}, bf16[16,3072]{1,0:T(8,128)(2,1)}, u32[]{:S(2)}, u32[]{:S(2)}) collective-permute-start(bf16[16,3072]{1,0:T(8,128)(2,1)} %add_terms.3), channel_id=1, source_target_pairs={{0,16},{4,20},{8,24},{12,28},{16,0},{20,4},{24,8},{28,12},{1,17},{... | collective-permute-start | bytes 294920 | tf_op jit(solution)/shard_map/cond/branch_1_fun/cond/branch_1_fun/ppermute | solution.py:291
  61.4 10.4 %collective-permute-start.3 = (bf16[16,3072]{1,0:T(8,128)(2,1)}, bf16[16,3072]{1,0:T(8,128)(2,1)}, u32[]{:S(2)}, u32[]{:S(2)}) collective-permute-start(bf16[16,3072]{1,0:T(8,128)(2,1)} %add_terms.3), channel_id=1, source_target_pairs={{0,4},{4,0},{8,12},{12,8},{16,20},{20,16},{24,28},{28,24},{1,5},{5... | collective-permute-start | bytes 294920 | tf_op jit(solution)/shard_map/cond/branch_1_fun/cond/branch_1_fun/ppermute | solution.py:288
  71.8 1.6 %collective-permute-start.4 = (bf16[16,3072]{1,0:T(8,128)(2,1)}, bf16[16,3072]{1,0:T(8,128)(2,1)}, u32[]{:S(2)}, u32[]{:S(2)}) collective-permute-start(bf16[16,3072]{1,0:T(8,128)(2,1)} %collective-permute-done.2), channel_id=1, source_target_pairs={{0,4},{4,0},{8,12},{12,8},{16,20},{20,16},{24,28},{28,24},{1,5},{5... | collective-permute-start | bytes 294920 | tf_op jit(solution)/shard_map/cond/branch_1_fun/cond/branch_1_fun/ppermute | solution.py:288
